TPU v7x, 128 devices: a whole 4x4x4 slice. The times are simulated.
128 devices in a mesh: span: 16 (over z, y), dp: 4 (over x_lo, core), mp: 2 (over x_hi).
Axes of the slice: x: 4 (x_hi: 2, x_lo: 2; x = x_hi * 2 + x_lo), y: 4, z: 4, core: 2. Of those that a mesh axis runs over, the one named last changes fastest.
Arguments:
- span_states: bfloat16 [8, 2048, 4096], P('dp', 'span', 'mp'), may hold values from -6 to 6
- queries: bfloat16 [8, 2048, 2048], P('dp', 'span', 'mp'), may hold values from -6 to 6
- out_grad: bfloat16 [8, 2048, 2048], P('dp', 'span', 'mp'), may hold values from -6 to 6
- neighbour_ids: int32 [8, 32, 2, 128], P('dp'), may hold values from 0 to 63999
- assignment: int32 [4, 16, 8, 1], P('dp'), may hold values from 0 to 15; in each aligned block of 8 rows (0 to 7, 8 to 15, ..., all dimensions but the last counted through in order) no two rows name the same one
- embed_table: bfloat16 [64000, 896], P('span'), may hold values from -6 to 6
- w_span_kv: bfloat16 [4096, 1792], P('mp'), may hold values from -0.09375 to 0.09375
- w_query_enc: bfloat16 [896, 896], P(None, 'mp'), may hold values from -0.1875 to 0.1875
- w_out_enc: bfloat16 [896, 896], P('mp'), may hold values from -0.1875 to 0.1875
- w_dec_kv: bfloat16 [896, 2, 2048], P(None, None, 'mp'), may hold values from -0.1875 to 0.1875
Outputs:
- cross_out: bfloat16 [8, 2048, 2048], P('dp', 'span', 'mp')
- attended: bfloat16 [4, 16, 16, 1, 128, 896], P('dp', 'span', None, None, None, 'mp')
- grad_query_enc: float32 [896, 896], P(('span', 'dp'), 'mp')
- grad_out_enc: float32 [896, 896], P('mp', ('span', 'dp'))
Inputs may be any that keep to these rules, and one draw needn't show every extreme that they name: `assignment`: among the 8 rows of one span device, no encoder index appears more than 1 times, and in every draw some device names one encoder exactly 1 times.
All inputs are finite; a program needn't handle non-finite values.
Results may differ from a plain program's by a relative error of at most 0.033.
Values may be sent and summed in bfloat16 or wider, within the bound.
A program may use at most 128 MiB of HBM per device.

v0:
```python
import math

import jax
import jax.numpy as jnp
from jax import lax
from jax.sharding import PartitionSpec as P

HD = 128
DE = 896
EHD = 64
R = 128
CH = 64
NB = 2


def softmax_grad(probs_full, grad_probs, row_terms, scale):
    return (probs_full * (grad_probs - row_terms[..., None]) / scale).astype(jnp.bfloat16)


def encoder_forward(enc_x, span_kv, w_query_enc, w_out_enc, n_mp):
    f32 = jnp.float32
    bf16 = jnp.bfloat16
    count = enc_x.shape[0]
    enc_cols = w_query_enc.shape[1]
    heads_enc = enc_cols // EHD
    key_rows = span_kv[:, :, :enc_cols].reshape(count, CH, heads_enc, EHD)
    value_rows = span_kv[:, :, enc_cols:].reshape(count, CH, heads_enc, EHD)
    enc_query = (
        jnp.dot(enc_x.reshape(-1, DE), w_query_enc, preferred_element_type=f32)
        .astype(bf16)
        .reshape(count, R, heads_enc, EHD)
    )
    scores = jnp.einsum(
        "sqhd,skhd->shqk", enc_query, key_rows, preferred_element_type=f32
    ) / math.sqrt(EHD)
    enc_full = jax.nn.softmax(scores, axis=-1)
    enc_weights = enc_full.astype(bf16)
    attended = jnp.einsum(
        "shqk,skhd->sqhd", enc_weights, value_rows, preferred_element_type=f32
    ).astype(bf16)
    att_flat = attended.reshape(-1, enc_cols)
    enc_part = (
        enc_x.reshape(-1, DE).astype(f32) / n_mp
        + jnp.dot(att_flat, w_out_enc, preferred_element_type=f32)
    ).astype(bf16)
    return (enc_part.reshape(count, R, DE), (key_rows, value_rows, enc_full, attended))


def encoder_backward(enc_x, grad_encoded, saved, w_out_enc):
    f32 = jnp.float32
    bf16 = jnp.bfloat16
    key_rows, value_rows, enc_full, attended = saved
    count, _, heads_enc, _ = attended.shape
    enc_cols = heads_enc * EHD
    att_flat = attended.reshape(-1, enc_cols)
    grad_out_part = lax.dot_general(
        att_flat, grad_encoded, (((0,), (0,)), ((), ())), preferred_element_type=f32
    )
    grad_att = lax.dot_general(
        grad_encoded, w_out_enc, (((1,), (1,)), ((), ())), preferred_element_type=f32
    ).astype(bf16)
    grad_att = grad_att.reshape(count, R, heads_enc, EHD)
    enc_grad_probs = jnp.einsum("sqhd,skhd->shqk", grad_att, value_rows, preferred_element_type=f32)
    enc_rows = jnp.einsum("sqhd,sqhd->shq", grad_att, attended, preferred_element_type=f32)
    enc_grad_scores = softmax_grad(enc_full, enc_grad_probs, enc_rows, math.sqrt(EHD))
    grad_enc_query = (
        jnp.einsum("shqk,skhd->sqhd", enc_grad_scores, key_rows, preferred_element_type=f32)
        .astype(bf16)
        .reshape(-1, enc_cols)
    )
    grad_query_part = lax.dot_general(
        enc_x.reshape(-1, DE), grad_enc_query, (((0,), (0,)), ((), ())), preferred_element_type=f32
    )
    return (grad_query_part, grad_out_part)


def body(
    span_states,
    queries,
    out_grad,
    neighbour_ids,
    assignment,
    embed_table,
    w_span_kv,
    w_query_enc,
    w_out_enc,
    w_dec_kv,
):
    f32 = jnp.float32
    bf16 = jnp.bfloat16
    n_span = lax.axis_size("span")
    n_mp = lax.axis_size("mp")
    span_index = lax.axis_index("span")
    half_index = lax.axis_index("mp")
    seq_count, local_tokens, half_width = span_states.shape
    span_share = local_tokens // CH
    count_units = seq_count * span_share * NB
    slot_count = max(1, 2 * count_units // n_span)
    half_len = R // n_mp
    enc_cols = w_query_enc.shape[1]
    dec_cols = queries.shape[2]
    vocab_rows = embed_table.shape[0]
    n_slots = n_span * slot_count
    own_dest = lax.dynamic_index_in_dim(assignment[0, :, :, 0], span_index, 0, keepdims=False)
    targets = jnp.arange(n_span, dtype=jnp.int32)
    onehot = (own_dest[:, None] == targets[None, :]).astype(jnp.int32)
    own_rank = jnp.sum(onehot * jnp.cumsum(onehot, axis=0), axis=1) - 1
    slot_ids = jnp.arange(slot_count, dtype=jnp.int32)
    placing = (
        (own_dest[None, None, :] == targets[:, None, None])
        & (own_rank[None, None, :] == slot_ids[None, :, None])
    ).astype(bf16)
    ids_all = neighbour_ids.reshape(seq_count, n_span, span_share, NB, R)
    ids_all = jnp.transpose(ids_all, (1, 0, 2, 3, 4)).reshape(n_span, count_units, R)
    ids_half = lax.dynamic_slice_in_dim(ids_all, half_index * half_len, half_len, 2).reshape(-1)
    shifted = ids_half - span_index * vocab_rows
    inside = (shifted >= 0) & (shifted < vocab_rows)
    rows = jnp.take(embed_table, jnp.clip(shifted, 0, vocab_rows - 1), axis=0)
    own_embed = (
        lax.psum_scatter(
            jnp.where(inside[:, None], rows, jnp.zeros_like(rows)).astype(f32).astype(jnp.bfloat16),
            "span",
            scatter_dimension=0,
            tiled=True,
        )
        .astype(jnp.float32)
        .astype(bf16)
    )
    own_embed = own_embed.reshape(count_units, half_len, DE)
    kv_part = jnp.dot(
        span_states.reshape(-1, half_width), w_span_kv, preferred_element_type=f32
    ).astype(bf16)
    kv_wide = kv_part.reshape(seq_count, span_share, 1, CH, 2, n_mp, enc_cols)
    kv_wide = jnp.broadcast_to(kv_wide, (seq_count, span_share, NB, CH, 2, n_mp, enc_cols))
    kv_units = jnp.transpose(
        kv_wide.reshape(count_units, CH, 2, n_mp, enc_cols), (0, 3, 1, 2, 4)
    ).reshape(count_units, n_mp, CH, 2 * enc_cols)
    embed_slots = jnp.einsum(
        "ecu,urd->ecrd", placing, own_embed, preferred_element_type=f32
    ).astype(bf16)
    kv_slots = jnp.einsum("ecu,umrd->emcrd", placing, kv_units, preferred_element_type=f32).astype(
        bf16
    )
    embed_send = jnp.broadcast_to(
        embed_slots[:, None], (n_span, n_mp, slot_count, half_len, DE)
    ).reshape(n_span * n_mp, slot_count, half_len, DE)
    kv_send = kv_slots.reshape(n_span * n_mp, slot_count, CH, 2 * enc_cols)
    got_embed, got_kv = (
        lax.all_to_all(embed_send, ("span", "mp"), split_axis=0, concat_axis=0, tiled=True),
        lax.all_to_all(kv_send, ("span", "mp"), split_axis=0, concat_axis=0, tiled=True),
    )
    got_embed = got_embed.reshape(n_span, n_mp, slot_count, half_len, DE)
    enc_in = jnp.transpose(got_embed, (0, 2, 1, 3, 4))
    kv_sum = jnp.sum(got_kv.reshape(n_span, n_mp, slot_count, CH, 2 * enc_cols).astype(f32), axis=1)
    enc_x = enc_in.reshape(n_slots, R, DE)
    span_kv = kv_sum.astype(bf16).reshape(n_slots, CH, 2 * enc_cols)
    enc_part, saved = encoder_forward(enc_x, span_kv, w_query_enc, w_out_enc, n_mp)
    enc_part = enc_part.reshape(n_span, slot_count, R, DE)
    back_send = jnp.broadcast_to(enc_part[:, None], (n_span, n_mp, slot_count, R, DE)).reshape(
        n_span * n_mp, slot_count, R, DE
    )
    got_back = lax.all_to_all(
        back_send, ("span", "mp"), split_axis=0, concat_axis=0, tiled=True
    ).reshape(n_span, n_mp, slot_count, R, DE)
    encoded_slots = jnp.sum(got_back.astype(f32), axis=1).astype(bf16)
    encoded_units = jnp.einsum(
        "ecu,ecrd->urd", placing, encoded_slots, preferred_element_type=f32
    ).astype(bf16)
    n_groups = seq_count * span_share
    heads_dec = dec_cols // HD
    w_dec_flat = w_dec_kv.reshape(DE, 2 * dec_cols)
    dec_kv = (
        jnp.dot(encoded_units.reshape(-1, DE), w_dec_flat, preferred_element_type=f32)
        .astype(bf16)
        .reshape(n_groups, NB * R, 2, heads_dec, HD)
    )
    dec_keys = dec_kv[:, :, 0]
    dec_values = dec_kv[:, :, 1]
    dec_query = queries.reshape(n_groups, CH, heads_dec, HD)
    dec_scores = jnp.einsum(
        "cqhd,ckhd->chqk", dec_query, dec_keys, preferred_element_type=f32
    ) / math.sqrt(HD)
    dec_full = jax.nn.softmax(dec_scores, axis=-1)
    dec_weights = dec_full.astype(bf16)
    cross = jnp.einsum(
        "chqk,ckhd->cqhd", dec_weights, dec_values, preferred_element_type=f32
    ).astype(bf16)
    cross_out = cross.reshape(seq_count, local_tokens, dec_cols)
    grad_cross = out_grad.reshape(n_groups, CH, heads_dec, HD)
    grad_values = jnp.einsum(
        "chqk,cqhd->ckhd", dec_weights, grad_cross, preferred_element_type=f32
    ).astype(bf16)
    grad_probs = jnp.einsum("cqhd,ckhd->chqk", grad_cross, dec_values, preferred_element_type=f32)
    row_terms = jnp.einsum("cqhd,cqhd->chq", grad_cross, cross, preferred_element_type=f32)
    grad_scores = softmax_grad(dec_full, grad_probs, row_terms, math.sqrt(HD))
    grad_keys = jnp.einsum(
        "chqk,cqhd->ckhd", grad_scores, dec_query, preferred_element_type=f32
    ).astype(bf16)
    grad_kv = jnp.stack([grad_keys, grad_values], axis=2).reshape(-1, 2 * dec_cols)
    grad_enc_part = lax.dot_general(
        grad_kv, w_dec_flat, (((1,), (1,)), ((), ())), preferred_element_type=f32
    ).astype(bf16)
    grad_enc_part = grad_enc_part.reshape(count_units, R, DE)
    grad_slots = jnp.einsum(
        "ecu,urd->ecrd", placing, grad_enc_part, preferred_element_type=f32
    ).astype(bf16)
    grad_send = jnp.broadcast_to(grad_slots[:, None], (n_span, n_mp, slot_count, R, DE)).reshape(
        n_span * n_mp, slot_count, R, DE
    )
    got_grad = lax.all_to_all(
        grad_send, ("span", "mp"), split_axis=0, concat_axis=0, tiled=True
    ).reshape(n_span, n_mp, slot_count, R, DE)
    grad_sum = jnp.sum(got_grad.astype(f32), axis=1)
    grad_encoded = grad_sum.astype(bf16).reshape(n_slots * R, DE)
    grad_query_part, grad_out_part = encoder_backward(enc_x, grad_encoded, saved, w_out_enc)
    attended_out = saved[3].reshape(1, 1, n_span, slot_count, R, enc_cols)
    grad_query_enc, grad_out_enc = (
        lax.psum_scatter(grad_query_part, ("span", "dp"), scatter_dimension=0, tiled=True),
        lax.psum_scatter(grad_out_part, ("span", "dp"), scatter_dimension=1, tiled=True),
    )
    return (cross_out, attended_out, grad_query_enc, grad_out_enc)


def solution(mesh):
    return jax.shard_map(
        body,
        mesh=mesh,
        in_specs=(
            P("dp", "span", "mp"),
            P("dp", "span", "mp"),
            P("dp", "span", "mp"),
            P("dp", None, None, None),
            P("dp", None, None, None),
            P("span", None),
            P("mp", None),
            P(None, "mp"),
            P("mp", None),
            P(None, None, "mp"),
        ),
        out_specs=(
            P("dp", "span", "mp"),
            P("dp", "span", None, None, None, "mp"),
            P(("span", "dp"), "mp"),
            P("mp", ("span", "dp")),
        ),
        check_vma=False,
    )
```

profile of v0, /device:TPU:0, one launch (start us, length us, event | category | flops | bytes accessed | tf_op | source)
XLA Modules:
  0.0 836.5 jit_solution(4471768899877448812)
XLA Ops:
  8.8 42.5 %gather_fusion = bf16[8192,896]{1,0:T(8,128)(2,1)} fusion(bf16[4000,896]{1,0:T(8,128)(2,1)} %param.15, s32[8192]{0:T(1024)S(1)} %broadcast_clamp_fusion), kind=kCustom, calls=%fused_computation | custom fusion | bytes 29392896 | tf_op jit(solution)/shard_map/jit(_take)/gather | solution.py:118
  51.3 15.8 %select_select_fusion = bf16[8192,896]{1,0:T(8,128)(2,1)} fusion(bf16[8192,896]{1,0:T(8,128)(2,1)} %gather_fusion, pred[8192]{0:T(1024)(128)(4,1)S(1)} %compare_and_fusion.1, pred[8192]{0:T(1024)(128)(4,1)S(1)} %and.67), kind=kLoop, calls=%fused_computation.4 | loop fusion | flops 14680064 | bytes 29376512 | tf_op jit(solution)/shard_map/jit(_where)/select_n | solution.py:121
  68.2 5.1 convolution_convert_fusion.2
  76.6 2.6 reshape.313
  79.3 2.8 convert_bitcast_fusion.1
  82.1 2.7 copy.146
  84.8 11.1 %all-to-all-start.1 = ((bf16[32,1,64,896]{3,2,1,0:T(8,128)(2,1)}), bf16[32,1,64,896]{3,2,1,0:T(8,128)(2,1)}, u32[]{:S(2)}, u32[]{:S(2)}) async-start(bf16[32,1,64,896]{3,2,1,0:T(8,128)(2,1)} %bitcast.214), calls=%async_computation.2 | async-start | bytes 7340032 | tf_op jit(solution)/shard_map/all_to_all | solution.py:150
  95.9 117.3 %reduce-scatter.6.cloned.1.call-done = bf16[512,896]{1,0:T(8,128)(2,1)} async-done(((bf16[8192,896]{1,0:T(8,128)(2,1)}), bf16[512,896]{1,0:T(8,128)(2,1)}) %reduce-scatter.6.cloned.1.call-update) | async-done | bytes 917520 | tf_op jit(solution)/shard_map/reduce_scatter | solution.py:120
  213.2 2.0 convolution_convert_fusion.5
  215.6 2.3 broadcast_in_dim.69
  217.9 7.3 all-to-all-start
  225.3 2.6 bitcast_reduce_fusion.2
  231.1 41.7 %all-to-all-done = bf16[32,1,64,896]{3,2,1,0:T(8,128)(2,1)} async-done(((bf16[32,1,64,896]{3,2,1,0:T(8,128)(2,1)}), bf16[32,1,64,896]{3,2,1,0:T(8,128)(2,1)}, u32[]{:S(2)}, u32[]{:S(2)}) %all-to-all-start) | async-done | bytes 3670048 | tf_op jit(solution)/shard_map/all_to_all | solution.py:149
  272.9 4.3 fusion.45
  278.9 5.2 fusion.94
  288.4 5.3 add_convert_fusion
  293.7 4.1 broadcast_in_dim.74
  297.8 10.6 %all-to-all-start.2 = ((bf16[32,1,128,896]{3,2,1,0:T(8,128)(2,1)}), bf16[32,1,128,896]{3,2,1,0:T(8,128)(2,1)}, u32[]{:S(2)}, u32[]{:S(2)}) async-start(bf16[32,1,128,896]{3,2,1,0:T(8,128)(2,1)} %bitcast.210), calls=%async_computation.3 | async-start | bytes 14680064 | tf_op jit(solution)/shard_map/all_to_all | solution.py:162
  308.5 5.2 copy.189
  313.9 95.4 %all-to-all-done.2 = bf16[32,1,128,896]{3,2,1,0:T(8,128)(2,1)} async-done(((bf16[32,1,128,896]{3,2,1,0:T(8,128)(2,1)}), bf16[32,1,128,896]{3,2,1,0:T(8,128)(2,1)}, u32[]{:S(2)}, u32[]{:S(2)}) %all-to-all-start.2) | async-done | bytes 7340064 | tf_op jit(solution)/shard_map/all_to_all | solution.py:162
  409.3 4.2 bitcast_reduce_fusion.1
  413.5 2.1 fusion.40
  417.7 4.9 convert_bitcast_fusion
  424.0 2.1 fusion.92
  426.9 1.8 fusion.95
  428.7 6.4 bitcast_convert_fusion.1
  435.1 5.7 convert_bitcast_fusion.2
  440.8 1.9 multiply_reduce_fusion.2
  442.7 5.3 convert_bitcast_fusion.3
  448.1 2.0 pad_maximum_fusion
  450.1 4.9 copy.161
  454.9 7.3 reshape.328
  462.2 7.8 convolution_convert_fusion.4
  470.1 2.6 convolution_convert_fusion.3
  474.6 103.8 %all_to_all.20 = bf16[32,1,128,896]{3,2,1,0:T(8,128)(2,1)} all-to-all(bf16[32,1,128,896]{3,2,1,0:T(8,128)(2,1)S(1)} %bitcast.211), channel_id=1, replica_groups=mesh['span'=16,'dp'=4,'mp'=2] {'span','mp'}, dimensions={0} | all-to-all | bytes 14680064 | tf_op jit(solution)/shard_map/all_to_all | solution.py:210
  578.4 4.3 bitcast_reduce_fusion
  582.7 2.1 fusion.46
  584.8 3.4 fusion.26
  591.6 3.6 fusion.2
  595.2 7.5 convert_bitcast_fusion.4
  602.7 2.7 copy.167
  605.4 5.8 fusion.23
  611.2 164.1 %fusion.91 = (f32[16,448]{1,0:T(8,128)S(1)}, f32[448,16]{0,1:T(8,128)S(1)}) fusion(f32[896,448]{1,0:T(8,128)} %fusion.23, f32[448,896]{0,1:T(8,128)S(1)} %copy-done.10), kind=kCustom, calls=%all-reduce-scatter.2 | all-reduce-scatter fusion | flops 917505 | bytes 3269120
  785.8 4.5 collective-permute-start.14
  796.3 15.8 %collective-permute-start.12 = (f32[448,16]{0,1:T(8,128)S(1)}, f32[448,16]{0,1:T(8,128)S(1)}, u32[]{:S(2)}, u32[]{:S(2)}) collective-permute-start(f32[448,16]{0,1:T(8,128)S(1)} %get-tuple-element.31), channel_id=1, source_target_pairs={{0,10},{2,12},{4,14},{6,16},{8,18},{10,20},{12,22},{14,24},{16,26}... | collective-permute-start | bytes 86024
  812.1 2.7 collective-permute-start.11
  815.9 5.3 collective-permute-start.10
  821.2 4.2 collective-permute-start.9
  (119 shorter events, 45.6 us)
Async XLA Ops:
  7.2 61.0 %copy-start = (bf16[2,128,2048]{2,1,0:T(8,128)(2,1)S(1)}, bf16[2,128,2048]{2,1,0:T(8,128)(2,1)}, u32[]{:S(2)}) copy-start(bf16[2,128,2048]{2,1,0:T(8,128)(2,1)} %param.10) | copy-start | bytes 3145732
  7.2 206.0 %reduce-scatter.6.cloned.1.call-start = ((), (), s32[]{:S(2)}) async-start(), calls=%async_computation.5 | async-start | bytes 15597568 | tf_op jit(solution)/shard_map/reduce_scatter | solution.py:120
  67.1 0.7 copy-start.17
  84.8 130.9 %all-to-all-start.1 = ((bf16[32,1,64,896]{3,2,1,0:T(8,128)(2,1)}), bf16[32,1,64,896]{3,2,1,0:T(8,128)(2,1)}, u32[]{:S(2)}, u32[]{:S(2)}) async-start(bf16[32,1,64,896]{3,2,1,0:T(8,128)(2,1)} %bitcast.214), calls=%async_computation.2 | async-start | bytes 7340032 | tf_op jit(solution)/shard_map/all_to_all | solution.py:150
  217.9 54.9 %all-to-all-start = ((bf16[32,1,64,896]{3,2,1,0:T(8,128)(2,1)}), bf16[32,1,64,896]{3,2,1,0:T(8,128)(2,1)}, u32[]{:S(2)}, u32[]{:S(2)}) async-start(bf16[32,1,64,896]{3,2,1,0:T(8,128)(2,1)} %bitcast.215), calls=%async_computation.1 | async-start | bytes 7340032 | tf_op jit(solution)/shard_map/all_to_all | solution.py:149
  231.1 46.6 %copy-start.2 = (bf16[16,64,448]{1,2,0:T(8,128)(2,1)}, bf16[16,64,448]{1,2,0:T(8,128)(2,1)S(1)}, u32[]{:S(2)}) copy-start(bf16[16,64,448]{1,2,0:T(8,128)(2,1)S(1)} %copy.186) | copy-start | bytes 2752516
  278.9 5.2 copy-start.13
  284.2 1.8 copy-start.7
  286.0 1.2 copy-start.4
  286.0 2.4 copy-start.19
  288.4 5.3 copy-start.11
  297.8 111.5 %all-to-all-start.2 = ((bf16[32,1,128,896]{3,2,1,0:T(8,128)(2,1)}), bf16[32,1,128,896]{3,2,1,0:T(8,128)(2,1)}, u32[]{:S(2)}, u32[]{:S(2)}) async-start(bf16[32,1,128,896]{3,2,1,0:T(8,128)(2,1)} %bitcast.210), calls=%async_computation.3 | async-start | bytes 14680064 | tf_op jit(solution)/shard_map/all_to_all | solution.py:162
  308.4 5.3 copy-start.14
  308.5 5.3 copy-start.15
  415.7 2.0 copy-start.8
  442.7 5.3 copy-start.9
  578.4 4.3 copy-start.20
  582.7 2.1 copy-start.12
  588.7 1.3 copy-start.6
  590.1 1.5 copy-start.5
  591.6 3.6 copy-start.3
  605.4 5.8 copy-start.10
  611.2 182.5 %copy-start.18 = (u32[128]{0:T(128)S(1)}, u32[128]{0:T(128)}, u32[]{:S(2)}) copy-start(u32[128]{0:T(128)} %constant.80) | copy-start | bytes 1540
  611.2 183.7 %copy-start.16 = (bf16[4,8,128,64]{2,3,1,0:T(8,128)(2,1)S(1)}, bf16[4,8,128,64]{2,3,1,0:T(8,128)(2,1)}, u32[]{:S(2)}) copy-start(bf16[4,8,128,64]{2,3,1,0:T(8,128)(2,1)} %get-tuple-element.41) | copy-start | bytes 1572868
  611.2 218.0 %copy-start.1 = (bf16[2,128,2048]{2,1,0:T(8,128)(2,1)S(1)}, bf16[2,128,2048]{2,1,0:T(8,128)(2,1)}, u32[]{:S(2)}) copy-start(bf16[2,128,2048]{2,1,0:T(8,128)(2,1)} %param.10) | copy-start | bytes 3145732
  775.4 6.5 collective-permute-start.7
  776.7 6.5 collective-permute-start.6
  778.0 6.5 collective-permute-start.5
  779.3 6.5 collective-permute-start.4
  780.6 9.8 %collective-permute-start.3 = (f32[16,448]{1,0:T(8,128)S(1)}, f32[16,448]{1,0:T(8,128)S(1)}, u32[]{:S(2)}, u32[]{:S(2)}) collective-permute-start(f32[16,448]{1,0:T(8,128)S(1)} %get-tuple-element.30), channel_id=1, source_target_pairs={{0,8},{2,10},{4,12},{6,14},{8,16},{10,18},{12,20},{14,22},{16,24},... | collective-permute-start | bytes 86024
  781.9 10.1 %collective-permute-start.2 = (f32[16,448]{1,0:T(8,128)S(1)}, f32[16,448]{1,0:T(8,128)S(1)}, u32[]{:S(2)}, u32[]{:S(2)}) collective-permute-start(f32[16,448]{1,0:T(8,128)S(1)} %get-tuple-element.30), channel_id=1, source_target_pairs={{0,6},{2,8},{4,10},{6,12},{8,14},{10,16},{12,18},{14,20},{16,22},{... | collective-permute-start | bytes 86024
  783.2 13.1 %collective-permute-start.1 = (f32[16,448]{1,0:T(8,128)S(1)}, f32[16,448]{1,0:T(8,128)S(1)}, u32[]{:S(2)}, u32[]{:S(2)}) collective-permute-start(f32[16,448]{1,0:T(8,128)S(1)} %get-tuple-element.30), channel_id=1, source_target_pairs={{0,4},{2,6},{4,8},{6,10},{8,12},{10,14},{12,16},{14,18},{16,20},{1... | collective-permute-start | bytes 86024
  784.5 27.6 %collective-permute-start = (f32[16,448]{1,0:T(8,128)S(1)}, f32[16,448]{1,0:T(8,128)S(1)}, u32[]{:S(2)}, u32[]{:S(2)}) collective-permute-start(f32[16,448]{1,0:T(8,128)S(1)} %get-tuple-element.30), channel_id=1, source_target_pairs={{0,2},{2,4},{4,6},{6,8},{8,10},{10,12},{12,14},{14,16},{16,18},{18... | collective-permute-start | bytes 86024
  785.8 35.4 %collective-permute-start.14 = (f32[448,16]{0,1:T(8,128)S(1)}, f32[448,16]{0,1:T(8,128)S(1)}, u32[]{:S(2)}, u32[]{:S(2)}) collective-permute-start(f32[448,16]{0,1:T(8,128)S(1)} %get-tuple-element.31), channel_id=1, source_target_pairs={{0,14},{2,16},{4,18},{6,20},{8,22},{10,24},{12,26},{14,28},{16,30}... | collective-permute-start | bytes 86024
  790.4 35.1 %collective-permute-start.13 = (f32[448,16]{0,1:T(8,128)S(1)}, f32[448,16]{0,1:T(8,128)S(1)}, u32[]{:S(2)}, u32[]{:S(2)}) collective-permute-start(f32[448,16]{0,1:T(8,128)S(1)} %get-tuple-element.31), channel_id=1, source_target_pairs={{0,12},{2,14},{4,16},{6,18},{8,20},{10,22},{12,24},{14,26},{16,28}... | collective-permute-start | bytes 86024
  792.0 23.9 %collective-permute-start.15 = (f32[448,14]{0,1:T(8,128)S(1)}, f32[448,14]{0,1:T(8,128)S(1)}, u32[]{:S(2)}, u32[]{:S(2)}) collective-permute-start(f32[448,14]{0,1:T(8,128)S(1)} %slice.23), channel_id=1, source_target_pairs={{0,16},{2,18},{4,20},{6,22},{8,24},{10,26},{12,28},{14,30},{16,32}... | collective-permute-start | bytes 75272
  796.3 31.1 %collective-permute-start.12 = (f32[448,16]{0,1:T(8,128)S(1)}, f32[448,16]{0,1:T(8,128)S(1)}, u32[]{:S(2)}, u32[]{:S(2)}) collective-permute-start(f32[448,16]{0,1:T(8,128)S(1)} %get-tuple-element.31), channel_id=1, source_target_pairs={{0,10},{2,12},{4,14},{6,16},{8,18},{10,20},{12,22},{14,24},{16,26}... | collective-permute-start | bytes 86024
  812.1 15.3 %collective-permute-start.11 = (f32[448,16]{0,1:T(8,128)S(1)}, f32[448,16]{0,1:T(8,128)S(1)}, u32[]{:S(2)}, u32[]{:S(2)}) collective-permute-start(f32[448,16]{0,1:T(8,128)S(1)} %get-tuple-element.31), channel_id=1, source_target_pairs={{0,8},{2,10},{4,12},{6,14},{8,16},{10,18},{12,20},{14,22},{16,24},... | collective-permute-start | bytes 86024
  815.9 11.5 %collective-permute-start.10 = (f32[448,16]{0,1:T(8,128)S(1)}, f32[448,16]{0,1:T(8,128)S(1)}, u32[]{:S(2)}, u32[]{:S(2)}) collective-permute-start(f32[448,16]{0,1:T(8,128)S(1)} %get-tuple-element.31), channel_id=1, source_target_pairs={{0,6},{2,8},{4,10},{6,12},{8,14},{10,16},{12,18},{14,20},{16,22},{... | collective-permute-start | bytes 86024
  821.2 6.2 collective-permute-start.9
  825.5 2.1 collective-permute-start.8
Sparse Core Ops, SparseCore 0:
  67.3 145.8 reduce-scatter.5
where the time goes:
time: 849 us; the launch traced here: 837 us
  blocking collectives  268 us (32%)
  waiting for transfers between devices  255 us (30%)
  local copies, waits for them, and re-layouts  103 us (12%)
  starting transfers between devices  76.6 us (9%)
  matrix products  75.9 us (9%)
  other arithmetic  42.3 us (5%)
  between operations  16 us (2%)
    unnamed x1, blocking collectives  164 us
    reduce_scatter x1, waiting for transfers between devices, body(): lax.psum_scatter(jnp.where(inside[:, None], rows, jnp.zeros_like(rows)).a...  117 us
    all_to_all x1, blocking collectives, body(): lax.all_to_all(grad_send, ('span', 'mp'), split_axis=0, concat_axis=0, ti...  104 us
    all_to_all x1, waiting for transfers between devices, body(): lax.all_to_all(back_send, ('span', 'mp'), split_axis=0, concat_axis=0, ti...  95.4 us
    unnamed x16, starting transfers between devices  47.5 us
    gather x1, local copies, waits for them, and re-layouts, body(): rows = jnp.take(embed_table, jnp.clip(shifted, 0, vocab_rows - 1), axis=0)  42.5 us
    all_to_all x1, waiting for transfers between devices, body(): lax.all_to_all(embed_send, ('span', 'mp'), split_axis=0, concat_axis=0, t...  41.7 us
    unnamed x56, local copies, waits for them, and re-layouts  19.9 us
  transfers between devices with their start and end apart: 20, of which 4 were waited for; matrix products, arithmetic and copies ran while one was open for 4% of the time, Pallas kernels for 0%

commit v1 on v0

v1 whole, which is shorter than its diff:
```python
import math

import jax
import jax.numpy as jnp
from jax import lax
from jax.sharding import PartitionSpec as P

HD = 128
DE = 896
EHD = 64
R = 128
CH = 64
NB = 2
ROOM = 48


def softmax_grad(probs_full, grad_probs, row_terms, scale):
    return (probs_full * (grad_probs - row_terms[..., None]) / scale).astype(jnp.bfloat16)


def lists(ids_m, span_index, vocab_rows, n_span):
    tokens = ids_m.shape[1]
    t = jnp.arange(tokens, dtype=jnp.int32)
    same = ids_m[:, :, None] == ids_m[:, None, :]
    dup = jnp.any(same & (t[None, None, :] < t[None, :, None]), axis=2)
    uniq = jnp.logical_not(dup)
    src = ids_m // vocab_rows
    shards = jnp.arange(n_span, dtype=jnp.int32)
    counts = jnp.sum(
        (uniq[:, None, :] & (src[:, None, :] == shards[None, :, None])).astype(jnp.int32), axis=2
    )
    over = jnp.max(counts) > ROOM
    sel = uniq & (src == span_index)
    tri = (t[:, None] < t[None, :]).astype(jnp.bfloat16)
    rank = jnp.dot(sel.astype(jnp.bfloat16), tri, preferred_element_type=jnp.float32).astype(
        jnp.int32
    )
    room = jnp.arange(ROOM, dtype=jnp.int32)
    local = ids_m - span_index * vocab_rows
    rows = jnp.sum(
        jnp.where(
            (rank[:, None, :] == room[None, :, None]) & sel[:, None, :], local[:, None, :], 0
        ),
        axis=2,
    )
    own = lax.dynamic_index_in_dim(ids_m, span_index, 0, keepdims=False)
    own_src = own // vocab_rows
    own_same = own[:, None] == own[None, :]
    first = jnp.min(jnp.where(own_same, t[None, :], tokens), axis=1)
    own_uniq = first == t
    own_rank = jnp.sum(
        (
            own_uniq[None, :]
            & (own_src[:, None] == own_src[None, :])
            & (t[None, :] < first[:, None])
        ).astype(jnp.int32),
        axis=1,
    )
    return rows, own_src * ROOM + own_rank, over


def body(
    span_states,
    queries,
    out_grad,
    neighbour_ids,
    assignment,
    embed_table,
    w_span_kv,
    w_query_enc,
    w_out_enc,
    w_dec_kv,
):
    f32 = jnp.float32
    bf16 = jnp.bfloat16
    n_span = lax.axis_size("span")
    span_index = lax.axis_index("span")
    half_index = lax.axis_index("mp")
    seq_count, local_tokens, half_width = span_states.shape
    spans = local_tokens // CH
    units = spans * NB
    dec_cols = 2 * queries.shape[2]
    heads_dec = dec_cols // HD
    heads_enc = DE // EHD
    enc_cols = w_query_enc.shape[1]
    vocab_rows = embed_table.shape[0]
    tokens = units * R

    ids_m = lax.dynamic_index_in_dim(
        neighbour_ids.reshape(seq_count, n_span, tokens), half_index, 0, keepdims=False
    )
    rows, pos, over = lists(ids_m, span_index, vocab_rows, n_span)
    over = lax.pmax(over.astype(jnp.int32), ("dp", "mp"))
    sent = jnp.take(embed_table, rows.reshape(-1), axis=0).reshape(n_span, ROOM, DE)
    got = lax.all_to_all(sent, "span", split_axis=0, concat_axis=0, tiled=True)
    pick = (pos[:, None] == jnp.arange(n_span * ROOM, dtype=jnp.int32)[None, :]).astype(bf16)
    embedded = jnp.dot(pick, got.reshape(-1, DE), preferred_element_type=f32).astype(bf16)

    def whole_gather(_):
        shifted = ids_m.reshape(-1) - span_index * vocab_rows
        inside = (shifted >= 0) & (shifted < vocab_rows)
        found = jnp.take(embed_table, jnp.clip(shifted, 0, vocab_rows - 1), axis=0)
        return lax.psum_scatter(
            jnp.where(inside[:, None], found, jnp.zeros_like(found)),
            "span",
            scatter_dimension=0,
            tiled=True,
        )

    embedded = lax.cond(over > 0, whole_gather, lambda e: e, embedded)

    kv_part = jnp.dot(
        span_states.reshape(-1, half_width), w_span_kv, preferred_element_type=f32
    ).astype(bf16)
    kv_part = kv_part.reshape(seq_count, local_tokens, 2 * DE)
    kv_both = lax.all_to_all(kv_part, "mp", split_axis=0, concat_axis=0, tiled=True)
    kv = jnp.sum(kv_both.astype(f32), axis=0).astype(bf16)

    def swap_heads(x):
        both = lax.all_to_all(x, "mp", split_axis=0, concat_axis=0, tiled=True)
        return jnp.transpose(both, (1, 0, 2)).reshape(local_tokens, dec_cols)

    q = swap_heads(queries)
    og = swap_heads(out_grad)
    w_q = lax.all_gather(w_query_enc, "mp", axis=1, tiled=True)
    w_o = lax.all_gather(w_out_enc, "mp", axis=0, tiled=True)
    w_d = lax.all_gather(w_dec_kv, "mp", axis=2, tiled=True).reshape(DE, 2 * dec_cols)

    kv = kv.reshape(spans, CH, 2, heads_enc, EHD)
    keys, values = kv[:, :, 0], kv[:, :, 1]
    enc_query = (
        jnp.dot(embedded, w_q, preferred_element_type=f32)
        .astype(bf16)
        .reshape(spans, NB * R, heads_enc, EHD)
    )
    scores = jnp.einsum("cqhd,ckhd->chqk", enc_query, keys, preferred_element_type=f32) / math.sqrt(
        EHD
    )
    enc_full = jax.nn.softmax(scores, axis=-1)
    attended = jnp.einsum(
        "chqk,ckhd->cqhd", enc_full.astype(bf16), values, preferred_element_type=f32
    ).astype(bf16)
    att_flat = attended.reshape(tokens, DE)
    encoded = (embedded.astype(f32) + jnp.dot(att_flat, w_o, preferred_element_type=f32)).astype(
        bf16
    )

    halves = jnp.transpose(att_flat.reshape(units, R, 2, enc_cols), (2, 0, 1, 3))
    all_units = lax.all_to_all(halves, "mp", split_axis=0, concat_axis=0, tiled=True).reshape(
        seq_count * units, R, enc_cols
    )
    dest = lax.dynamic_index_in_dim(assignment[0, :, :, 0], span_index, 0, keepdims=False)
    placing = (dest[None, :] == jnp.arange(n_span, dtype=jnp.int32)[:, None]).astype(bf16)
    slots = jnp.einsum("eu,urd->erd", placing, all_units, preferred_element_type=f32).astype(bf16)
    attended_out = lax.all_to_all(slots, "span", split_axis=0, concat_axis=0, tiled=True)
    attended_out = attended_out.reshape(1, 1, n_span, 1, R, enc_cols)

    dec_kv = (
        jnp.dot(encoded, w_d, preferred_element_type=f32)
        .astype(bf16)
        .reshape(spans, NB * R, 2, heads_dec, HD)
    )
    dec_keys, dec_values = dec_kv[:, :, 0], dec_kv[:, :, 1]
    dec_query = q.reshape(spans, CH, heads_dec, HD)
    dec_scores = jnp.einsum(
        "cqhd,ckhd->chqk", dec_query, dec_keys, preferred_element_type=f32
    ) / math.sqrt(HD)
    dec_full = jax.nn.softmax(dec_scores, axis=-1)
    dec_weights = dec_full.astype(bf16)
    cross = jnp.einsum(
        "chqk,ckhd->cqhd", dec_weights, dec_values, preferred_element_type=f32
    ).astype(bf16)
    cross_halves = jnp.transpose(cross.reshape(local_tokens, 2, dec_cols // 2), (1, 0, 2))
    cross_out = lax.all_to_all(cross_halves, "mp", split_axis=0, concat_axis=0, tiled=True)
    grad_cross = og.reshape(spans, CH, heads_dec, HD)
    grad_values = jnp.einsum(
        "chqk,cqhd->ckhd", dec_weights, grad_cross, preferred_element_type=f32
    ).astype(bf16)
    grad_probs = jnp.einsum("cqhd,ckhd->chqk", grad_cross, dec_values, preferred_element_type=f32)
    row_terms = jnp.einsum("cqhd,cqhd->chq", grad_cross, cross, preferred_element_type=f32)
    grad_scores = softmax_grad(dec_full, grad_probs, row_terms, math.sqrt(HD))
    grad_keys = jnp.einsum(
        "chqk,cqhd->ckhd", grad_scores, dec_query, preferred_element_type=f32
    ).astype(bf16)
    grad_kv = jnp.stack([grad_keys, grad_values], axis=2).reshape(tokens, 2 * dec_cols)
    grad_encoded = lax.dot_general(
        grad_kv, w_d, (((1,), (1,)), ((), ())), preferred_element_type=f32
    ).astype(bf16)

    grad_out_part = lax.dot_general(
        att_flat, grad_encoded, (((0,), (0,)), ((), ())), preferred_element_type=f32
    )
    grad_att = (
        lax.dot_general(grad_encoded, w_o, (((1,), (1,)), ((), ())), preferred_element_type=f32)
        .astype(bf16)
        .reshape(spans, NB * R, heads_enc, EHD)
    )
    enc_grad_probs = jnp.einsum("cqhd,ckhd->chqk", grad_att, values, preferred_element_type=f32)
    enc_rows = jnp.einsum("cqhd,cqhd->chq", grad_att, attended, preferred_element_type=f32)
    enc_grad_scores = softmax_grad(enc_full, enc_grad_probs, enc_rows, math.sqrt(EHD))
    grad_enc_query = (
        jnp.einsum("chqk,ckhd->cqhd", enc_grad_scores, keys, preferred_element_type=f32)
        .astype(bf16)
        .reshape(tokens, DE)
    )
    grad_query_part = lax.dot_general(
        embedded, grad_enc_query, (((0,), (0,)), ((), ())), preferred_element_type=f32
    )
    gq = lax.psum_scatter(grad_query_part, "mp", scatter_dimension=1, tiled=True)
    go = lax.psum_scatter(grad_out_part, "mp", scatter_dimension=0, tiled=True)
    grad_query_enc, grad_out_enc = (
        lax.psum_scatter(gq, ("span", "dp"), scatter_dimension=0, tiled=True),
        lax.psum_scatter(go, ("span", "dp"), scatter_dimension=1, tiled=True),
    )
    return (cross_out, attended_out, grad_query_enc, grad_out_enc)


def solution(mesh):
    return jax.shard_map(
        body,
        mesh=mesh,
        in_specs=(
            P("dp", "span", "mp"),
            P("dp", "span", "mp"),
            P("dp", "span", "mp"),
            P("dp", None, None, None),
            P("dp", None, None, None),
            P("span", None),
            P("mp", None),
            P(None, "mp"),
            P("mp", None),
            P(None, None, "mp"),
        ),
        out_specs=(
            P("dp", "span", "mp"),
            P("dp", "span", None, None, None, "mp"),
            P(("span", "dp"), "mp"),
            P("mp", ("span", "dp")),
        ),
        check_vma=False,
    )
```

time: 849 us -> 971 us (1.14)
  waiting for transfers between devices: 255 us -> 730 us
  blocking collectives: 268 us -> 21.6 us
  starting transfers between devices: 76.6 us -> 30.7 us
  local copies, waits for them, and re-layouts: 103 us -> 63.3 us
  other arithmetic: 42.3 us -> 19 us
    unnamed x17 -> x7, waiting for transfers between devices: 0.25 us -> 483 us
    unnamed x1 -> x0, blocking collectives: 164 us -> none
    all_gather x0 -> x3, waiting for transfers between devices: none -> 94.4 us  [the longest x1 72.7 us: body(): lax.all_gather(w_dec_kv, 'mp', axis=2, tiled=True).reshape(DE, 2 * dec_cols)]
    all_to_all x1, blocking collectives: 104 us -> 12.2 us  [swap_heads(): both = lax.all_to_all(x, 'mp', split_axis=0, concat_axis=0, tiled=True)]
    all_to_all x3 -> x6, waiting for transfers between devices: 137 us -> 72 us  [the longest x1 25.2 us: body(): lax.all_to_all(slots, 'span', split_axis=0, concat_axis=0, tiled=True)]
    unnamed x16 -> x1, starting transfers between devices: 47.5 us -> 0.04 us
    reduce_scatter x1 -> x2, waiting for transfers between devices: 117 us -> 80.6 us  [the longest x1 50 us: body(): lax.psum_scatter(grad_query_part, 'mp', scatter_dimension=1, tiled=True)]
    gather x1, local copies, waits for them, and re-layouts: 42.5 us -> 7.47 us  [body(): jnp.take(embed_table, rows.reshape(-1), axis=0).reshape(n_span, ROOM, DE)]
  transfers between devices with their start and end apart: 20 -> 12, of which waited for: 4 -> 11; matrix products, arithmetic and copies ran while one was open for 4% -> 6% of each run, Pallas kernels for 0% -> 0%
where the time goes in v1:
time: 971 us; the launch traced here: 961 us
  waiting for transfers between devices  730 us (75%)
  matrix products  77.7 us (8%)
  local copies, waits for them, and re-layouts  63.3 us (7%)
  starting transfers between devices  30.7 us (3%)
  blocking collectives  21.6 us (2%)
  other arithmetic  19 us (2%)
  between operations  18.5 us (2%)
    unnamed x7, waiting for transfers between devices  483 us
    all_gather x1, waiting for transfers between devices, body(): lax.all_gather(w_dec_kv, 'mp', axis=2, tiled=True).reshape(DE, 2 * dec_cols)  72.7 us
    reduce_scatter x1, waiting for transfers between devices, body(): lax.psum_scatter(grad_query_part, 'mp', scatter_dimension=1, tiled=True)  50 us
    reduce_scatter x1, waiting for transfers between devices, body(): go = lax.psum_scatter(grad_out_part, 'mp', scatter_dimension=0, tiled=True)  30.6 us
    all_to_all x1, waiting for transfers between devices, body(): lax.all_to_all(slots, 'span', split_axis=0, concat_axis=0, tiled=True)  25.2 us
    unnamed x46, local copies, waits for them, and re-layouts  22.9 us
    all_gather x1, waiting for transfers between devices, body(): w_o = lax.all_gather(w_out_enc, 'mp', axis=0, tiled=True)  21.7 us
    dot_general x1, matrix products, body(): jnp.dot(encoded, w_d, preferred_element_type=f32).astype(bf16)  19.5 us
  transfers between devices with their start and end apart: 12, of which 11 were waited for; matrix products, arithmetic and copies ran while one was open for 6% of the time, Pallas kernels for 0%

profile of v1, /device:TPU:0, one launch (start us, length us, event | category | flops | bytes accessed | tf_op | source)
XLA Modules:
  0.0 961.1 jit_solution(1085966607137883726)
XLA Ops:
  9.1 4.2 and_reduce_fusion
  14.1 7.5 gather_fusion.1
  22.9 8.1 all-to-all-start
  32.7 9.4 pmax.7
  43.6 9.2 all-to-all-done
  52.8 2.0 fusion.22
  55.9 12.2 %all_to_all.35 = bf16[2,128,1024]{2,1,0:T(8,128)(2,1)S(1)} all-to-all(bf16[2,128,1024]{2,1,0:T(8,128)(2,1)S(1)} %copy-done.12), channel_id=1, replica_groups=mesh['span'=16,'dp'=4,'mp'=2] {'mp'}, dimensions={0} | all-to-all | bytes 1048576 | tf_op jit(solution)/shard_map/all_to_all | solution.py:120
  68.1 3.5 all-to-all-start.6
  71.6 6.1 convolution_convert_fusion.1
  77.7 8.7 all-to-all-done.6
  86.4 3.6 all-to-all-start.1
  94.2 6.9 all-to-all-done.1
  102.0 1.7 fusion.71
  104.2 4.4 convolution_convert_fusion.5
  108.5 3.0 reshape.309
  113.6 1.7 fusion.72
  115.3 2.3 convolution_convert_fusion.7
  118.8 72.7 %all-gather.8.cloned.1.call-done = bf16[896,2,2048]{2,1,0:T(2,128)(2,1)} async-done(((bf16[896,2,1024]{2,1,0:T(2,128)(2,1)}), bf16[896,2,2048]{2,1,0:T(2,128)(2,1)}) %all-gather.8.cloned.1.call-update) | async-done | bytes 7340048 | tf_op jit(solution)/shard_map/all_gather | solution.py:127
  191.5 10.8 %copy.130 = bf16[112,8,2,2048]{3,1,2,0:T(8,128)(2,1)} copy(bf16[112,8,2,2048]{3,2,1,0:T(2,128)(2,1)} %bitcast.173) | data formatting | bytes 14680064
  202.3 21.7 %all-gather.6.cloned.1.call-done = bf16[896,896]{1,0:T(8,128)(2,1)} async-done(((bf16[448,896]{1,0:T(8,128)(2,1)}), bf16[896,896]{1,0:T(8,128)(2,1)}) %all-gather.6.cloned.1.call-update) | async-done | bytes 1605648 | tf_op jit(solution)/shard_map/all_gather | solution.py:126
  224.0 19.5 %fusion.3 = bf16[64,8,32,128]{3,1,2,0:T(8,128)(2,1)} fusion(bf16[896,4096]{1,0:T(8,128)(2,1)} %bitcast.174, bf16[512,896]{1,0:T(8,128)(2,1)} %get-tuple-element.68, bf16[512,896]{0,1:T(8,128)(2,1)S(1)} %bitcast.177, bf16[896,896]{1,0:T(8,128)(2,1)} %all-gather.6.cloned.1.call-done), kind=kOutput, calls=%fused_computation.17 | convolution fusion | flops 4583653376 | bytes 14974976 | tf_op jit(solution)/shard_map/dot_general | solution.py:159
  243.5 3.4 copy.131
  246.9 2.1 fusion.70
  249.9 1.8 fusion.73
  251.7 6.4 bitcast_convert_fusion.1
  258.1 6.8 convert_bitcast_fusion
  264.9 2.0 multiply_reduce_fusion.2
  267.0 5.7 convert_bitcast_fusion.1
  272.7 2.0 pad_maximum_fusion
  274.6 5.0 copy.92
  279.6 7.3 reshape.283
  286.9 8.9 convolution_convert_fusion.3
  295.9 2.8 fusion.76
  298.8 2.6 convolution_convert_fusion.4
  303.1 1.9 bitcast_convert_fusion
  306.7 3.7 fusion.23
  311.6 4.0 fusion.77
  315.6 30.6 %reduce-scatter.10.cloned.1.call-done = f32[448,896]{1,0:T(8,128)} async-done(((f32[896,896]{1,0:T(8,128)}), f32[448,896]{1,0:T(8,128)}) %reduce-scatter.10.cloned.1.call-update) | async-done | bytes 1605648 | tf_op jit(solution)/shard_map/reduce_scatter | solution.py:210
  346.3 50.0 %reduce-scatter.8.cloned.1.call-done = f32[896,448]{0,1:T(8,128)} async-done(((f32[896,896]{0,1:T(8,128)}), f32[896,448]{0,1:T(8,128)}) %reduce-scatter.8.cloned.1.call-update) | async-done | bytes 1605648 | tf_op jit(solution)/shard_map/reduce_scatter | solution.py:209
  396.3 1.5 reshape_reshape.10
  397.8 3.8 all-to-all-start.4
  401.9 14.6 %all-to-all-done.4 = bf16[2,4,128,448]{2,1,3,0:T(4,128)(2,1)S(1)} async-done(((bf16[2,4,128,448]{2,1,3,0:T(4,128)(2,1)}), bf16[2,4,128,448]{2,1,3,0:T(4,128)(2,1)S(1)}, u32[]{:S(2)}, u32[]{:S(2)}) %all-to-all-start.4) | async-done | bytes 917536 | tf_op jit(solution)/shard_map/all_to_all | solution.py:149
  417.6 1.7 copy.87
  419.3 7.7 all-to-all-start.5
  428.4 25.2 %all-to-all-done.5 = bf16[16,128,448]{1,2,0:T(8,128)(2,1)S(1)} async-done(((bf16[16,128,448]{1,2,0:T(8,128)(2,1)}), bf16[16,128,448]{1,2,0:T(8,128)(2,1)S(1)}, u32[]{:S(2)}, u32[]{:S(2)}) %all-to-all-start.5) | async-done | bytes 1835040 | tf_op jit(solution)/shard_map/all_to_all | solution.py:155
  453.6 3.5 all-to-all-start.3
  458.4 7.4 all-to-all-done.3
  465.8 481.6 %all-reduce.5.cloned.1.call-done = (f32[896,448]{0,1:T(8,128)}, f32[448,896]{1,0:T(8,128)}) async-done(((f32[896,448]{0,1:T(8,128)}, f32[448,896]{1,0:T(8,128)}), (f32[896,448]{0,1:T(8,128)}, f32[448,896]{1,0:T(8,128)})) %all-reduce.5.cloned.1.call-update) | async-done | bytes 3211280
  (98 shorter events, 29.5 us)
Async XLA Ops:
  8.0 63.6 %copy-start = (bf16[2,128,2048]{2,1,0:T(8,128)(2,1)S(1)}, bf16[2,128,2048]{2,1,0:T(8,128)(2,1)}, u32[]{:S(2)}) copy-start(bf16[2,128,2048]{2,1,0:T(8,128)(2,1)} %param.12) | copy-start | bytes 3145732
  22.9 29.9 %all-to-all-start = ((bf16[16,48,896]{2,1,0:T(8,128)(2,1)}), bf16[16,48,896]{2,1,0:T(8,128)(2,1)S(1)}, u32[]{:S(2)}, u32[]{:S(2)}) async-start(bf16[16,48,896]{2,1,0:T(8,128)(2,1)} %broadcast_select_fusion), calls=%async_computation.1 | async-start | bytes 2752512 | tf_op jit(solution)/shard_map/all_to_all | solution.py:95
  54.8 49.4 %all-gather.4.cloned.1.call-start = ((), (), s32[]{:S(2)}) async-start(), calls=%async_computation.11 | async-start | bytes 2408448 | tf_op jit(solution)/shard_map/all_gather | solution.py:125
  54.8 1.2 copy-start.12
  55.3 136.2 %all-gather.8.cloned.1.call-start = ((), (), s32[]{:S(2)}) async-start(), calls=%async_computation.13 | async-start | bytes 11010048 | tf_op jit(solution)/shard_map/all_gather | solution.py:127
  68.1 18.3 %all-to-all-start.6 = ((bf16[2,128,1024]{2,1,0:T(8,128)(2,1)}), bf16[2,128,1024]{2,1,0:T(8,128)(2,1)S(1)}, u32[]{:S(2)}, u32[]{:S(2)}) async-start(bf16[2,128,1024]{2,1,0:T(8,128)(2,1)} %param.14), calls=%async_computation.7 | async-start | bytes 1048576 | tf_op jit(solution)/shard_map/all_to_all | solution.py:120
  86.4 14.7 %all-to-all-start.1 = ((bf16[2,128,1792]{2,1,0:T(8,128)(2,1)}), bf16[2,128,1792]{2,1,0:T(8,128)(2,1)S(1)}, u32[]{:S(2)}, u32[]{:S(2)}) async-start(bf16[2,128,1792]{2,1,0:T(8,128)(2,1)} %bitcast.10), calls=%async_computation.2 | async-start | bytes 1835008 | tf_op jit(solution)/shard_map/all_to_all | solution.py:116
  90.0 134.0 %all-gather.6.cloned.1.call-start = ((), (), s32[]{:S(2)}) async-start(), calls=%async_computation.12 | async-start | bytes 2408448 | tf_op jit(solution)/shard_map/all_gather | solution.py:126
  90.6 255.7 %reduce-scatter.10.cloned.1.call-start = ((), (), s32[]{:S(2)}) async-start(), calls=%async_computation.15 | async-start | bytes 4816896 | tf_op jit(solution)/shard_map/reduce_scatter | solution.py:210
  104.1 7.4 copy-start.10
  112.3 1.3 copy-start.2
  113.6 1.7 copy-start.14
  117.6 1.0 copy-start.5
  118.8 105.2 %copy-start.3 = (bf16[112,8,2,256]{3,1,2,0:T(8,128)(2,1)}, bf16[112,8,2,256]{3,1,2,0:T(8,128)(2,1)S(1)}, u32[]{:S(2)}) copy-start(bf16[112,8,2,256]{3,1,2,0:T(8,128)(2,1)S(1)} %copy.129) | copy-start | bytes 2752516
  246.9 2.1 copy-start.8
  267.0 5.7 copy-start.9
  286.9 9.0 copy-start.4
  298.7 97.6 %reduce-scatter.8.cloned.1.call-start = ((), (), s32[]{:S(2)}) async-start(), calls=%async_computation.14 | async-start | bytes 4816896 | tf_op jit(solution)/shard_map/reduce_scatter | solution.py:209
  301.9 3.1 copy-start.6
  305.0 1.5 copy-start.7
  305.1 1.7 copy-start.11
  315.6 631.8 %all-reduce.5.cloned.1.call-start = ((), (), s32[]{:S(2)}) async-start(), calls=%async_computation.16 | async-start | bytes 6422528
  396.3 5.3 copy-start.15
  397.8 18.7 %all-to-all-start.4 = ((bf16[2,4,128,448]{2,1,3,0:T(4,128)(2,1)}), bf16[2,4,128,448]{2,1,3,0:T(4,128)(2,1)S(1)}, u32[]{:S(2)}, u32[]{:S(2)}) async-start(bf16[2,4,128,448]{2,1,3,0:T(4,128)(2,1)} %bitcast.21), calls=%async_computation.5 | async-start | bytes 1835008 | tf_op jit(solution)/shard_map/all_to_all | solution.py:149
  419.3 7.7 copy-start.13
  419.3 34.3 %all-to-all-start.5 = ((bf16[16,128,448]{1,2,0:T(8,128)(2,1)}), bf16[16,128,448]{1,2,0:T(8,128)(2,1)S(1)}, u32[]{:S(2)}, u32[]{:S(2)}) async-start(bf16[16,128,448]{1,2,0:T(8,128)(2,1)} %copy.87), calls=%async_computation.6 | async-start | bytes 3670016 | tf_op jit(solution)/shard_map/all_to_all | solution.py:155
  427.0 30.1 %copy-start.16 = (u32[128]{0:T(128)S(1)}, u32[128]{0:T(128)}, u32[]{:S(2)}) copy-start(u32[128]{0:T(128)} %constant.132) | copy-start | bytes 1540
  453.6 12.2 %all-to-all-start.3 = ((bf16[2,128,1024]{2,1,0:T(8,128)(2,1)}), bf16[2,128,1024]{2,1,0:T(8,128)(2,1)S(1)}, u32[]{:S(2)}, u32[]{:S(2)}) async-start(bf16[2,128,1024]{2,1,0:T(8,128)(2,1)} %copy.84), calls=%async_computation.4 | async-start | bytes 1048576 | tf_op jit(solution)/shard_map/all_to_all | solution.py:174
  951.2 2.0 copy-start.1
Sparse Core Ops, SparseCore 1:
  56.9 35.6 all-gather.3
  94.0 97.4 all-gather.7
  193.0 30.9 all-gather.5
  298.8 47.4 reduce-scatter.9
  348.8 47.4 reduce-scatter.7
  398.9 548.5 all-reduce.4

commit v2 on v1

v2 whole, which is shorter than its diff:
```python
import math

import jax
import jax.numpy as jnp
import numpy as np
from jax import lax
from jax.experimental import pallas as pl
from jax.experimental.pallas import tpu as pltpu
from jax.sharding import PartitionSpec as P

HD = 128
DE = 896
EHD = 64
R = 128
CH = 64
NB = 2
ROOM = 48


def lists(ids_m, span_index, vocab_rows, n_span):
    tokens = ids_m.shape[1]
    t = jnp.arange(tokens, dtype=jnp.int32)
    same = ids_m[:, :, None] == ids_m[:, None, :]
    dup = jnp.any(same & (t[None, None, :] < t[None, :, None]), axis=2)
    uniq = jnp.logical_not(dup)
    src = ids_m // vocab_rows
    shards = jnp.arange(n_span, dtype=jnp.int32)
    counts = jnp.sum(
        (uniq[:, None, :] & (src[:, None, :] == shards[None, :, None])).astype(jnp.int32), axis=2
    )
    over = jnp.max(counts) > ROOM
    sel = uniq & (src == span_index)
    tri = (t[:, None] < t[None, :]).astype(jnp.bfloat16)
    rank = jnp.dot(sel.astype(jnp.bfloat16), tri, preferred_element_type=jnp.float32).astype(
        jnp.int32
    )
    room = jnp.arange(ROOM, dtype=jnp.int32)
    local = ids_m - span_index * vocab_rows
    rows = jnp.sum(
        jnp.where(
            (rank[:, None, :] == room[None, :, None]) & sel[:, None, :], local[:, None, :], 0
        ),
        axis=2,
    )
    own = lax.dynamic_index_in_dim(ids_m, span_index, 0, keepdims=False)
    own_src = own // vocab_rows
    own_same = own[:, None] == own[None, :]
    first = jnp.min(jnp.where(own_same, t[None, :], tokens), axis=1)
    own_uniq = first == t
    own_rank = jnp.sum(
        (
            own_uniq[None, :]
            & (own_src[:, None] == own_src[None, :])
            & (t[None, :] < first[:, None])
        ).astype(jnp.int32),
        axis=1,
    )
    return rows, own_src * ROOM + own_rank, over


F32 = jnp.float32
BF16 = jnp.bfloat16
PAIR = 2 * EHD
HEADS_ENC = DE // EHD
PAIRS = HEADS_ENC // 2
TOK = 512
SPANS = 2
DEC = 2048
HALF = DE // 2
PADDED = 1024
PIECE = 14
TILES = ((0, 256), (256, 256), (512, 256), (768, 128))


def dot(a, b):
    return jnp.dot(a, b, preferred_element_type=F32)


def dot_nt(a, b):
    return lax.dot_general(a, b, (((1,), (1,)), ((), ())), preferred_element_type=F32)


def dot_tn(a, b):
    return lax.dot_general(a, b, (((0,), (0,)), ((), ())), preferred_element_type=F32)


def piece_rows():
    rows = np.full((2, PADDED), -1, np.int32)
    n = 0
    for core in range(2):
        for first in range(4):
            for second in range(4):
                for low in range(2):
                    for r in range(16):
                        if r < PIECE:
                            rows[0, n] = (((first * 4 + second) * 2 + low) * 2 + core) * PIECE + r
                            rows[1, n] = (((second * 4 + first) * 2 + low) * 2 + core) * PIECE + r
                        n += 1
    return rows


def pair_blocks(kv_ref, c, j, low, high):
    rows = pl.ds(pl.multiple_of(c * CH, CH), CH)
    k = kv_ref[rows, pl.ds(pl.multiple_of(j * PAIR, PAIR), PAIR)]
    v = kv_ref[rows, pl.ds(pl.multiple_of(DE + j * PAIR, PAIR), PAIR)]
    return (
        jnp.concatenate([k * low, k * high], axis=0),
        jnp.concatenate([v * low, v * high], axis=0),
    )


def middle(
    rows_ref,
    emb_ref,
    kv_ref,
    q_ref,
    og_ref,
    wq_ref,
    wo_ref,
    wd_own_ref,
    wd_oth_ref,
    att_own_ref,
    att_oth_ref,
    cross_ref,
    gq_ref,
    go_ref,
    eq_ref,
    att_ref,
    probs_ref,
    enc_ref,
    dkv_ref,
    gkv_ref,
    sum_ref,
    pad_ref,
):
    half = lax.axis_index("mp")
    lane = lax.broadcasted_iota(jnp.int32, (1, PAIR), 1)
    is_low = lane < EHD
    low = is_low.astype(F32).astype(BF16)
    high = (lane >= EHD).astype(F32).astype(BF16)

    for at, size in TILES:
        eq_ref[:, at : at + size] = dot(emb_ref[...], wq_ref[:, at : at + size]).astype(BF16)

    def forward(i, _):
        c, j = i // PAIRS, i % PAIRS
        rows = pl.ds(pl.multiple_of(c * NB * R, NB * R), NB * R)
        cols = pl.ds(pl.multiple_of(j * PAIR, PAIR), PAIR)
        kbd, vbd = pair_blocks(kv_ref, c, j, low, high)
        s = dot_nt(eq_ref[rows, cols], kbd) * (1.0 / math.sqrt(EHD))
        top0 = jnp.max(jnp.where(is_low, s, -jnp.inf), axis=1, keepdims=True)
        top1 = jnp.max(jnp.where(is_low, -jnp.inf, s), axis=1, keepdims=True)
        p = jnp.exp(s - jnp.where(is_low, top0, top1))
        sum0 = jnp.sum(jnp.where(is_low, p, 0.0), axis=1, keepdims=True)
        sum1 = jnp.sum(jnp.where(is_low, 0.0, p), axis=1, keepdims=True)
        p = p / jnp.where(is_low, sum0, sum1)
        probs_ref[i] = p
        att_ref[rows, cols] = dot(p.astype(BF16), vbd).astype(BF16)
        return 0

    lax.fori_loop(0, SPANS * PAIRS, forward, 0)

    for at, size in TILES:
        enc_ref[:, at : at + size] = (
            emb_ref[:, at : at + size].astype(F32) + dot(att_ref[...], wo_ref[:, at : at + size])
        ).astype(BF16)

    feature = lax.broadcasted_iota(jnp.int32, (DE, HALF), 0)
    column = lax.broadcasted_iota(jnp.int32, (DE, HALF), 1)
    for ref, which in ((att_own_ref, half), (att_oth_ref, 1 - half)):
        pick = (feature == column + which * HALF).astype(F32).astype(BF16)
        ref[...] = dot(att_ref[...], pick).astype(BF16)

    def project(i, _):
        cols = pl.ds(pl.multiple_of(i * 256, 256), 256)
        dkv_ref[0, :, cols] = dot(enc_ref[...], wd_own_ref[:, cols]).astype(BF16)
        dkv_ref[1, :, cols] = dot(enc_ref[...], wd_oth_ref[:, cols]).astype(BF16)
        return 0

    lax.fori_loop(0, DEC // 256, project, 0)
    scale = 1.0 / math.sqrt(HD)

    def decode(i, _):
        c, h = i // 8, i % 8
        few = pl.ds(pl.multiple_of(c * CH, CH), CH)
        rows = pl.ds(pl.multiple_of(c * NB * R, NB * R), NB * R)
        kcols = pl.ds(pl.multiple_of(h * HD, HD), HD)
        vcols = pl.ds(pl.multiple_of(DEC // 2 + h * HD, HD), HD)
        for g in range(2):
            cols = pl.ds(pl.multiple_of(g * (DEC // 2) + h * HD, HD), HD)
            q, og = q_ref[few, cols], og_ref[few, cols]
            k, v = dkv_ref[g, rows, kcols], dkv_ref[g, rows, vcols]
            s = dot_nt(q, k) * scale
            p = jnp.exp(s - jnp.max(s, axis=1, keepdims=True))
            p = p / jnp.sum(p, axis=1, keepdims=True)
            pb = p.astype(BF16)
            cross = dot(pb, v).astype(BF16)
            cross_ref[g, few, kcols] = cross
            gkv_ref[g, rows, vcols] = dot_tn(pb, og).astype(BF16)
            row = jnp.sum(og.astype(F32) * cross.astype(F32), axis=1, keepdims=True)
            ds = (p * (dot_nt(og, v) - row) * scale).astype(BF16)
            gkv_ref[g, rows, kcols] = dot_tn(ds, q).astype(BF16)
        return 0

    lax.fori_loop(0, SPANS * 8, decode, 0)
    sum_ref[...] = jnp.zeros_like(sum_ref)

    def collect(i, _):
        cols = pl.ds(pl.multiple_of(i * 256, 256), 256)
        sum_ref[...] += dot_nt(gkv_ref[0, :, cols], wd_own_ref[:, cols]) + dot_nt(
            gkv_ref[1, :, cols], wd_oth_ref[:, cols]
        )
        return 0

    lax.fori_loop(0, DEC // 256, collect, 0)
    enc_ref[...] = sum_ref[...].astype(BF16)

    def pad(ref, order):
        for at in range(0, PADDED, 256):
            spread = (
                lax.broadcasted_iota(jnp.int32, (DE, 256), 0)
                == rows_ref[order : order + 1, at : at + 256]
            )
            pad_ref[:, at : at + 256] = dot(ref[...], spread.astype(F32).astype(BF16)).astype(BF16)

    def outer(out_ref, ref):
        def tile(i, _):
            cols = pl.ds(pl.multiple_of(i * 256, 256), 256)
            out_ref[cols, :] = dot_tn(pad_ref[:, cols], ref[...]).astype(BF16)
            return 0

        lax.fori_loop(0, PADDED // 256, tile, 0)

    pad(enc_ref, 1)
    outer(go_ref, att_ref)
    for at, size in TILES:
        eq_ref[:, at : at + size] = dot_nt(enc_ref[...], wo_ref[at : at + size, :]).astype(BF16)

    def backward(i, _):
        c, j = i // PAIRS, i % PAIRS
        rows = pl.ds(pl.multiple_of(c * NB * R, NB * R), NB * R)
        cols = pl.ds(pl.multiple_of(j * PAIR, PAIR), PAIR)
        kbd, vbd = pair_blocks(kv_ref, c, j, low, high)
        ga = eq_ref[rows, cols]
        prod = ga.astype(F32) * att_ref[rows, cols].astype(F32)
        row0 = jnp.sum(jnp.where(is_low, prod, 0.0), axis=1, keepdims=True)
        row1 = jnp.sum(jnp.where(is_low, 0.0, prod), axis=1, keepdims=True)
        diff = dot_nt(ga, vbd) - jnp.where(is_low, row0, row1)
        ds = (probs_ref[i] * diff * (1.0 / math.sqrt(EHD))).astype(BF16)
        eq_ref[rows, cols] = dot(ds, kbd).astype(BF16)
        return 0

    lax.fori_loop(0, SPANS * PAIRS, backward, 0)
    pad(emb_ref, 0)
    outer(gq_ref, eq_ref)


def run_middle(embedded, kv, q, og, w_q, w_o, wd_own, wd_oth):
    vmem = pl.BlockSpec(memory_space=pltpu.VMEM)
    return pl.pallas_call(
        middle,
        out_shape=(
            jax.ShapeDtypeStruct((TOK, HALF), BF16),
            jax.ShapeDtypeStruct((TOK, HALF), BF16),
            jax.ShapeDtypeStruct((2, SPANS * CH, DEC // 2), BF16),
            jax.ShapeDtypeStruct((PADDED, DE), BF16),
            jax.ShapeDtypeStruct((PADDED, DE), BF16),
        ),
        in_specs=[vmem] * 9,
        out_specs=(vmem,) * 5,
        scratch_shapes=[
            pltpu.VMEM((TOK, DE), BF16),
            pltpu.VMEM((TOK, DE), BF16),
            pltpu.VMEM((SPANS * PAIRS, NB * R, PAIR), F32),
            pltpu.VMEM((TOK, DE), BF16),
            pltpu.VMEM((2, TOK, DEC), BF16),
            pltpu.VMEM((2, TOK, DEC), BF16),
            pltpu.VMEM((TOK, DE), F32),
            pltpu.VMEM((TOK, PADDED), BF16),
        ],
        compiler_params=pltpu.CompilerParams(vmem_limit_bytes=60 * 2**20),
        cost_estimate=pl.CostEstimate(
            flops=15 * 10**9, bytes_accessed=20 * 2**20, transcendentals=10**6
        ),
    )(jnp.asarray(piece_rows()), embedded, kv, q, og, w_q, w_o, wd_own, wd_oth)


def ending(
    slot_ref,
    own_ref,
    oth_ref,
    cross_ref,
    gq_ref,
    go_ref,
    att_out,
    cross_out,
    rq_ref,
    ro_ref,
    all_ref,
    slots_ref,
    core_ref,
    acc1_ref,
    first1_ref,
    first2_ref,
    acc2_ref,
    second1_ref,
    second2_ref,
    acc3_ref,
    last_ref,
    swap_sems,
    slot_sems,
    core_sems,
    ring_sems,
    last_sems,
    local_sem,
):
    span, dp, half = lax.axis_index("span"), lax.axis_index("dp"), lax.axis_index("mp")
    z, y, x_low, core = span // 4, span % 4, dp // 2, dp % 2
    partner = {"span": span, "dp": dp, "mp": 1 - half}
    peer = {"span": span, "dp": x_low * 2 + 1 - core, "mp": half}

    def in_span(k):
        return {"span": lax.rem(span + k, 16), "dp": dp, "mp": half}

    def along(axis, by):
        if axis == 0:
            return {"span": lax.rem(z + by + 4, 4) * 4 + y, "dp": dp, "mp": half}
        return {"span": z * 4 + lax.rem(y + by + 4, 4), "dp": dp, "mp": half}

    others = [
        {"span": span, "dp": (1 - x_low) * 2 + core, "mp": half},
        partner,
        {"span": span, "dp": (1 - x_low) * 2 + core, "mp": 1 - half},
    ]
    barrier = pltpu.get_barrier_semaphore()
    friends = [in_span(k) for k in range(1, 16)] + [peer] + others
    for friend in friends:
        pl.semaphore_signal(barrier, inc=1, device_id=friend, device_id_type=pl.DeviceIdType.MESH)
    pl.semaphore_wait(barrier, len(friends))

    def send(src, dst, sems, device):
        copy = pltpu.make_async_remote_copy(
            src_ref=src,
            dst_ref=dst,
            send_sem=sems.at[0],
            recv_sem=sems.at[1],
            device_id=device,
            device_id_type=pl.DeviceIdType.MESH,
        )
        copy.start()
        return copy

    waiting = []
    swap = send(oth_ref, all_ref.at[half], swap_sems.at[0], partner)
    cores = [
        send(ref.at[1 - core], core_ref.at[k], core_sems.at[k], peer)
        for k, ref in enumerate((gq_ref, go_ref))
    ]
    waiting.append(send(cross_ref.at[1], cross_out.at[half], swap_sems.at[1], partner))
    mine = pltpu.make_async_copy(cross_ref.at[0], cross_out.at[half], local_sem.at[0])
    mine.start()
    all_ref[half] = own_ref[...]

    def add(*parts):
        total = parts[0].astype(F32)
        for part in parts[1:]:
            total = total + part.astype(F32)
        return total

    for k, ref in enumerate((gq_ref, go_ref)):
        cores[k].wait()
        for i in range(4):
            acc1_ref[k, i] = add(ref[core, i], core_ref[k, i]).astype(BF16)

    where = (z, y)

    def ring(level, acc, got1, width):
        cut = width // 2
        copies = []
        for k in range(2):
            axis = k if level == 0 else 1 - k
            p = where[axis]
            far = lax.rem(p + 2, 4)
            copies.append(
                (
                    send(acc.at[k, far, pl.ds(0, cut)], got1.at[k, 0], ring_sems.at[level, k, 0], along(axis, 1)),
                    send(acc.at[k, far, pl.ds(cut, cut)], got1.at[k, 1], ring_sems.at[level, k, 1], along(axis, -1)),
                )
            )
        return copies

    def ring_next(level, copies, acc, got1, got2, width):
        cut = width // 2
        nexts = []
        for k in range(2):
            axis = k if level == 0 else 1 - k
            p = where[axis]
            up, down = lax.rem(p + 1, 4), lax.rem(p + 3, 4)
            for copy in copies[k]:
                copy.wait()
            acc[k, up, pl.ds(0, cut)] = add(acc[k, up, pl.ds(0, cut)], got1[k, 0]).astype(BF16)
            acc[k, down, pl.ds(cut, cut)] = add(acc[k, down, pl.ds(cut, cut)], got1[k, 1]).astype(BF16)
            nexts.append(
                (
                    send(acc.at[k, up], got2.at[k, 0], ring_sems.at[level, k, 2], along(axis, 1)),
                    send(acc.at[k, down], got2.at[k, 1], ring_sems.at[level, k, 3], along(axis, -1)),
                )
            )
        return nexts

    copies = ring(0, acc1_ref, first1_ref, 4)

    swap.wait()
    for e in range(16):
        unit, there = slot_ref[0, e], slot_ref[1, e]
        slots_ref[e] = all_ref[unit // 4, unit % 4] * there.astype(F32).astype(BF16)
    for k in range(1, 16):
        to = lax.rem(span + k, 16)
        waiting.append(send(slots_ref.at[to], att_out.at[span], slot_sems.at[k], in_span(k)))
    stay = pltpu.make_async_copy(slots_ref.at[span], att_out.at[span], local_sem.at[1])
    stay.start()

    nexts = ring_next(0, copies, acc1_ref, first1_ref, first2_ref, 4)
    for k in range(2):
        for copy in nexts[k]:
            copy.wait()
        acc2_ref[k] = add(acc1_ref[k, where[k]], first2_ref[k, 0], first2_ref[k, 1]).astype(BF16)
    copies = ring(1, acc2_ref, second1_ref, 2)
    nexts = ring_next(1, copies, acc2_ref, second1_ref, second2_ref, 2)
    for k in range(2):
        for copy in nexts[k]:
            copy.wait()
        acc3_ref[k] = add(acc2_ref[k, where[1 - k]], second2_ref[k, 0], second2_ref[k, 1]).astype(BF16)

    lasts = []
    for n, other in enumerate(others):
        low = x_low if n == 1 else 1 - x_low
        lasts.append(send(acc3_ref.at[:, low], last_ref.at[n], last_sems.at[n], other))
    for copy in lasts:
        copy.wait()
    for k, ref in enumerate((rq_ref, ro_ref)):
        ref[...] = add(acc3_ref[k, x_low], last_ref[0, k], last_ref[1, k], last_ref[2, k])
    for copy in waiting:
        copy.wait()
    mine.wait()
    stay.wait()


def run_ending(slot, own, oth, cross, gq, go):
    vmem = pl.BlockSpec(memory_space=pltpu.VMEM)
    anywhere = pl.BlockSpec(memory_space=pl.ANY)
    dma = pltpu.SemaphoreType.DMA
    return pl.pallas_call(
        ending,
        out_shape=(
            jax.ShapeDtypeStruct((16, R, HALF), BF16),
            jax.ShapeDtypeStruct((2, SPANS * CH, DEC // 2), BF16),
            jax.ShapeDtypeStruct((16, DE), F32),
            jax.ShapeDtypeStruct((16, DE), F32),
        ),
        in_specs=[pl.BlockSpec(memory_space=pltpu.SMEM)] + [vmem] * 5,
        out_specs=(anywhere, anywhere, vmem, vmem),
        scratch_shapes=[
            pltpu.VMEM((2, 4, R, HALF), BF16),
            pltpu.VMEM((16, R, HALF), BF16),
            pltpu.VMEM((2, 4, 4, 2, 16, DE), BF16),
            pltpu.VMEM((2, 4, 4, 2, 16, DE), BF16),
            pltpu.VMEM((2, 2, 2, 2, 16, DE), BF16),
            pltpu.VMEM((2, 2, 4, 2, 16, DE), BF16),
            pltpu.VMEM((2, 4, 2, 16, DE), BF16),
            pltpu.VMEM((2, 2, 1, 16, DE), BF16),
            pltpu.VMEM((2, 2, 2, 16, DE), BF16),
            pltpu.VMEM((2, 2, 16, DE), BF16),
            pltpu.VMEM((3, 2, 16, DE), BF16),
            dma((2, 2)),
            dma((16, 2)),
            dma((2, 2)),
            dma((2, 2, 4, 2)),
            dma((3, 2)),
            dma((2,)),
        ],
        compiler_params=pltpu.CompilerParams(
            vmem_limit_bytes=48 * 2**20, collective_id=1, has_side_effects=True
        ),
        cost_estimate=pl.CostEstimate(
            flops=10**7, bytes_accessed=10 * 2**20, transcendentals=0
        ),
    )(slot, own.reshape(4, R, HALF), oth.reshape(4, R, HALF), cross, gq.reshape(2, 4, 4, 2, 16, DE), go.reshape(2, 4, 4, 2, 16, DE))


def body(
    span_states,
    queries,
    out_grad,
    neighbour_ids,
    assignment,
    embed_table,
    w_span_kv,
    w_query_enc,
    w_out_enc,
    w_dec_kv,
):
    f32 = jnp.float32
    bf16 = jnp.bfloat16
    n_span = lax.axis_size("span")
    span_index = lax.axis_index("span")
    half_index = lax.axis_index("mp")
    seq_count, local_tokens, half_width = span_states.shape
    spans = local_tokens // CH
    units = spans * NB
    dec_cols = 2 * queries.shape[2]
    vocab_rows = embed_table.shape[0]
    tokens = units * R

    ids_m = lax.dynamic_index_in_dim(
        neighbour_ids.reshape(seq_count, n_span, tokens), half_index, 0, keepdims=False
    )
    rows, pos, over = lists(ids_m, span_index, vocab_rows, n_span)
    over = lax.pmax(over.astype(jnp.int32), ("dp", "mp"))
    sent = jnp.take(embed_table, rows.reshape(-1), axis=0).reshape(n_span, ROOM, DE)
    got = lax.all_to_all(sent, "span", split_axis=0, concat_axis=0, tiled=True)
    pick = (pos[:, None] == jnp.arange(n_span * ROOM, dtype=jnp.int32)[None, :]).astype(bf16)
    embedded = jnp.dot(pick, got.reshape(-1, DE), preferred_element_type=f32).astype(bf16)

    def whole_gather(_):
        shifted = ids_m.reshape(-1) - span_index * vocab_rows
        inside = (shifted >= 0) & (shifted < vocab_rows)
        found = jnp.take(embed_table, jnp.clip(shifted, 0, vocab_rows - 1), axis=0)
        return lax.psum_scatter(
            jnp.where(inside[:, None], found, jnp.zeros_like(found)),
            "span",
            scatter_dimension=0,
            tiled=True,
        )

    embedded = lax.cond(over > 0, whole_gather, lambda e: e, embedded)

    kv_part = jnp.dot(
        span_states.reshape(-1, half_width), w_span_kv, preferred_element_type=f32
    ).astype(bf16)
    kv_part = kv_part.reshape(seq_count, local_tokens, 2 * DE)
    kv_both = lax.all_to_all(kv_part, "mp", split_axis=0, concat_axis=0, tiled=True)
    kv = jnp.sum(kv_both.astype(f32), axis=0).astype(bf16)

    def swap_heads(x):
        both = lax.all_to_all(x, "mp", split_axis=0, concat_axis=0, tiled=True)
        own = lax.dynamic_index_in_dim(both, half_index, 0, keepdims=False)
        oth = lax.dynamic_index_in_dim(both, 1 - half_index, 0, keepdims=False)
        return jnp.concatenate([own, oth], axis=1)

    q = swap_heads(queries)
    og = swap_heads(out_grad)

    def other_half(w, rows):
        part = lax.dynamic_slice_in_dim(w, span_index * rows, rows, 0)
        part = lax.ppermute(part, "mp", [(0, 1), (1, 0)])
        return lax.all_gather(part, "span", axis=0, tiled=True)

    wd_own = w_dec_kv.reshape(DE, dec_cols)
    wq_oth = other_half(w_query_enc, DE // n_span)
    wo_oth = other_half(w_out_enc, 32)[:HALF]
    wd_oth = other_half(wd_own, DE // n_span)
    first = half_index == 0
    w_q = jnp.where(
        first,
        jnp.concatenate([w_query_enc, wq_oth], axis=1),
        jnp.concatenate([wq_oth, w_query_enc], axis=1),
    )
    w_o = jnp.where(
        first,
        jnp.concatenate([w_out_enc, wo_oth], axis=0),
        jnp.concatenate([wo_oth, w_out_enc], axis=0),
    )
    own, oth, cross, gq, go = run_middle(embedded, kv, q, og, w_q, w_o, wd_own, wd_oth)

    dest = lax.dynamic_index_in_dim(assignment[0, :, :, 0], span_index, 0, keepdims=False)
    at = dest[None, :] == jnp.arange(n_span, dtype=jnp.int32)[:, None]
    numbers = jnp.arange(seq_count * units, dtype=jnp.int32)
    slot = jnp.stack(
        [jnp.sum(jnp.where(at, numbers[None, :], 0), axis=1), jnp.sum(at.astype(jnp.int32), axis=1)]
    )
    attended_out, cross_out, rq, ro = run_ending(slot, own, oth, cross, gq, go)
    grad_query_enc = lax.dynamic_slice_in_dim(rq[:PIECE], half_index * HALF, HALF, 1)
    grad_out_enc = lax.dynamic_slice_in_dim(ro[:PIECE], half_index * HALF, HALF, 1).T
    return (
        cross_out,
        attended_out.reshape(1, 1, n_span, 1, R, HALF),
        grad_query_enc,
        grad_out_enc,
    )


def solution(mesh):
    return jax.shard_map(
        body,
        mesh=mesh,
        in_specs=(
            P("dp", "span", "mp"),
            P("dp", "span", "mp"),
            P("dp", "span", "mp"),
            P("dp", None, None, None),
            P("dp", None, None, None),
            P("span", None),
            P("mp", None),
            P(None, "mp"),
            P("mp", None),
            P(None, None, "mp"),
        ),
        out_specs=(
            P("dp", "span", "mp"),
            P("dp", "span", None, None, None, "mp"),
            P(("span", "dp"), "mp"),
            P("mp", ("span", "dp")),
        ),
        check_vma=False,
    )
```

time: 971 us -> 282 us (0.29)
  waiting for transfers between devices: 730 us -> 8.7 us
  Pallas kernels: 0 us -> 115 us
  matrix products: 77.7 us -> 8.26 us
  blocking collectives: 21.6 us -> 58.6 us
  local copies, waits for them, and re-layouts: 63.3 us -> 30.2 us
    unnamed x7 -> x1, waiting for transfers between devices: 483 us -> 0.02 us
    pallas_call x0 -> x2, Pallas kernels: none -> 115 us  [the longest x1 57.9 us: run_middle(): pl.pallas_call(middle, out_shape=(jax.ShapeDtypeStruct((TOK, HALF), BF16)...]
    all_gather x3 -> x1, waiting for transfers between devices: 94.4 us -> 0.01 us  [other_half(): return lax.all_gather(part, 'span', axis=0, tiled=True)]
    reduce_scatter x2 -> x0, waiting for transfers between devices: 80.6 us -> none  [the longest x1 50 us: body(): lax.psum_scatter(grad_query_part, 'mp', scatter_dimension=1, tiled=True)]
    dot_general x14 -> x0, matrix products: 69.5 us -> none  [the longest x1 19.5 us: body(): jnp.dot(encoded, w_d, preferred_element_type=f32).astype(bf16)]
    all_gather x0 -> x2, blocking collectives: none -> 49.2 us  [other_half(): return lax.all_gather(part, 'span', axis=0, tiled=True)]
    all_to_all x3 -> x0, waiting for transfers between devices: 47.2 us -> none  [the longest x1 25.2 us: body(): lax.all_to_all(slots, 'span', split_axis=0, concat_axis=0, tiled=True)]
    all_to_all x3 -> x0, starting transfers between devices: 15 us -> none  [the longest x1 7.72 us: body(): lax.all_to_all(slots, 'span', split_axis=0, concat_axis=0, tiled=True)]
  transfers between devices with their start and end apart: 12 -> 8, of which waited for: 11 -> 2; matrix products, arithmetic and copies ran while one was open for 6% -> 9% of each run, Pallas kernels for 0% -> 0%
where the time goes in v2:
time: 282 us; the launch traced here: 281 us
  Pallas kernels  115 us (41%)
  blocking collectives  58.6 us (21%)
  local copies, waits for them, and re-layouts  30.2 us (11%)
  starting transfers between devices  28.8 us (10%)
  between operations  17 us (6%)
  other arithmetic  15 us (5%)
  waiting for transfers between devices  8.7 us (3%)
  matrix products  8.26 us (3%)
    pallas_call x1, Pallas kernels, run_middle(): pl.pallas_call(middle, out_shape=(jax.ShapeDtypeStruct((TOK, HALF), BF16)...  57.9 us
    pallas_call x1, Pallas kernels, run_ending(): pl.pallas_call(ending, out_shape=(jax.ShapeDtypeStruct((16, R, HALF), BF1...  56.9 us
    all_gather x2, blocking collectives, other_half(): return lax.all_gather(part, 'span', axis=0, tiled=True)  49.2 us
    unnamed x26, local copies, waits for them, and re-layouts  17.3 us
    pmax x1, blocking collectives, body(): over = lax.pmax(over.astype(jnp.int32), ('dp', 'mp'))  9.44 us
    all_to_all x2, starting transfers between devices, swap_heads(): both = lax.all_to_all(x, 'mp', split_axis=0, concat_axis=0, tiled=True)  9.21 us
    all_to_all x1, waiting for transfers between devices, body(): lax.all_to_all(kv_part, 'mp', split_axis=0, concat_axis=0, tiled=True)  8.37 us
    all_to_all x1, starting transfers between devices, body(): got = lax.all_to_all(sent, 'span', split_axis=0, concat_axis=0, tiled=True)  8.13 us
  transfers between devices with their start and end apart: 8, of which 2 were waited for; matrix products, arithmetic and copies ran while one was open for 9% of the time, Pallas kernels for 0%

profile of v2, /device:TPU:0, one launch (start us, length us, event | category | flops | bytes accessed | tf_op | source)
XLA Modules:
  0.0 281.4 jit_solution(2932886141841772597)
XLA Ops:
  8.0 0.1 iota_compare_fusion.7
  8.1 1.0 reshape.249
  9.1 4.2 %and_reduce_fusion = pred[16,512]{1,0:T(8,128)(4,1)S(1)} fusion(s32[16,512]{1,0:T(8,128)S(1)} %get-tuple-element.52, pred[512,512]{1,0:T(8,128)(4,1)S(1)} %iota_compare_fusion.7), kind=kLoop, calls=%fused_computation.10 | loop fusion | flops 12574720 | bytes 303104 | tf_op jit(solution)/shard_map/reduce_or | solution.py:24
  13.4 0.2 convolution_convert_fusion.1
  13.5 0.5 select_reduce_fusion
  14.1 7.5 %gather_fusion.1 = bf16[768,896]{1,0:T(8,128)(2,1)S(1)} fusion(bf16[4000,896]{1,0:T(8,128)(2,1)} %param.18, s32[1024]{0:T(1024)S(1)} %pad_clamp_fusion), kind=kCustom, calls=%fused_computation.1 | custom fusion | bytes 2755584 | tf_op jit(solution)/shard_map/jit(_take)/gather | solution.py:520
  21.6 1.3 broadcast_select_fusion
  22.9 8.1 %all-to-all-start = ((bf16[16,48,896]{2,1,0:T(8,128)(2,1)}), bf16[16,48,896]{2,1,0:T(8,128)(2,1)S(1)}, u32[]{:S(2)}, u32[]{:S(2)}) async-start(bf16[16,48,896]{2,1,0:T(8,128)(2,1)} %broadcast_select_fusion), calls=%async_computation.1 | async-start | bytes 2752512 | tf_op jit(solution)/shard_map/all_to_all | solution.py:521
  31.1 0.4 convert_reduce_fusion.1
  31.4 0.6 reduce_max.9
  32.7 5.1 %copy.30 = bf16[112,8,2,1024]{3,1,2,0:T(8,128)(2,1)} copy(bf16[112,8,2,1024]{3,2,1,0:T(2,128)(2,1)} %bitcast.55) | data formatting | bytes 7340032
  37.8 1.6 constant_dynamic-slice_fusion.1
  39.4 3.0 %collective-permute-start.2 = (bf16[56,2048]{1,0:T(8,128)(2,1)}, bf16[56,2048]{1,0:T(8,128)(2,1)S(1)}, u32[]{:S(2)}, u32[]{:S(2)}) collective-permute-start(bf16[56,2048]{1,0:T(8,128)(2,1)} %constant_dynamic-slice_fusion.1), channel_id=1, source_target_pairs={{0,1},{1,0},{2,3},{3,2},{4,5},{5,4},{6,7},{7,6},{8,9},{9,8},{10,11... | collective-permute-start | bytes 688136 | tf_op jit(solution)/shard_map/ppermute | solution.py:556
  42.5 9.4 %pmax.7 = s32[]{:T(128)} all-reduce(s32[]{:T(128)S(6)} %convert_element_type.34), channel_id=1, replica_groups=mesh['span'=16,'dp'=4,'mp'=2] {'dp','mp'}, use_global_device_ids=true, to_apply=%region_5.6 | all-reduce | flops 1 | bytes 8 | tf_op jit(solution)/shard_map/pmax | solution.py:519
  52.6 0.3 select_reduce_fusion.1
  52.9 0.5 convert_reduce_fusion
  53.4 1.9 fusion.2
  55.4 0.7 copy-done.8
  56.1 4.0 %all-to-all-start.2 = ((bf16[2,128,1024]{2,1,0:T(8,128)(2,1)}), bf16[2,128,1024]{2,1,0:T(8,128)(2,1)S(1)}, u32[]{:S(2)}, u32[]{:S(2)}) async-start(bf16[2,128,1024]{2,1,0:T(8,128)(2,1)} %param.14), calls=%async_computation.3 | async-start | bytes 1048576 | tf_op jit(solution)/shard_map/all_to_all | solution.py:546
  60.1 0.7 copy.24
  60.9 3.6 %collective-permute-start = (bf16[56,448]{1,0:T(8,128)(2,1)S(1)}, bf16[56,448]{1,0:T(8,128)(2,1)S(1)}, u32[]{:S(2)}, u32[]{:S(2)}) collective-permute-start(bf16[56,448]{1,0:T(8,128)(2,1)S(1)} %constant_dynamic-slice_fusion.3), channel_id=1, source_target_pairs={{0,1},{1,0},{2,3},{3,2},{4,5},{5,4},{6,7},{7,6},{8,9},{9,8},{10,11... | collective-permute-start | bytes 150536 | tf_op jit(solution)/shard_map/ppermute | solution.py:556
  64.5 0.8 constant_dynamic-slice_fusion.2
  65.3 0.3 dynamic-slice_reduce_fusion
  65.7 0.1 select_reduce_fusion.2
  65.8 6.1 %convolution_convert_fusion = bf16[256,1792]{1,0:T(8,128)(2,1)} fusion(bf16[256,2048]{1,0:T(8,128)(2,1)S(1)} %bitcast.45, bf16[2048,1792]{1,0:T(8,128)(2,1)} %param.19), kind=kOutput, calls=%fused_computation.11 | convolution fusion | flops 1879506944 | bytes 9306112 | tf_op jit(solution)/shard_map/dot_general | solution.py:538
  71.9 0.3 collective-permute-done
  72.2 25.6 %all_gather.9 = bf16[896,448]{1,0:T(8,128)(2,1)S(1)} all-gather(bf16[56,448]{1,0:T(8,128)(2,1)S(1)} %collective-permute-done), channel_id=1, replica_groups=mesh['span'=16,'dp'=4,'mp'=2] {'span'}, dimensions={0}, use_global_device_ids=true | all-gather | bytes 852992 | tf_op jit(solution)/shard_map/all_gather | solution.py:557
  97.8 2.4 maximum_select_fusion.wq_ref
  100.2 5.2 %all-to-all-start.3 = ((bf16[2,128,1024]{2,1,0:T(8,128)(2,1)}), bf16[2,128,1024]{2,1,0:T(8,128)(2,1)S(1)}, u32[]{:S(2)}, u32[]{:S(2)}) async-start(bf16[2,128,1024]{2,1,0:T(8,128)(2,1)} %param.15), calls=%async_computation.4 | async-start | bytes 1048576 | tf_op jit(solution)/shard_map/all_to_all | solution.py:546
  105.4 23.5 %all_gather.10 = bf16[512,896]{1,0:T(8,128)(2,1)S(1)} all-gather(bf16[32,896]{1,0:T(8,128)(2,1)S(1)} %collective-permute-done.1), channel_id=1, replica_groups=mesh['span'=16,'dp'=4,'mp'=2] {'span'}, dimensions={0}, use_global_device_ids=true | all-gather | bytes 974848 | tf_op jit(solution)/shard_map/all_gather | solution.py:557
  129.0 1.9 maximum_select_fusion.1.wo_ref
  130.9 4.8 %all-to-all-start.1 = ((bf16[2,128,1792]{2,1,0:T(8,128)(2,1)}), bf16[2,128,1792]{2,1,0:T(8,128)(2,1)S(1)}, u32[]{:S(2)}, u32[]{:S(2)}) async-start(bf16[2,128,1792]{2,1,0:T(8,128)(2,1)} %bitcast.58), calls=%async_computation.2 | async-start | bytes 1835008 | tf_op jit(solution)/shard_map/all_to_all | solution.py:542
  135.7 0.1 dynamic-slice_bitcast_fusion.1
  135.8 0.8 pad_maximum_fusion.q_ref
  136.6 0.9 pad_maximum_fusion.1.og_ref
  137.5 8.4 %all-to-all-done.1 = bf16[2,128,1792]{2,1,0:T(8,128)(2,1)S(1)} async-done(((bf16[2,128,1792]{2,1,0:T(8,128)(2,1)}), bf16[2,128,1792]{2,1,0:T(8,128)(2,1)S(1)}, u32[]{:S(2)}, u32[]{:S(2)}) %all-to-all-start.1) | async-done | bytes 917536 | tf_op jit(solution)/shard_map/all_to_all | solution.py:542
  145.9 1.0 reduce_sum.62.kv_ref
  146.9 57.9 %shard_map.138 = (bf16[512,448]{1,0:T(8,128)(2,1)}, bf16[512,448]{1,0:T(8,128)(2,1)}, bf16[2,128,1024]{2,1,0:T(8,128)(2,1)}, bf16[1024,896]{1,0:T(8,128)(2,1)}, bf16[1024,896]{1,0:T(8,128)(2,1)}) custom-call(s32[2,1024]{1,0:T(2,128)} %constant.133.clone.rows_ref, bf16[512,896]{1,0:T(8,128)(2,1)S(1)} %copy-done.10, bf16[128,1792]{1,0:T(8,128)(2,1)} %reduce_sum.62.kv_ref, ...), custom_call_target="tpu_custom_call" | custom-call | flops 15000000512 | bytes 20971520 | tf_op jit(solution)/shard_map/pallas_call | solution.py:260
  204.9 1.5 copy-done.1
  206.4 1.5 copy-done.2
  207.9 1.0 copy-done.3
  208.9 1.0 copy-done.4
  210.0 1.0 copy-done.5
  211.0 56.9 %shard_map.139 = (bf16[16,128,448]{2,1,0:T(8,128)(2,1)}, bf16[2,128,1024]{2,1,0:T(8,128)(2,1)S(1)}, f32[16,896]{1,0:T(8,128)S(1)}, f32[16,896]{1,0:T(8,128)S(1)}) custom-call(s32[2,16]{1,0:T(2,128)S(1)} %pad_add_fusion.slot_ref, bf16[4,128,448]{2,1,0:T(8,128)(2,1)S(1)} %bitcast.48, bf16[4,128,448]{2,1,0:T(8,128)(2,1)S(1)} %bitcast.49, ...), custom_call_target="tpu_custom_call" | custom-call | flops 10000000 | bytes 10485760 | tf_op jit(solution)/shard_map/pallas_call | solution.py:453
  267.9 3.9 %copy.26 = bf16[1,1,16,1,128,448]{4,5,3,2,1,0:T(8,128)(2,1)} copy(bf16[1,1,16,1,128,448]{5,4,2,3,1,0:T(8,128)(2,1)} %bitcast.56) | data formatting | bytes 3670016
  271.8 0.7 constant_dynamic-slice_fusion
  272.5 0.7 dynamic-slice_bitcast_fusion.4
  273.1 0.8 copy.34
  (39 shorter events, 0.4 us)
Async XLA Ops:
  8.0 57.8 %copy-start = (bf16[2,128,2048]{2,1,0:T(8,128)(2,1)S(1)}, bf16[2,128,2048]{2,1,0:T(8,128)(2,1)}, u32[]{:S(2)}) copy-start(bf16[2,128,2048]{2,1,0:T(8,128)(2,1)} %param.13) | copy-start | bytes 3145732
  22.9 30.5 %all-to-all-start = ((bf16[16,48,896]{2,1,0:T(8,128)(2,1)}), bf16[16,48,896]{2,1,0:T(8,128)(2,1)S(1)}, u32[]{:S(2)}, u32[]{:S(2)}) async-start(bf16[16,48,896]{2,1,0:T(8,128)(2,1)} %broadcast_select_fusion), calls=%async_computation.1 | async-start | bytes 2752512 | tf_op jit(solution)/shard_map/all_to_all | solution.py:521
  39.4 15.9 %collective-permute-start.2 = (bf16[56,2048]{1,0:T(8,128)(2,1)}, bf16[56,2048]{1,0:T(8,128)(2,1)S(1)}, u32[]{:S(2)}, u32[]{:S(2)}) collective-permute-start(bf16[56,2048]{1,0:T(8,128)(2,1)} %constant_dynamic-slice_fusion.1), channel_id=1, source_target_pairs={{0,1},{1,0},{2,3},{3,2},{4,5},{5,4},{6,7},{7,6},{8,9},{9,8},{10,11... | collective-permute-start | bytes 688136 | tf_op jit(solution)/shard_map/ppermute | solution.py:556
  55.4 4.8 %copy-start.7 = (bf16[896,448]{0,1:T(8,128)(2,1)S(1)}, bf16[896,448]{0,1:T(8,128)(2,1)}, u32[]{:S(2)}) copy-start(bf16[896,448]{0,1:T(8,128)(2,1)} %param.20) | copy-start | bytes 2408452
  55.4 10.0 %copy-start.9 = (s32[1,16,8,1]{1,3,2,0:T(1,128)S(1)}, s32[1,16,8,1]{1,3,2,0:T(1,128)}, u32[]{:S(2)}) copy-start(s32[1,16,8,1]{1,3,2,0:T(1,128)} %param.17) | copy-start | bytes 1540
  55.4 91.5 %all-gather.2.cloned.1.call-start = ((), (), s32[]{:S(2)}) async-start(), calls=%async_computation.6 | async-start | bytes 3899392 | tf_op jit(solution)/shard_map/all_gather | solution.py:557
  55.4 0.7 copy-start.8
  56.1 44.1 %all-to-all-start.2 = ((bf16[2,128,1024]{2,1,0:T(8,128)(2,1)}), bf16[2,128,1024]{2,1,0:T(8,128)(2,1)S(1)}, u32[]{:S(2)}, u32[]{:S(2)}) async-start(bf16[2,128,1024]{2,1,0:T(8,128)(2,1)} %param.14), calls=%async_computation.3 | async-start | bytes 1048576 | tf_op jit(solution)/shard_map/all_to_all | solution.py:546
  60.9 11.3 %collective-permute-start = (bf16[56,448]{1,0:T(8,128)(2,1)S(1)}, bf16[56,448]{1,0:T(8,128)(2,1)S(1)}, u32[]{:S(2)}, u32[]{:S(2)}) collective-permute-start(bf16[56,448]{1,0:T(8,128)(2,1)S(1)} %constant_dynamic-slice_fusion.3), channel_id=1, source_target_pairs={{0,1},{1,0},{2,3},{3,2},{4,5},{5,4},{6,7},{7,6},{8,9},{9,8},{10,11... | collective-permute-start | bytes 150536 | tf_op jit(solution)/shard_map/ppermute | solution.py:556
  65.3 40.1 %collective-permute-start.1 = (bf16[32,896]{1,0:T(8,128)(2,1)S(1)}, bf16[32,896]{1,0:T(8,128)(2,1)S(1)}, u32[]{:S(2)}, u32[]{:S(2)}) collective-permute-start(bf16[32,896]{1,0:T(8,128)(2,1)S(1)} %constant_dynamic-slice_fusion.2), channel_id=1, source_target_pairs={{0,1},{1,0},{2,3},{3,2},{4,5},{5,4},{6,7},{7,6},{8,9},{9,8},{10,11... | collective-permute-start | bytes 172040 | tf_op jit(solution)/shard_map/ppermute | solution.py:556
  100.2 28.8 %copy-start.6 = (bf16[448,896]{1,0:T(8,128)(2,1)S(1)}, bf16[448,896]{1,0:T(8,128)(2,1)}, u32[]{:S(2)}) copy-start(bf16[448,896]{1,0:T(8,128)(2,1)} %param.21) | copy-start | bytes 2408452
  100.2 30.7 %all-to-all-start.3 = ((bf16[2,128,1024]{2,1,0:T(8,128)(2,1)}), bf16[2,128,1024]{2,1,0:T(8,128)(2,1)S(1)}, u32[]{:S(2)}, u32[]{:S(2)}) async-start(bf16[2,128,1024]{2,1,0:T(8,128)(2,1)} %param.15), calls=%async_computation.4 | async-start | bytes 1048576 | tf_op jit(solution)/shard_map/all_to_all | solution.py:546
  130.9 15.0 %all-to-all-start.1 = ((bf16[2,128,1792]{2,1,0:T(8,128)(2,1)}), bf16[2,128,1792]{2,1,0:T(8,128)(2,1)S(1)}, u32[]{:S(2)}, u32[]{:S(2)}) async-start(bf16[2,128,1792]{2,1,0:T(8,128)(2,1)} %bitcast.58), calls=%async_computation.2 | async-start | bytes 1835008 | tf_op jit(solution)/shard_map/all_to_all | solution.py:542
  135.8 11.1 %copy-start.10 = (bf16[512,896]{1,0:T(8,128)(2,1)S(1)}, bf16[512,896]{1,0:T(8,128)(2,1)}, u32[]{:S(2)}) copy-start(bf16[512,896]{1,0:T(8,128)(2,1)} %get-tuple-element.70.emb_ref) | copy-start | bytes 2752516
  204.9 1.5 copy-start.1
  206.4 1.5 copy-start.2
  207.9 1.0 copy-start.3
  208.9 1.0 copy-start.4
  209.9 1.0 copy-start.5
Sparse Core Ops, SparseCore 1:
  58.0 52.0 all-gather.1

commit v3 on v1

v3 whole, which is shorter than its diff:
```python
import math

import jax
import jax.numpy as jnp
import numpy as np
from jax import lax
from jax.experimental import pallas as pl
from jax.experimental.pallas import tpu as pltpu
from jax.sharding import PartitionSpec as P

HD = 128
DE = 896
EHD = 64
R = 128
CH = 64
NB = 2
ROOM = 48


def lists(ids_m, span_index, vocab_rows, n_span):
    tokens = ids_m.shape[1]
    t = jnp.arange(tokens, dtype=jnp.int32)
    same = ids_m[:, :, None] == ids_m[:, None, :]
    dup = jnp.any(same & (t[None, None, :] < t[None, :, None]), axis=2)
    uniq = jnp.logical_not(dup)
    src = ids_m // vocab_rows
    shards = jnp.arange(n_span, dtype=jnp.int32)
    counts = jnp.sum(
        (uniq[:, None, :] & (src[:, None, :] == shards[None, :, None])).astype(jnp.int32), axis=2
    )
    over = jnp.max(counts) > ROOM
    sel = uniq & (src == span_index)
    tri = (t[:, None] < t[None, :]).astype(jnp.bfloat16)
    rank = jnp.dot(sel.astype(jnp.bfloat16), tri, preferred_element_type=jnp.float32).astype(
        jnp.int32
    )
    room = jnp.arange(ROOM, dtype=jnp.int32)
    local = ids_m - span_index * vocab_rows
    rows = jnp.sum(
        jnp.where(
            (rank[:, None, :] == room[None, :, None]) & sel[:, None, :], local[:, None, :], 0
        ),
        axis=2,
    )
    own = lax.dynamic_index_in_dim(ids_m, span_index, 0, keepdims=False)
    own_src = own // vocab_rows
    own_same = own[:, None] == own[None, :]
    first = jnp.min(jnp.where(own_same, t[None, :], tokens), axis=1)
    own_uniq = first == t
    own_rank = jnp.sum(
        (
            own_uniq[None, :]
            & (own_src[:, None] == own_src[None, :])
            & (t[None, :] < first[:, None])
        ).astype(jnp.int32),
        axis=1,
    )
    return rows, own_src * ROOM + own_rank, over


F32 = jnp.float32
BF16 = jnp.bfloat16
PAIR = 2 * EHD
HEADS_ENC = DE // EHD
PAIRS = HEADS_ENC // 2
TOK = 512
SPANS = 2
DEC = 2048
HALF = DE // 2
PADDED = 1024
PIECE = 14
TILES = ((0, 256), (256, 256), (512, 256), (768, 128))


def dot(a, b):
    return jnp.dot(a, b, preferred_element_type=F32)


def dot_nt(a, b):
    return lax.dot_general(a, b, (((1,), (1,)), ((), ())), preferred_element_type=F32)


def dot_tn(a, b):
    return lax.dot_general(a, b, (((0,), (0,)), ((), ())), preferred_element_type=F32)


def piece_rows():
    rows = np.full((2, PADDED), -1, np.int32)
    n = 0
    for core in range(2):
        for first in range(4):
            for second in range(4):
                for low in range(2):
                    for r in range(16):
                        if r < PIECE:
                            rows[0, n] = (((first * 4 + second) * 2 + low) * 2 + core) * PIECE + r
                            rows[1, n] = (((second * 4 + first) * 2 + low) * 2 + core) * PIECE + r
                        n += 1
    return rows


def pair_blocks(kv_ref, c, j, low, high):
    rows = slice(c * CH, (c + 1) * CH)
    k = kv_ref[rows, pl.ds(pl.multiple_of(j * PAIR, PAIR), PAIR)]
    v = kv_ref[rows, pl.ds(pl.multiple_of(DE + j * PAIR, PAIR), PAIR)]
    return (
        jnp.concatenate([k * low, k * high], axis=0),
        jnp.concatenate([v * low, v * high], axis=0),
    )


def mega(
    slot_ref,
    rows_ref,
    pos_ref,
    alt_ref,
    sent_ref,
    states_ref,
    wspan_ref,
    q_ref,
    og_ref,
    wq_own_ref,
    wo_own_ref,
    wd_ref,
    wqo_ref,
    att_out,
    cross_out,
    rq_ref,
    ro_ref,
    got_ref,
    emb_ref,
    kvp_ref,
    kvg_ref,
    kv_ref,
    qo_ref,
    ogo_ref,
    wb_ref,
    sb_ref,
    wq_ref,
    wo_ref,
    eq_ref,
    att_ref,
    probs_ref,
    enc_ref,
    dkv_ref,
    gkv_ref,
    sum_ref,
    pad_ref,
    own_ref,
    cross_ref,
    all_ref,
    slots_ref,
    g_ref,
    core_ref,
    acc1_ref,
    first1_ref,
    first2_ref,
    acc2_ref,
    second1_ref,
    second2_ref,
    acc3_ref,
    last_ref,
    emb_sems,
    swap_sems,
    weight_sems,
    slot_sems,
    sum_sems,
    local_sems,
):
    span, dp, half = lax.axis_index("span"), lax.axis_index("dp"), lax.axis_index("mp")
    z, y, x_low, core = span // 4, span % 4, dp // 2, dp % 2
    partner = {"span": span, "dp": dp, "mp": 1 - half}
    peer = {"span": span, "dp": x_low * 2 + 1 - core, "mp": half}
    where = (z, y)

    def in_span(k):
        return {"span": lax.rem(span + k, 16), "dp": dp, "mp": half}

    def along(axis, by):
        if axis == 0:
            return {"span": lax.rem(z + by + 4, 4) * 4 + y, "dp": dp, "mp": half}
        return {"span": z * 4 + lax.rem(y + by + 4, 4), "dp": dp, "mp": half}

    others = [
        {"span": span, "dp": (1 - x_low) * 2 + core, "mp": half},
        partner,
        {"span": span, "dp": (1 - x_low) * 2 + core, "mp": 1 - half},
    ]
    spans_in = [
        pltpu.make_async_copy(
            wspan_ref.at[pl.ds(i * 512, 512)],
            (dkv_ref, gkv_ref)[i // 2].at[i % 2, :, pl.ds(0, 2 * DE)],
            local_sems.at[i],
        )
        for i in range(4)
    ]
    alt_in = pltpu.make_async_copy(alt_ref, eq_ref, local_sems.at[4])
    for copy in spans_in:
        copy.start()
    alt_in.start()

    barrier = pltpu.get_barrier_semaphore()
    friends = [in_span(k) for k in range(1, 16)] + [peer] + others
    for friend in friends:
        pl.semaphore_signal(barrier, inc=1, device_id=friend, device_id_type=pl.DeviceIdType.MESH)
    pl.semaphore_wait(barrier, len(friends))

    def send(src, dst, sems, device):
        copy = pltpu.make_async_remote_copy(
            src_ref=src,
            dst_ref=dst,
            send_sem=sems.at[0],
            recv_sem=sems.at[1],
            device_id=device,
            device_id_type=pl.DeviceIdType.MESH,
        )
        copy.start()
        return copy

    def add(*parts):
        total = parts[0].astype(F32)
        for part in parts[1:]:
            total = total + part.astype(F32)
        return total

    embs = [
        send(sent_ref.at[lax.rem(span + k, 16)], got_ref.at[span], emb_sems.at[k], in_span(k))
        for k in range(1, 16)
    ]
    def mod(v):
        return lax.rem(v + 4, 4)

    def wide_at(r, group, piece, count):
        n = core * 2 + r
        return wb_ref.at[
            pl.ds(pl.multiple_of(n * 224, 224), 224),
            pl.ds(pl.multiple_of(group * 512 + piece * 128, 128), count * 128),
        ]

    def small_at(r, group, piece, count):
        n = core * 2 + r
        return sb_ref.at[pl.ds(group * 4 + piece, count), pl.ds(pl.multiple_of(n * 112, 112), 112)]

    def share(r, sem, device, wide, small):
        return [
            send(wide, wide, weight_sems.at[r, sem], device),
            send(small, small, weight_sems.at[r, sem + 1], device),
        ]

    ranks = ((z, y), (y, z))
    weights = []
    for r in range(2):
        n = core * 2 + r
        p, s = ranks[r]
        weights.append(
            [
                send(
                    wd_ref.at[
                        pl.ds(pl.multiple_of(n * 224, 224), 224),
                        pl.ds(pl.multiple_of(s * 512 + p * 128, 128), 128),
                    ],
                    wide_at(r, s, p, 1),
                    weight_sems.at[r, 0],
                    others[2],
                ),
                send(wqo_ref.at[pl.ds(r, 1)], small_at(r, s, p, 1), weight_sems.at[r, 1], others[2]),
            ]
        )
    got_ref[span] = sent_ref[span]

    for copy in spans_in:
        copy.wait()

    def project_span(i, _):
        cols = pl.ds(pl.multiple_of(i * 256, 256), 256)
        total = jnp.zeros((2 * SPANS * CH, 256), F32)
        for n in range(4):
            total += dot(states_ref[:, n * 512 : (n + 1) * 512], (dkv_ref, gkv_ref)[n // 2][n % 2, :, cols])
        total = total.astype(BF16)
        kvp_ref[0, :, cols] = total[: SPANS * CH]
        kvp_ref[1, :, cols] = total[SPANS * CH :]
        return 0

    lax.fori_loop(0, 2 * DE // 256, project_span, 0)
    kv_swap = send(kvp_ref.at[1 - half], kvg_ref, swap_sems.at[0], partner)
    q_swap = send(q_ref.at[1 - half], qo_ref, swap_sems.at[1], partner)
    og_swap = send(og_ref.at[1 - half], ogo_ref, swap_sems.at[2], partner)

    def settle(r):
        for copy in weights[r]:
            copy.wait()

    for r in range(2):
        settle(r)
        p, s = ranks[r]
        weights[r] = []
        for i, by in enumerate((1, -1)):
            weights[r] += share(r, 2 + 2 * i, along(r, by), wide_at(r, s, p, 1), small_at(r, s, p, 1))
    for r in range(2):
        settle(r)
        p, s = ranks[r]
        weights[r] = []
        for i, by in enumerate((1, -1)):
            f = mod(p - by)
            wide, small = wide_at(r, s, f, 1), small_at(r, s, f, 1)
            weights[r] += share(
                r,
                6 + 2 * i,
                along(r, by),
                wide.at[pl.ds(112 * i, 112)],
                small.at[:, pl.ds(48 * i, 48 + 16 * i)],
            )
    for r in range(2):
        settle(r)
        p, s = ranks[r]
        weights[r] = []
        for i, by in enumerate((1, -1)):
            weights[r] += share(r, 10 + 2 * i, along(1 - r, by), wide_at(r, s, 0, 4), small_at(r, s, 0, 4))

    for copy in embs:
        copy.wait()
    alt_in.wait()
    slot_of = lax.broadcasted_iota(jnp.int32, (1, 16 * ROOM), 1)
    pick = (pos_ref[...] == slot_of).astype(F32).astype(BF16)
    over = slot_ref[2, 0] > 0
    for lane_at, size in TILES:
        cols = slice(lane_at, lane_at + size)
        rows = jnp.concatenate([got_ref[i, :, cols] for i in range(16)], axis=0)
        emb_ref[:, cols] = jnp.where(over, eq_ref[:, cols].astype(F32), dot(pick, rows)).astype(BF16)

    for r in range(2):
        settle(r)
        p, s = ranks[r]
        weights[r] = []
        for i, by in enumerate((1, -1)):
            f = mod(s - by)
            weights[r] += share(r, 14 + 2 * i, along(1 - r, by), wide_at(r, f, 2 * i, 2), small_at(r, f, 2 * i, 2))
    for r in range(2):
        settle(r)
        n = core * 2 + r
        weights[r] = share(
            r,
            18,
            peer,
            wb_ref.at[pl.ds(pl.multiple_of(n * 224, 224), 224)],
            sb_ref.at[:, pl.ds(pl.multiple_of(n * 112, 112), 112)],
        )
    kv_swap.wait()
    kv_ref[...] = add(kvp_ref[half], kvg_ref[...]).astype(BF16)
    for r in range(2):
        settle(r)

    place = lax.broadcasted_iota(jnp.int32, (HALF, 256), 0)
    wide = lax.broadcasted_iota(jnp.int32, (512, 256), 0)
    wide = jnp.where(wide < 384, wide, jnp.where(wide >= 448, wide - 64, -DE))
    col = lax.broadcasted_iota(jnp.int32, (HALF, 256), 1)
    wide_col = lax.broadcasted_iota(jnp.int32, (512, 256), 1)
    for lane_at, size in TILES:
        mine = (place + half * HALF == col + lane_at).astype(F32).astype(BF16)[:, :size]
        his = (wide + (1 - half) * HALF == wide_col + lane_at).astype(F32).astype(BF16)[:, :size]
        for up in range(2):
            rows = slice(up * HALF, (up + 1) * HALF)
            other = jnp.concatenate([sb_ref[up * 4 + i] for i in range(4)], axis=1)
            wq_ref[rows, lane_at : lane_at + size] = (dot(wq_own_ref[rows, :], mine) + dot(other, his)).astype(BF16)
    wo_ref[pl.ds(pl.multiple_of(half * HALF, HALF), HALF), :] = wo_own_ref[...]
    for i in range(7):
        wo_ref[pl.ds(pl.multiple_of((1 - half) * HALF, HALF), HALF), i * 128 : (i + 1) * 128] = sb_ref[8 + i]

    lane = lax.broadcasted_iota(jnp.int32, (1, PAIR), 1)
    is_low = lane < EHD
    low = is_low.astype(F32).astype(BF16)
    high = (lane >= EHD).astype(F32).astype(BF16)

    for lane_at, size in TILES:
        cols = slice(lane_at, lane_at + size)
        eq_ref[:, cols] = dot(emb_ref[...], wq_ref[:, cols]).astype(BF16)

    def forward(j, _):
        cols = pl.ds(pl.multiple_of(j * PAIR, PAIR), PAIR)
        for c in range(SPANS):
            rows = slice(c * NB * R, (c + 1) * NB * R)
            kbd, vbd = pair_blocks(kv_ref, c, j, low, high)
            s = dot_nt(eq_ref[rows, cols], kbd) * (1.0 / math.sqrt(EHD))
            top0 = jnp.max(jnp.where(is_low, s, -jnp.inf), axis=1, keepdims=True)
            top1 = jnp.max(jnp.where(is_low, -jnp.inf, s), axis=1, keepdims=True)
            p = jnp.exp(s - jnp.where(is_low, top0, top1))
            sum0 = jnp.sum(jnp.where(is_low, p, 0.0), axis=1, keepdims=True)
            sum1 = jnp.sum(jnp.where(is_low, 0.0, p), axis=1, keepdims=True)
            p = p * jnp.where(is_low, 1.0 / sum0, 1.0 / sum1)
            probs_ref[c, j] = p
            att_ref[rows, cols] = dot(p.astype(BF16), vbd).astype(BF16)
        return 0

    lax.fori_loop(0, PAIRS, forward, 0)

    feature = lax.broadcasted_iota(jnp.int32, (DE, HALF), 0)
    column = lax.broadcasted_iota(jnp.int32, (DE, HALF), 1)

    def half_of(which):
        chosen = (feature == column + which * HALF).astype(F32).astype(BF16)
        return dot(att_ref[...], chosen).astype(BF16)

    own_ref[...] = half_of(1 - half).reshape(4, R, HALF)
    att_swap = send(own_ref, all_ref.at[half], swap_sems.at[3], partner)
    all_ref[half] = half_of(half).reshape(4, R, HALF)

    for lane_at, size in TILES:
        cols = slice(lane_at, lane_at + size)
        enc_ref[:, cols] = (emb_ref[:, cols].astype(F32) + dot(att_ref[...], wo_ref[:, cols])).astype(BF16)

    def project(i, _):
        cols = pl.ds(pl.multiple_of(i * 256, 256), 256)
        dkv_ref[0, :, cols] = dot(enc_ref[...], wd_ref[:, cols]).astype(BF16)
        dkv_ref[1, :, cols] = dot(enc_ref[...], wb_ref[:, cols]).astype(BF16)
        return 0

    lax.fori_loop(0, DEC // 256, project, 0)

    att_swap.wait()
    for e in range(16):
        unit, there = slot_ref[0, e], slot_ref[1, e]
        slots_ref[e] = all_ref[unit // 4, unit % 4] * there.astype(F32).astype(BF16)
    waiting = [
        send(slots_ref.at[lax.rem(span + k, 16)], att_out.at[span], slot_sems.at[k], in_span(k))
        for k in range(1, 16)
    ]
    stay = pltpu.make_async_copy(slots_ref.at[span], att_out.at[span], local_sems.at[0])
    stay.start()
    q_swap.wait()
    og_swap.wait()
    scale = 1.0 / math.sqrt(HD)

    def decode(h, _):
        kcols = pl.ds(pl.multiple_of(h * HD, HD), HD)
        vcols = pl.ds(pl.multiple_of(DEC // 2 + h * HD, HD), HD)
        for g in range(2):
            for c in range(SPANS):
                few = slice(c * CH, (c + 1) * CH)
                rows = slice(c * NB * R, (c + 1) * NB * R)
                q = q_ref[half, few, kcols] if g == 0 else qo_ref[few, kcols]
                og = og_ref[half, few, kcols] if g == 0 else ogo_ref[few, kcols]
                k, v = dkv_ref[g, rows, kcols], dkv_ref[g, rows, vcols]
                s = dot_nt(q, k) * scale
                p = jnp.exp(s - jnp.max(s, axis=1, keepdims=True))
                p = p * (1.0 / jnp.sum(p, axis=1, keepdims=True))
                pb = p.astype(BF16)
                cross = dot(pb, v).astype(BF16)
                cross_ref[g, few, kcols] = cross
                gkv_ref[g, rows, vcols] = dot_tn(pb, og).astype(BF16)
                row = jnp.sum(og.astype(F32) * cross.astype(F32), axis=1, keepdims=True)
                ds = (p * (dot_nt(og, v) - row) * scale).astype(BF16)
                gkv_ref[g, rows, kcols] = dot_tn(ds, q).astype(BF16)
        return 0

    lax.fori_loop(0, 8, decode, 0)
    waiting.append(send(cross_ref.at[1], cross_out.at[half], swap_sems.at[4], partner))
    mine = pltpu.make_async_copy(cross_ref.at[0], cross_out.at[half], local_sems.at[1])
    mine.start()
    sum_ref[...] = jnp.zeros_like(sum_ref)

    def collect(i, _):
        cols = pl.ds(pl.multiple_of(i * 256, 256), 256)
        sum_ref[...] += dot_nt(gkv_ref[0, :, cols], wd_ref[:, cols]) + dot_nt(
            gkv_ref[1, :, cols], wb_ref[:, cols]
        )
        return 0

    lax.fori_loop(0, DEC // 256, collect, 0)
    enc_ref[...] = sum_ref[...].astype(BF16)

    def steps(k):
        sems = sum_sems.at[k]
        copies = [send(g_ref.at[k, 1 - core], core_ref.at[k], sems.at[0], peer)]
        yield
        copies[0].wait()
        for i in range(4):
            acc1_ref[k, i] = add(g_ref[k, core, i], core_ref[k, i]).astype(BF16)
        levels = ((acc1_ref, first1_ref, first2_ref, acc2_ref, 2, 1), (acc2_ref, second1_ref, second2_ref, acc3_ref, 1, 5))
        for level, (acc, got1, got2, out, cut, sem) in enumerate(levels):
            axis = k if level == 0 else 1 - k
            p = where[axis]
            far, up, down = mod(p + 2), mod(p + 1), mod(p - 1)
            one, two = pl.ds(0, cut), pl.ds(cut, cut)
            copies = [
                send(acc.at[k, far, one], got1.at[k, 0], sems.at[sem], along(axis, 1)),
                send(acc.at[k, far, two], got1.at[k, 1], sems.at[sem + 1], along(axis, -1)),
            ]
            yield
            for copy in copies:
                copy.wait()
            acc[k, up, one] = add(acc[k, up, one], got1[k, 0]).astype(BF16)
            acc[k, down, two] = add(acc[k, down, two], got1[k, 1]).astype(BF16)
            copies = [
                send(acc.at[k, up], got2.at[k, 0], sems.at[sem + 2], along(axis, 1)),
                send(acc.at[k, down], got2.at[k, 1], sems.at[sem + 3], along(axis, -1)),
            ]
            yield
            for copy in copies:
                copy.wait()
            out[k] = add(acc[k, p], got2[k, 0], got2[k, 1]).astype(BF16)
        copies = []
        for n, other in enumerate(others):
            to_low = x_low if n == 1 else 1 - x_low
            copies.append(send(acc3_ref.at[k, to_low], last_ref.at[k, n], sems.at[9 + n], other))
        yield
        for copy in copies:
            copy.wait()
        (rq_ref, ro_ref)[k][...] = add(acc3_ref[k, x_low], last_ref[k, 0], last_ref[k, 1], last_ref[k, 2])
        yield

    def pad(ref, order):
        for lane_at in range(0, PADDED, 256):
            spread = (
                lax.broadcasted_iota(jnp.int32, (DE, 256), 0)
                == rows_ref[order : order + 1, lane_at : lane_at + 256]
            )
            pad_ref[:, lane_at : lane_at + 256] = dot(ref[...], spread.astype(F32).astype(BF16)).astype(BF16)

    def outer(k, ref):
        def tile(i, _):
            cols = pl.ds(pl.multiple_of(i * 256, 256), 256)
            g_ref[k, i // 2, pl.ds((i % 2) * 2, 2)] = (
                dot_tn(pad_ref[:, cols], ref[...]).astype(BF16).reshape(2, 4, 2, 16, DE)
            )
            return 0

        lax.fori_loop(0, PADDED // 256, tile, 0)

    pad(enc_ref, 1)
    outer(1, att_ref)
    out_sum = steps(1)
    next(out_sum)
    for lane_at, size in TILES:
        cols = slice(lane_at, lane_at + size)
        eq_ref[:, cols] = dot_nt(enc_ref[...], wo_ref[cols, :]).astype(BF16)
    next(out_sum)

    def backward(j, _):
        cols = pl.ds(pl.multiple_of(j * PAIR, PAIR), PAIR)
        for c in range(SPANS):
            rows = slice(c * NB * R, (c + 1) * NB * R)
            kbd, vbd = pair_blocks(kv_ref, c, j, low, high)
            ga = eq_ref[rows, cols]
            prod = ga.astype(F32) * att_ref[rows, cols].astype(F32)
            row0 = jnp.sum(jnp.where(is_low, prod, 0.0), axis=1, keepdims=True)
            row1 = jnp.sum(jnp.where(is_low, 0.0, prod), axis=1, keepdims=True)
            diff = dot_nt(ga, vbd) - jnp.where(is_low, row0, row1)
            ds = (probs_ref[c, j] * diff * (1.0 / math.sqrt(EHD))).astype(BF16)
            eq_ref[rows, cols] = dot(ds, kbd).astype(BF16)
        return 0

    lax.fori_loop(0, PAIRS, backward, 0)
    next(out_sum)
    pad(emb_ref, 0)
    next(out_sum)
    outer(0, eq_ref)
    query_sum = steps(0)
    for _ in range(7):
        next(query_sum)
        next(out_sum, None)
    for copy in waiting:
        copy.wait()
    mine.wait()
    stay.wait()


def run(slot, pos, alt, sent, states, w_span, q, og, w_q, w_o, w_d, wqo):
    vmem = pl.BlockSpec(memory_space=pltpu.VMEM)
    anywhere = pl.BlockSpec(memory_space=pl.ANY)
    dma = pltpu.SemaphoreType.DMA
    return pl.pallas_call(
        mega,
        out_shape=(
            jax.ShapeDtypeStruct((16, R, HALF), BF16),
            jax.ShapeDtypeStruct((2, SPANS * CH, DEC // 2), BF16),
            jax.ShapeDtypeStruct((16, DE), F32),
            jax.ShapeDtypeStruct((16, DE), F32),
        ),
        in_specs=[pl.BlockSpec(memory_space=pltpu.SMEM), vmem, vmem, anywhere, vmem, vmem, anywhere]
        + [vmem] * 6,
        out_specs=(anywhere, anywhere, vmem, vmem),
        scratch_shapes=[
            pltpu.VMEM((16, ROOM, DE), BF16),
            pltpu.VMEM((TOK, DE), BF16),
            pltpu.VMEM((2, SPANS * CH, 2 * DE), BF16),
            pltpu.VMEM((SPANS * CH, 2 * DE), BF16),
            pltpu.VMEM((SPANS * CH, 2 * DE), BF16),
            pltpu.VMEM((SPANS * CH, DEC // 2), BF16),
            pltpu.VMEM((SPANS * CH, DEC // 2), BF16),
            pltpu.VMEM((DE, DEC), BF16),
            pltpu.VMEM((16, HALF, 128), BF16),
            pltpu.VMEM((DE, DE), BF16),
            pltpu.VMEM((DE, DE), BF16),
            pltpu.VMEM((TOK, DE), BF16),
            pltpu.VMEM((TOK, DE), BF16),
            pltpu.VMEM((SPANS, PAIRS, NB * R, PAIR), F32),
            pltpu.VMEM((TOK, DE), BF16),
            pltpu.VMEM((2, TOK, DEC), BF16),
            pltpu.VMEM((2, TOK, DEC), BF16),
            pltpu.VMEM((TOK, DE), F32),
            pltpu.VMEM((TOK, PADDED), BF16),
            pltpu.VMEM((4, R, HALF), BF16),
            pltpu.VMEM((2, SPANS * CH, DEC // 2), BF16),
            pltpu.VMEM((2, 4, R, HALF), BF16),
            pltpu.VMEM((16, R, HALF), BF16),
            pltpu.VMEM((2, 2, 4, 4, 2, 16, DE), BF16),
            pltpu.VMEM((2, 4, 4, 2, 16, DE), BF16),
            pltpu.VMEM((2, 4, 4, 2, 16, DE), BF16),
            pltpu.VMEM((2, 2, 2, 2, 16, DE), BF16),
            pltpu.VMEM((2, 2, 4, 2, 16, DE), BF16),
            pltpu.VMEM((2, 4, 2, 16, DE), BF16),
            pltpu.VMEM((2, 2, 1, 16, DE), BF16),
            pltpu.VMEM((2, 2, 2, 16, DE), BF16),
            pltpu.VMEM((2, 2, 16, DE), BF16),
            pltpu.VMEM((2, 3, 16, DE), BF16),
            dma((16, 2)),
            dma((5, 2)),
            dma((2, 20, 2)),
            dma((16, 2)),
            dma((2, 12, 2)),
            dma((5,)),
        ],
        compiler_params=pltpu.CompilerParams(
            vmem_limit_bytes=63 * 2**20, collective_id=1, has_side_effects=True
        ),
        cost_estimate=pl.CostEstimate(
            flops=16 * 10**9, bytes_accessed=30 * 2**20, transcendentals=10**6
        ),
    )(slot, jnp.asarray(piece_rows()), pos, alt, sent, states, w_span, q, og, w_q, w_o, w_d, wqo)


def body(
    span_states,
    queries,
    out_grad,
    neighbour_ids,
    assignment,
    embed_table,
    w_span_kv,
    w_query_enc,
    w_out_enc,
    w_dec_kv,
):
    bf16 = jnp.bfloat16
    n_span = lax.axis_size("span")
    span_index = lax.axis_index("span")
    half_index = lax.axis_index("mp")
    seq_count, local_tokens, half_width = span_states.shape
    spans = local_tokens // CH
    units = spans * NB
    dec_cols = 2 * queries.shape[2]
    vocab_rows = embed_table.shape[0]
    tokens = units * R

    ids_m = lax.dynamic_index_in_dim(
        neighbour_ids.reshape(seq_count, n_span, tokens), half_index, 0, keepdims=False
    )
    rows, pos, over = lists(ids_m, span_index, vocab_rows, n_span)
    sent = jnp.take(embed_table, rows.reshape(-1), axis=0).reshape(n_span, ROOM, DE)

    def whole_gather():
        shifted = ids_m.reshape(-1) - span_index * vocab_rows
        inside = (shifted >= 0) & (shifted < vocab_rows)
        found = jnp.take(embed_table, jnp.clip(shifted, 0, vocab_rows - 1), axis=0)
        found = jnp.where(inside[:, None], found, jnp.zeros_like(found))
        found = lax.all_to_all(
            found.reshape(n_span, tokens, DE), "span", split_axis=0, concat_axis=0, tiled=True
        )
        return jnp.sum(found.astype(F32), axis=0).astype(bf16)

    alt = lax.cond(over, whole_gather, lambda: jnp.zeros((tokens, DE), bf16))

    core = lax.axis_index("dp") % 2
    wqo = []
    for r in range(2):
        piece = (span_index % 4) * 4 + span_index // 4 if r == 0 else span_index
        start = (core * 2 + r) * 112
        from_q = lax.dynamic_slice(
            w_query_enc,
            ((piece // 4) * HALF + start, jnp.minimum((piece % 4) * 128, HALF - 128)),
            (112, 128),
        )
        from_o = lax.dynamic_slice(w_out_enc, (start, (piece - 8) * 128), (112, 128))
        wqo.append(jnp.where(piece < 8, from_q, from_o))
    wqo = jnp.stack(wqo)

    dest = lax.dynamic_index_in_dim(assignment[0, :, :, 0], span_index, 0, keepdims=False)
    at = dest[None, :] == jnp.arange(n_span, dtype=jnp.int32)[:, None]
    numbers = jnp.arange(seq_count * units, dtype=jnp.int32)
    slot = jnp.stack(
        [
            jnp.sum(jnp.where(at, numbers[None, :], 0), axis=1),
            jnp.sum(at.astype(jnp.int32), axis=1),
            jnp.full((n_span,), over.astype(jnp.int32)),
        ]
    )
    attended_out, cross_out, rq, ro = run(
        slot,
        pos[:, None],
        alt,
        sent,
        span_states.reshape(-1, half_width),
        w_span_kv,
        queries,
        out_grad,
        w_query_enc,
        w_out_enc,
        w_dec_kv.reshape(DE, dec_cols),
        wqo,
    )
    grad_query_enc = lax.dynamic_slice_in_dim(rq[:PIECE], half_index * HALF, HALF, 1)
    grad_out_enc = lax.dynamic_slice_in_dim(ro[:PIECE], half_index * HALF, HALF, 1).T
    return (
        cross_out,
        attended_out.reshape(1, 1, n_span, 1, R, HALF),
        grad_query_enc,
        grad_out_enc,
    )


def solution(mesh):
    return jax.shard_map(
        body,
        mesh=mesh,
        in_specs=(
            P("dp", "span", "mp"),
            P("dp", "span", "mp"),
            P("dp", "span", "mp"),
            P("dp", None, None, None),
            P("dp", None, None, None),
            P("span", None),
            P("mp", None),
            P(None, "mp"),
            P("mp", None),
            P(None, None, "mp"),
        ),
        out_specs=(
            P("dp", "span", "mp"),
            P("dp", "span", None, None, None, "mp"),
            P(("span", "dp"), "mp"),
            P("mp", ("span", "dp")),
        ),
        check_vma=False,
    )
```

time: 971 us -> 193 us (0.20)
  waiting for transfers between devices: 730 us -> 0 us
  Pallas kernels: 0 us -> 157 us
  matrix products: 77.7 us -> 0.18 us
  local copies, waits for them, and re-layouts: 63.3 us -> 22.9 us
  starting transfers between devices: 30.7 us -> 0 us
  blocking collectives: 21.6 us -> 0 us
  between operations: 18.5 us -> 1.63 us
    unnamed x7 -> x0, waiting for transfers between devices: 483 us -> none
    pallas_call x0 -> x1, Pallas kernels: none -> 157 us  [run(): pl.pallas_call(mega, out_shape=(jax.ShapeDtypeStruct((16, R, HALF), BF16)...]
    all_gather x3 -> x0, waiting for transfers between devices: 94.4 us -> none  [the longest x1 72.7 us: body(): lax.all_gather(w_dec_kv, 'mp', axis=2, tiled=True).reshape(DE, 2 * dec_cols)]
    reduce_scatter x2 -> x0, waiting for transfers between devices: 80.6 us -> none  [the longest x1 50 us: body(): lax.psum_scatter(grad_query_part, 'mp', scatter_dimension=1, tiled=True)]
    dot_general x16 -> x0, matrix products: 77.5 us -> none  [the longest x1 19.5 us: body(): jnp.dot(encoded, w_d, preferred_element_type=f32).astype(bf16)]
    all_to_all x6 -> x0, waiting for transfers between devices: 72 us -> none  [the longest x1 25.2 us: body(): lax.all_to_all(slots, 'span', split_axis=0, concat_axis=0, tiled=True)]
    all_to_all x6 -> x0, starting transfers between devices: 30.2 us -> none  [the longest x1 8.13 us: body(): got = lax.all_to_all(sent, 'span', split_axis=0, concat_axis=0, tiled=True)]
    all_to_all x1 -> x0, blocking collectives: 12.2 us -> none  [swap_heads(): both = lax.all_to_all(x, 'mp', split_axis=0, concat_axis=0, tiled=True)]
  transfers between devices with their start and end apart: 12 -> 0, of which waited for: 11 -> 0; matrix products, arithmetic and copies ran while one was open for 6% -> 0% of each run, Pallas kernels for 0% -> 0%
where the time goes in v3:
time: 193 us
  Pallas kernels  157 us (81%)
  local copies, waits for them, and re-layouts  22.9 us (12%)
  other arithmetic  11.1 us (6%)
    pallas_call x1, Pallas kernels, run(): pl.pallas_call(mega, out_shape=(jax.ShapeDtypeStruct((16, R, HALF), BF16)...  157 us
    unnamed x18, local copies, waits for them, and re-layouts  12 us
    gather x1, local copies, waits for them, and re-layouts, body(): jnp.take(embed_table, rows.reshape(-1), axis=0).reshape(n_span, ROOM, DE)  7.47 us
    reduce_or x1, other arithmetic, lists(): dup = jnp.any(same & (t[None, None, :] < t[None, :, None]), axis=2)  4.28 us

profile of v3, /device:TPU:0, one launch (start us, length us, event | category | flops | bytes accessed | tf_op | source)
XLA Modules:
  0.0 192.6 jit_solution(10935367822741924566)
XLA Ops:
  0.6 0.0 copy-start
  0.8 0.5 copy-done
  1.3 0.3 dynamic-slice_reduce_fusion
  1.6 0.1 select_reduce_fusion.2
  1.7 0.9 reshape.272
  2.7 0.3 select_reduce_fusion.1
  3.0 0.5 convert_reduce_fusion
  3.5 0.2 copy.36
  3.7 0.1 copy.39
  3.9 0.1 copy.35
  4.0 0.8 fusion.4.pos_ref
  4.8 0.1 iota_compare_fusion.3
  4.9 4.3 %and_reduce_fusion = pred[16,512]{1,0:T(8,128)(4,1)S(1)} fusion(s32[16,512]{1,0:T(8,128)S(1)} %get-tuple-element.45, pred[512,512]{1,0:T(8,128)(4,1)S(1)} %iota_compare_fusion.3), kind=kLoop, calls=%fused_computation.9 | loop fusion | flops 12574720 | bytes 303104 | tf_op jit(solution)/shard_map/reduce_or | solution.py:24
  9.2 0.4 convert_reduce_fusion.1
  9.6 0.6 reduce_max.9
  10.8 0.1 pad.4.clone
  10.9 0.7 add_add_fusion.slot_ref
  11.6 0.2 convolution_convert_fusion
  11.8 0.5 select_reduce_fusion
  12.2 0.1 reshape.273
  12.3 0.0 copy-start.5
  12.4 0.3 conditional.1
  12.4 0.1 broadcast.270
  12.6 0.0 copy-start.3
  12.6 0.8 copy-done.5
  13.5 0.7 copy.42.wq_own_ref
  14.2 0.0 copy-start.2
  14.2 1.0 select_bitcast_fusion.1
  15.2 0.0 copy-done.3
  15.2 0.6 pad_maximum_fusion.wqo_ref
  15.9 7.5 %gather_fusion.1 = bf16[768,896]{1,0:T(8,128)(2,1)S(1)} fusion(bf16[4000,896]{1,0:T(8,128)(2,1)} %param.18, s32[1024]{0:T(1024)S(1)} %pad_clamp_fusion), kind=kCustom, calls=%fused_computation.1 | custom fusion | bytes 2755584 | tf_op jit(solution)/shard_map/jit(_take)/gather | solution.py:659
  23.3 0.0 copy-done.2
  23.3 1.3 broadcast_select_fusion.sent_ref
  24.7 0.0 copy-start.4
  24.7 5.1 %copy.46 = bf16[112,8,2,1024]{3,1,2,0:T(8,128)(2,1)} copy(bf16[112,8,2,1024]{3,2,1,0:T(2,128)(2,1)} %bitcast.35) | data formatting | bytes 7340032
  29.8 0.0 copy-done.4
  29.8 0.0 copy-start.1
  29.8 156.5 %shard_map.138 = (bf16[16,128,448]{2,1,0:T(8,128)(2,1)}, bf16[2,128,1024]{2,1,0:T(8,128)(2,1)}, f32[16,896]{1,0:T(8,128)}, f32[16,896]{1,0:T(8,128)}) custom-call(s32[3,16]{1,0:T(4,128)} %add_add_fusion.slot_ref, s32[2,1024]{1,0:T(2,128)} %constant.179.clone.rows_ref, s32[512,1]{1,0:T(8,128)} %fusion.4.pos_ref, bf16[512,896]{1,0:T(8,128)(2,1)S(1)} %copy-done.4, ...), custom_call_target="tpu_custom_call" | custom-call | flops 16000000000 | bytes 31457280 | tf_op jit(solution)/shard_map/pallas_call | solution.py:571
  186.3 0.0 copy-start.6
  186.4 3.9 %copy.43 = bf16[1,1,16,1,128,448]{4,5,3,2,1,0:T(8,128)(2,1)} copy(bf16[1,1,16,1,128,448]{5,4,2,3,1,0:T(8,128)(2,1)} %bitcast.37) | data formatting | bytes 3670016
  190.3 1.5 dynamic-slice_bitcast_fusion
  191.8 0.0 copy-done.6
  191.8 0.8 copy.50
  192.6 0.0 copy-done.1
  (9 shorter events, 0.1 us)
Async XLA Ops:
  0.6 0.7 copy-start
  12.3 1.1 copy-start.5
  12.6 2.6 %copy-start.3 = (bf16[512,896]{1,0:T(8,128)(2,1)}, bf16[512,896]{1,0:T(8,128)(2,1)S(1)}, u32[]{:S(2)}) copy-start(bf16[512,896]{1,0:T(8,128)(2,1)S(1)} %get-tuple-element.63.alt_ref) | copy-start | bytes 2752516
  14.2 9.1 %copy-start.2 = (bf16[896,448]{1,0:T(8,128)(2,1)}, bf16[896,448]{1,0:T(8,128)(2,1)S(1)}, u32[]{:S(2)}) copy-start(bf16[896,448]{1,0:T(8,128)(2,1)S(1)} %copy.42.wq_own_ref) | copy-start | bytes 2408452
  24.7 5.2 %copy-start.4 = (bf16[512,896]{1,0:T(8,128)(2,1)S(1)}, bf16[512,896]{1,0:T(8,128)(2,1)}, u32[]{:S(2)}) copy-start(bf16[512,896]{1,0:T(8,128)(2,1)} %copy-done.3) | copy-start | bytes 2752516
  29.8 162.8 %copy-start.1 = (s32[1,16,8,1]{1,3,2,0:T(1,128)S(1)}, s32[1,16,8,1]{1,3,2,0:T(1,128)}, u32[]{:S(2)}) copy-start(s32[1,16,8,1]{1,3,2,0:T(1,128)} %param.17) | copy-start | bytes 1540
  186.3 5.5 %copy-start.6 = (bf16[2,128,1024]{2,1,0:T(8,128)(2,1)S(1)}, bf16[2,128,1024]{2,1,0:T(8,128)(2,1)}, u32[]{:S(2)}) copy-start(bf16[2,128,1024]{2,1,0:T(8,128)(2,1)} %get-tuple-element.59) | copy-start | bytes 1572868

commit v4 on v3

--- a/solution.py
+++ b/solution.py
@@ -114,7 +114,8 @@
     rows_ref,
     pos_ref,
     alt_ref,
-    sent_ref,
+    list_ref,
+    table_ref,
     states_ref,
     wspan_ref,
     q_ref,
@@ -127,6 +128,8 @@
     cross_out,
     rq_ref,
     ro_ref,
+    picked_ref,
+    sent_ref,
     got_ref,
     emb_ref,
     kvp_ref,
@@ -146,7 +149,7 @@
     gkv_ref,
     sum_ref,
     pad_ref,
-    own_ref,
+    pad_emb_ref,
     cross_ref,
     all_ref,
     slots_ref,
@@ -156,8 +159,7 @@
     first1_ref,
     first2_ref,
     acc2_ref,
-    second1_ref,
-    second2_ref,
+    second_ref,
     acc3_ref,
     last_ref,
     emb_sems,
@@ -173,8 +175,13 @@
     peer = {"span": span, "dp": x_low * 2 + 1 - core, "mp": half}
     where = (z, y)
 
+    offsets = ((0, 1), (1, 0), (0, 3), (3, 0), (2, 1), (1, 2), (2, 3), (3, 2), (1, 1), (3, 3), (1, 3), (3, 1), (2, 0), (0, 2), (2, 2))
+
+    def span_at(k):
+        return lax.rem(z + offsets[k][0], 4) * 4 + lax.rem(y + offsets[k][1], 4)
+
     def in_span(k):
-        return {"span": lax.rem(span + k, 16), "dp": dp, "mp": half}
+        return {"span": span_at(k), "dp": dp, "mp": half}
 
     def along(axis, by):
         if axis == 0:
@@ -185,6 +192,17 @@
         {"span": span, "dp": (1 - x_low) * 2 + core, "mp": half},
         partner,
         {"span": span, "dp": (1 - x_low) * 2 + core, "mp": 1 - half},
+    ]
+    def area(i):
+        return (dkv_ref, gkv_ref)[i // 4].at[(i // 2) % 2, :, pl.ds((i % 2) * 1024, DE)]
+
+    vocab = table_ref.shape[0]
+    sizes = [min(512, vocab - at) for at in range(0, vocab, 512)]
+    table_in = [
+        pltpu.make_async_copy(
+            table_ref.at[pl.ds(i * 512, size)], area(i).at[pl.ds(0, size)], local_sems.at[5 + i]
+        )
+        for i, size in enumerate(sizes)
     ]
     spans_in = [
         pltpu.make_async_copy(
@@ -195,12 +213,12 @@
         for i in range(4)
     ]
     alt_in = pltpu.make_async_copy(alt_ref, eq_ref, local_sems.at[4])
-    for copy in spans_in:
+    for copy in table_in:
         copy.start()
     alt_in.start()
 
     barrier = pltpu.get_barrier_semaphore()
-    friends = [in_span(k) for k in range(1, 16)] + [peer] + others
+    friends = [in_span(k) for k in range(15)] + [peer] + others
     for friend in friends:
         pl.semaphore_signal(barrier, inc=1, device_id=friend, device_id_type=pl.DeviceIdType.MESH)
     pl.semaphore_wait(barrier, len(friends))
@@ -223,50 +241,94 @@
             total = total + part.astype(F32)
         return total
 
-    embs = [
-        send(sent_ref.at[lax.rem(span + k, 16)], got_ref.at[span], emb_sems.at[k], in_span(k))
-        for k in range(1, 16)
-    ]
     def mod(v):
         return lax.rem(v + 4, 4)
 
-    def wide_at(r, group, piece, count):
+    ranks = ((z, y), (y, z))
+
+    def at(kind, r, group, piece, count):
         n = core * 2 + r
-        return wb_ref.at[
-            pl.ds(pl.multiple_of(n * 224, 224), 224),
-            pl.ds(pl.multiple_of(group * 512 + piece * 128, 128), count * 128),
-        ]
-
-    def small_at(r, group, piece, count):
-        n = core * 2 + r
+        if kind:
+            return wb_ref.at[
+                pl.ds(pl.multiple_of(n * 224, 224), 224),
+                pl.ds(pl.multiple_of(group * 512 + piece * 128, 128), count * 128),
+            ]
         return sb_ref.at[pl.ds(group * 4 + piece, count), pl.ds(pl.multiple_of(n * 112, 112), 112)]
 
-    def share(r, sem, device, wide, small):
-        return [
-            send(wide, wide, weight_sems.at[r, sem], device),
-            send(small, small, weight_sems.at[r, sem + 1], device),
-        ]
-
-    ranks = ((z, y), (y, z))
-    weights = []
-    for r in range(2):
-        n = core * 2 + r
-        p, s = ranks[r]
-        weights.append(
-            [
-                send(
-                    wd_ref.at[
-                        pl.ds(pl.multiple_of(n * 224, 224), 224),
-                        pl.ds(pl.multiple_of(s * 512 + p * 128, 128), 128),
-                    ],
-                    wide_at(r, s, p, 1),
-                    weight_sems.at[r, 0],
-                    others[2],
-                ),
-                send(wqo_ref.at[pl.ds(r, 1)], small_at(r, s, p, 1), weight_sems.at[r, 1], others[2]),
+    def weight_steps(kind):
+        sems = weight_sems.at[kind]
+        copies = []
+        for r in range(2):
+            s = ranks[r][1]
+            n = core * 2 + r
+            if kind:
+                src = wd_ref.at[
+                    pl.ds(pl.multiple_of(n * 224, 224), 224), pl.ds(pl.multiple_of(s * 512, 512), 512)
+                ]
+            else:
+                src = wqo_ref.at[r]
+            copies.append([send(src, at(kind, r, s, 0, 4), sems.at[r, 0], others[2])])
+        yield
+        for r in range(2):
+            s = ranks[r][1]
+            for copy in copies[r]:
+                copy.wait()
+            whole = at(kind, r, s, 0, 4)
+            copies[r] = [
+                send(whole, whole, sems.at[r, 1 + i], along(1 - r, by)) for i, by in enumerate((1, -1))
             ]
-        )
+        yield
+        for r in range(2):
+            s = ranks[r][1]
+            for copy in copies[r]:
+                copy.wait()
+            copies[r] = []
+            for i, by in enumerate((1, -1)):
+                part = at(kind, r, mod(s - by), 2 * i, 2)
+                copies[r].append(send(part, part, sems.at[r, 3 + i], along(1 - r, by)))
+        yield
+        for r in range(2):
+            for copy in copies[r]:
+                copy.wait()
+            n = core * 2 + r
+            if kind:
+                mine = wb_ref.at[pl.ds(pl.multiple_of(n * 224, 224), 224)]
+            else:
+                mine = sb_ref.at[:, pl.ds(pl.multiple_of(n * 112, 112), 112)]
+            copies[r] = [send(mine, mine, sems.at[r, 5], peer)]
+        yield
+        for r in range(2):
+            for copy in copies[r]:
+                copy.wait()
+        yield
+
+    small_steps, wide_steps = weight_steps(0), weight_steps(1)
+    next(small_steps)
+    next(wide_steps)
+
+    rank = lax.broadcasted_iota(jnp.int32, (1, 512), 1)
+    for i, size in enumerate(sizes):
+        table_in[i].wait()
+        chosen = (list_ref[...] == rank + i * 512).astype(F32).astype(BF16)
+        part = dot(chosen[:, :size], area(i)[:size, :])
+        if i == 0:
+            sum_ref[...], picked_ref[...] = part[:TOK], part[TOK:]
+        else:
+            sum_ref[...] += part[:TOK]
+            picked_ref[...] += part[TOK:]
+        if i == 4:
+            next(small_steps)
+    picked = jnp.concatenate([sum_ref[...], picked_ref[...]], axis=0)
+    sent_ref[...] = picked.astype(BF16).reshape(16, ROOM, DE)
+    for copy in spans_in:
+        copy.start()
+    embs = [
+        send(sent_ref.at[span_at(k)], got_ref.at[span], emb_sems.at[k], in_span(k))
+        for k in range(15)
+    ]
     got_ref[span] = sent_ref[span]
+    next(small_steps)
+    next(wide_steps)
 
     for copy in spans_in:
         copy.wait()
@@ -286,69 +348,8 @@
     q_swap = send(q_ref.at[1 - half], qo_ref, swap_sems.at[1], partner)
     og_swap = send(og_ref.at[1 - half], ogo_ref, swap_sems.at[2], partner)
 
-    def settle(r):
-        for copy in weights[r]:
-            copy.wait()
-
-    for r in range(2):
-        settle(r)
-        p, s = ranks[r]
-        weights[r] = []
-        for i, by in enumerate((1, -1)):
-            weights[r] += share(r, 2 + 2 * i, along(r, by), wide_at(r, s, p, 1), small_at(r, s, p, 1))
-    for r in range(2):
-        settle(r)
-        p, s = ranks[r]
-        weights[r] = []
-        for i, by in enumerate((1, -1)):
-            f = mod(p - by)
-            wide, small = wide_at(r, s, f, 1), small_at(r, s, f, 1)
-            weights[r] += share(
-                r,
-                6 + 2 * i,
-                along(r, by),
-                wide.at[pl.ds(112 * i, 112)],
-                small.at[:, pl.ds(48 * i, 48 + 16 * i)],
-            )
-    for r in range(2):
-        settle(r)
-        p, s = ranks[r]
-        weights[r] = []
-        for i, by in enumerate((1, -1)):
-            weights[r] += share(r, 10 + 2 * i, along(1 - r, by), wide_at(r, s, 0, 4), small_at(r, s, 0, 4))
-
-    for copy in embs:
-        copy.wait()
-    alt_in.wait()
-    slot_of = lax.broadcasted_iota(jnp.int32, (1, 16 * ROOM), 1)
-    pick = (pos_ref[...] == slot_of).astype(F32).astype(BF16)
-    over = slot_ref[2, 0] > 0
-    for lane_at, size in TILES:
-        cols = slice(lane_at, lane_at + size)
-        rows = jnp.concatenate([got_ref[i, :, cols] for i in range(16)], axis=0)
-        emb_ref[:, cols] = jnp.where(over, eq_ref[:, cols].astype(F32), dot(pick, rows)).astype(BF16)
-
-    for r in range(2):
-        settle(r)
-        p, s = ranks[r]
-        weights[r] = []
-        for i, by in enumerate((1, -1)):
-            f = mod(s - by)
-            weights[r] += share(r, 14 + 2 * i, along(1 - r, by), wide_at(r, f, 2 * i, 2), small_at(r, f, 2 * i, 2))
-    for r in range(2):
-        settle(r)
-        n = core * 2 + r
-        weights[r] = share(
-            r,
-            18,
-            peer,
-            wb_ref.at[pl.ds(pl.multiple_of(n * 224, 224), 224)],
-            sb_ref.at[:, pl.ds(pl.multiple_of(n * 112, 112), 112)],
-        )
-    kv_swap.wait()
-    kv_ref[...] = add(kvp_ref[half], kvg_ref[...]).astype(BF16)
-    for r in range(2):
-        settle(r)
+    next(small_steps)
+    next(small_steps)
 
     place = lax.broadcasted_iota(jnp.int32, (HALF, 256), 0)
     wide = lax.broadcasted_iota(jnp.int32, (512, 256), 0)
@@ -364,12 +365,32 @@
             wq_ref[rows, lane_at : lane_at + size] = (dot(wq_own_ref[rows, :], mine) + dot(other, his)).astype(BF16)
     wo_ref[pl.ds(pl.multiple_of(half * HALF, HALF), HALF), :] = wo_own_ref[...]
     for i in range(7):
-        wo_ref[pl.ds(pl.multiple_of((1 - half) * HALF, HALF), HALF), i * 128 : (i + 1) * 128] = sb_ref[8 + i]
-
+        wo_ref[pl.ds(pl.multiple_of((1 - half) * HALF, HALF), HALF), i * 128 : (i + 1) * 128] = sb_ref[8 + i if i < 4 else 9 + i]
+
+    for copy in embs:
+        copy.wait()
+    alt_in.wait()
+    slot_of = lax.broadcasted_iota(jnp.int32, (1, 16 * ROOM), 1)
+    pick = (pos_ref[...] == slot_of).astype(F32).astype(BF16)
+    over = slot_ref[2, 0] > 0
+    for lane_at, size in TILES:
+        cols = slice(lane_at, lane_at + size)
+        rows = jnp.concatenate([got_ref[i, :, cols] for i in range(16)], axis=0)
+        emb_ref[:, cols] = jnp.where(over, eq_ref[:, cols].astype(F32), dot(pick, rows)).astype(BF16)
+
+    next(wide_steps)
     lane = lax.broadcasted_iota(jnp.int32, (1, PAIR), 1)
     is_low = lane < EHD
     low = is_low.astype(F32).astype(BF16)
     high = (lane >= EHD).astype(F32).astype(BF16)
+
+    def pad(to_ref, ref, order):
+        for lane_at in range(0, PADDED, 256):
+            spread = (
+                lax.broadcasted_iota(jnp.int32, (DE, 256), 0)
+                == rows_ref[order : order + 1, lane_at : lane_at + 256]
+            )
+            to_ref[:, lane_at : lane_at + 256] = dot(ref[...], spread.astype(F32).astype(BF16)).astype(BF16)
 
     for lane_at, size in TILES:
         cols = slice(lane_at, lane_at + size)
@@ -391,7 +412,10 @@
             att_ref[rows, cols] = dot(p.astype(BF16), vbd).astype(BF16)
         return 0
 
+    kv_swap.wait()
+    kv_ref[...] = add(kvp_ref[half], kvg_ref[...]).astype(BF16)
     lax.fori_loop(0, PAIRS, forward, 0)
+    next(wide_steps)
 
     feature = lax.broadcasted_iota(jnp.int32, (DE, HALF), 0)
     column = lax.broadcasted_iota(jnp.int32, (DE, HALF), 1)
@@ -400,32 +424,39 @@
         chosen = (feature == column + which * HALF).astype(F32).astype(BF16)
         return dot(att_ref[...], chosen).astype(BF16)
 
-    own_ref[...] = half_of(1 - half).reshape(4, R, HALF)
-    att_swap = send(own_ref, all_ref.at[half], swap_sems.at[3], partner)
+    slots_ref[0:4] = half_of(1 - half).reshape(4, R, HALF)
+    att_swap = send(slots_ref.at[pl.ds(0, 4)], all_ref.at[half], swap_sems.at[3], partner)
     all_ref[half] = half_of(half).reshape(4, R, HALF)
 
     for lane_at, size in TILES:
         cols = slice(lane_at, lane_at + size)
         enc_ref[:, cols] = (emb_ref[:, cols].astype(F32) + dot(att_ref[...], wo_ref[:, cols])).astype(BF16)
 
-    def project(i, _):
+    def project_own(i, _):
         cols = pl.ds(pl.multiple_of(i * 256, 256), 256)
         dkv_ref[0, :, cols] = dot(enc_ref[...], wd_ref[:, cols]).astype(BF16)
+        return 0
+
+    def project_other(i, _):
+        cols = pl.ds(pl.multiple_of(i * 256, 256), 256)
         dkv_ref[1, :, cols] = dot(enc_ref[...], wb_ref[:, cols]).astype(BF16)
         return 0
 
-    lax.fori_loop(0, DEC // 256, project, 0)
+    lax.fori_loop(0, DEC // 256, project_own, 0)
+    pad(pad_emb_ref, emb_ref, 0)
 
     att_swap.wait()
     for e in range(16):
         unit, there = slot_ref[0, e], slot_ref[1, e]
         slots_ref[e] = all_ref[unit // 4, unit % 4] * there.astype(F32).astype(BF16)
     waiting = [
-        send(slots_ref.at[lax.rem(span + k, 16)], att_out.at[span], slot_sems.at[k], in_span(k))
-        for k in range(1, 16)
+        send(slots_ref.at[span_at(k)], att_out.at[span], slot_sems.at[k], in_span(k))
+        for k in range(15)
     ]
     stay = pltpu.make_async_copy(slots_ref.at[span], att_out.at[span], local_sems.at[0])
     stay.start()
+    next(wide_steps)
+    lax.fori_loop(0, DEC // 256, project_other, 0)
     q_swap.wait()
     og_swap.wait()
     scale = 1.0 / math.sqrt(HD)
@@ -475,59 +506,56 @@
         copies[0].wait()
         for i in range(4):
             acc1_ref[k, i] = add(g_ref[k, core, i], core_ref[k, i]).astype(BF16)
-        levels = ((acc1_ref, first1_ref, first2_ref, acc2_ref, 2, 1), (acc2_ref, second1_ref, second2_ref, acc3_ref, 1, 5))
-        for level, (acc, got1, got2, out, cut, sem) in enumerate(levels):
-            axis = k if level == 0 else 1 - k
-            p = where[axis]
-            far, up, down = mod(p + 2), mod(p + 1), mod(p - 1)
-            one, two = pl.ds(0, cut), pl.ds(cut, cut)
-            copies = [
-                send(acc.at[k, far, one], got1.at[k, 0], sems.at[sem], along(axis, 1)),
-                send(acc.at[k, far, two], got1.at[k, 1], sems.at[sem + 1], along(axis, -1)),
-            ]
-            yield
-            for copy in copies:
-                copy.wait()
-            acc[k, up, one] = add(acc[k, up, one], got1[k, 0]).astype(BF16)
-            acc[k, down, two] = add(acc[k, down, two], got1[k, 1]).astype(BF16)
-            copies = [
-                send(acc.at[k, up], got2.at[k, 0], sems.at[sem + 2], along(axis, 1)),
-                send(acc.at[k, down], got2.at[k, 1], sems.at[sem + 3], along(axis, -1)),
-            ]
-            yield
-            for copy in copies:
-                copy.wait()
-            out[k] = add(acc[k, p], got2[k, 0], got2[k, 1]).astype(BF16)
+        p, q = where[k], where[1 - k]
+        far, up, down = mod(p + 2), mod(p + 1), mod(p - 1)
+        one, two = pl.ds(0, 2), pl.ds(2, 2)
+        copies = [
+            send(acc1_ref.at[k, far, one], first1_ref.at[k, 0], sems.at[1], along(k, 1)),
+            send(acc1_ref.at[k, far, two], first1_ref.at[k, 1], sems.at[2], along(k, -1)),
+        ]
+        yield
+        for copy in copies:
+            copy.wait()
+        acc1_ref[k, up, one] = add(acc1_ref[k, up, one], first1_ref[k, 0]).astype(BF16)
+        acc1_ref[k, down, two] = add(acc1_ref[k, down, two], first1_ref[k, 1]).astype(BF16)
+        copies = [
+            send(acc1_ref.at[k, up], first2_ref.at[k, 0], sems.at[3], along(k, 1)),
+            send(acc1_ref.at[k, down], first2_ref.at[k, 1], sems.at[4], along(k, -1)),
+        ]
+        yield
+        for copy in copies:
+            copy.wait()
+        acc2_ref[k] = add(acc1_ref[k, p], first2_ref[k, 0], first2_ref[k, 1]).astype(BF16)
+        copies = [
+            send(acc2_ref.at[k, mod(q + j)], second_ref.at[k, j - 1], sems.at[4 + j], along(1 - k, j))
+            for j in range(1, 4)
+        ]
+        yield
+        for copy in copies:
+            copy.wait()
+        acc3_ref[k] = add(acc2_ref[k, q], second_ref[k, 0], second_ref[k, 1], second_ref[k, 2]).astype(BF16)
         copies = []
         for n, other in enumerate(others):
             to_low = x_low if n == 1 else 1 - x_low
-            copies.append(send(acc3_ref.at[k, to_low], last_ref.at[k, n], sems.at[9 + n], other))
+            copies.append(send(acc3_ref.at[k, to_low], last_ref.at[k, n], sems.at[8 + n], other))
         yield
         for copy in copies:
             copy.wait()
         (rq_ref, ro_ref)[k][...] = add(acc3_ref[k, x_low], last_ref[k, 0], last_ref[k, 1], last_ref[k, 2])
         yield
 
-    def pad(ref, order):
-        for lane_at in range(0, PADDED, 256):
-            spread = (
-                lax.broadcasted_iota(jnp.int32, (DE, 256), 0)
-                == rows_ref[order : order + 1, lane_at : lane_at + 256]
-            )
-            pad_ref[:, lane_at : lane_at + 256] = dot(ref[...], spread.astype(F32).astype(BF16)).astype(BF16)
-
-    def outer(k, ref):
+    def outer(k, padded_ref, ref):
         def tile(i, _):
             cols = pl.ds(pl.multiple_of(i * 256, 256), 256)
             g_ref[k, i // 2, pl.ds((i % 2) * 2, 2)] = (
-                dot_tn(pad_ref[:, cols], ref[...]).astype(BF16).reshape(2, 4, 2, 16, DE)
+                dot_tn(padded_ref[:, cols], ref[...]).astype(BF16).reshape(2, 4, 2, 16, DE)
             )
             return 0
 
         lax.fori_loop(0, PADDED // 256, tile, 0)
 
-    pad(enc_ref, 1)
-    outer(1, att_ref)
+    pad(pad_ref, enc_ref, 1)
+    outer(1, pad_ref, att_ref)
     out_sum = steps(1)
     next(out_sum)
     for lane_at, size in TILES:
@@ -551,11 +579,10 @@
 
     lax.fori_loop(0, PAIRS, backward, 0)
     next(out_sum)
-    pad(emb_ref, 0)
     next(out_sum)
-    outer(0, eq_ref)
+    outer(0, pad_emb_ref, eq_ref)
     query_sum = steps(0)
-    for _ in range(7):
+    for _ in range(6):
         next(query_sum)
         next(out_sum, None)
     for copy in waiting:
@@ -564,7 +591,7 @@
     stay.wait()
 
 
-def run(slot, pos, alt, sent, states, w_span, q, og, w_q, w_o, w_d, wqo):
+def run(slot, pos, alt, rows, table, states, w_span, q, og, w_q, w_o, w_d, wqo):
     vmem = pl.BlockSpec(memory_space=pltpu.VMEM)
     anywhere = pl.BlockSpec(memory_space=pl.ANY)
     dma = pltpu.SemaphoreType.DMA
@@ -576,10 +603,12 @@
             jax.ShapeDtypeStruct((16, DE), F32),
             jax.ShapeDtypeStruct((16, DE), F32),
         ),
-        in_specs=[pl.BlockSpec(memory_space=pltpu.SMEM), vmem, vmem, anywhere, vmem, vmem, anywhere]
+        in_specs=[pl.BlockSpec(memory_space=pltpu.SMEM), vmem, vmem, anywhere, vmem, anywhere, vmem, anywhere]
         + [vmem] * 6,
         out_specs=(anywhere, anywhere, vmem, vmem),
         scratch_shapes=[
+            pltpu.VMEM((16 * ROOM - TOK, DE), F32),
+            pltpu.VMEM((16, ROOM, DE), BF16),
             pltpu.VMEM((16, ROOM, DE), BF16),
             pltpu.VMEM((TOK, DE), BF16),
             pltpu.VMEM((2, SPANS * CH, 2 * DE), BF16),
@@ -599,7 +628,7 @@
             pltpu.VMEM((2, TOK, DEC), BF16),
             pltpu.VMEM((TOK, DE), F32),
             pltpu.VMEM((TOK, PADDED), BF16),
-            pltpu.VMEM((4, R, HALF), BF16),
+            pltpu.VMEM((TOK, PADDED), BF16),
             pltpu.VMEM((2, SPANS * CH, DEC // 2), BF16),
             pltpu.VMEM((2, 4, R, HALF), BF16),
             pltpu.VMEM((16, R, HALF), BF16),
@@ -609,16 +638,15 @@
             pltpu.VMEM((2, 2, 2, 2, 16, DE), BF16),
             pltpu.VMEM((2, 2, 4, 2, 16, DE), BF16),
             pltpu.VMEM((2, 4, 2, 16, DE), BF16),
-            pltpu.VMEM((2, 2, 1, 16, DE), BF16),
-            pltpu.VMEM((2, 2, 2, 16, DE), BF16),
+            pltpu.VMEM((2, 3, 2, 16, DE), BF16),
             pltpu.VMEM((2, 2, 16, DE), BF16),
             pltpu.VMEM((2, 3, 16, DE), BF16),
-            dma((16, 2)),
+            dma((15, 2)),
             dma((5, 2)),
-            dma((2, 20, 2)),
-            dma((16, 2)),
-            dma((2, 12, 2)),
-            dma((5,)),
+            dma((2, 2, 6, 2)),
+            dma((15, 2)),
+            dma((2, 11, 2)),
+            dma((13,)),
         ],
         compiler_params=pltpu.CompilerParams(
             vmem_limit_bytes=63 * 2**20, collective_id=1, has_side_effects=True
@@ -626,7 +654,7 @@
         cost_estimate=pl.CostEstimate(
             flops=16 * 10**9, bytes_accessed=30 * 2**20, transcendentals=10**6
         ),
-    )(slot, jnp.asarray(piece_rows()), pos, alt, sent, states, w_span, q, og, w_q, w_o, w_d, wqo)
+    )(slot, jnp.asarray(piece_rows()), pos, alt, rows, table, states, w_span, q, og, w_q, w_o, w_d, wqo)
 
 
 def body(
@@ -656,7 +684,6 @@
         neighbour_ids.reshape(seq_count, n_span, tokens), half_index, 0, keepdims=False
     )
     rows, pos, over = lists(ids_m, span_index, vocab_rows, n_span)
-    sent = jnp.take(embed_table, rows.reshape(-1), axis=0).reshape(n_span, ROOM, DE)
 
     def whole_gather():
         shifted = ids_m.reshape(-1) - span_index * vocab_rows
@@ -673,16 +700,13 @@
     core = lax.axis_index("dp") % 2
     wqo = []
     for r in range(2):
-        piece = (span_index % 4) * 4 + span_index // 4 if r == 0 else span_index
+        group = span_index % 4 if r == 0 else span_index // 4
         start = (core * 2 + r) * 112
-        from_q = lax.dynamic_slice(
-            w_query_enc,
-            ((piece // 4) * HALF + start, jnp.minimum((piece % 4) * 128, HALF - 128)),
-            (112, 128),
-        )
-        from_o = lax.dynamic_slice(w_out_enc, (start, (piece - 8) * 128), (112, 128))
-        wqo.append(jnp.where(piece < 8, from_q, from_o))
-    wqo = jnp.stack(wqo)
+        from_q = lax.dynamic_slice(w_query_enc, (group * HALF + start, 0), (112, HALF))
+        from_o = lax.dynamic_slice(w_out_enc, (start, (group - 2) * 512), (112, 512))
+        from_q = jnp.concatenate([from_q[:, :384], from_q[:, HALF - 128 :]], axis=1)
+        wqo.append(jnp.where(group < 2, from_q, from_o))
+    wqo = jnp.transpose(jnp.stack(wqo).reshape(2, 112, 4, 128), (0, 2, 1, 3))
 
     dest = lax.dynamic_index_in_dim(assignment[0, :, :, 0], span_index, 0, keepdims=False)
     at = dest[None, :] == jnp.arange(n_span, dtype=jnp.int32)[:, None]
@@ -698,7 +722,8 @@
         slot,
         pos[:, None],
         alt,
-        sent,
+        rows.reshape(-1, 1),
+        embed_table,
         span_states.reshape(-1, half_width),
         w_span_kv,
         queries,

time: 193 us -> 168 us (0.87)
  Pallas kernels: 157 us -> 139 us
  local copies, waits for them, and re-layouts: 22.9 us -> 17.1 us
    pallas_call x1, Pallas kernels: 157 us -> 139 us  [run(): pl.pallas_call(mega, out_shape=(jax.ShapeDtypeStruct((16, R, HALF), BF16)...]
    gather x1 -> x0, local copies, waits for them, and re-layouts: 7.47 us -> none  [body(): jnp.take(embed_table, rows.reshape(-1), axis=0).reshape(n_span, ROOM, DE)]
    unnamed x18 -> x14, local copies, waits for them, and re-layouts: 12 us -> 12.6 us
where the time goes in v4:
time: 168 us
  Pallas kernels  139 us (83%)
  local copies, waits for them, and re-layouts  17.1 us (10%)
  other arithmetic  9.93 us (6%)
    pallas_call x1, Pallas kernels, run(): pl.pallas_call(mega, out_shape=(jax.ShapeDtypeStruct((16, R, HALF), BF16)...  139 us
    unnamed x14, local copies, waits for them, and re-layouts  12.6 us
    reduce_or x1, other arithmetic, lists(): dup = jnp.any(same & (t[None, None, :] < t[None, :, None]), axis=2)  4.28 us

profile of v4, /device:TPU:0, one launch (start us, length us, event | category | flops | bytes accessed | tf_op | source)
XLA Modules:
  0.0 168.0 jit_solution(16665526382942969912)
XLA Ops:
  0.6 0.0 copy-start
  0.7 0.7 copy-done
  1.3 0.3 dynamic-slice_reduce_fusion
  1.6 0.1 select_reduce_fusion.2
  1.7 0.9 reshape.237
  2.6 0.1 iota_compare_fusion.3
  2.7 4.3 %and_reduce_fusion = pred[16,512]{1,0:T(8,128)(4,1)S(1)} fusion(s32[16,512]{1,0:T(8,128)S(1)} %get-tuple-element.45, pred[512,512]{1,0:T(8,128)(4,1)S(1)} %iota_compare_fusion.3), kind=kLoop, calls=%fused_computation.8 | loop fusion | flops 12574720 | bytes 303104 | tf_op jit(solution)/shard_map/reduce_or | solution.py:24
  7.1 0.4 convert_reduce_fusion.1
  7.4 0.6 reduce_max.9
  8.7 0.1 pad.8.clone
  8.8 0.7 add_add_fusion.slot_ref
  9.5 0.3 select_reduce_fusion.1
  9.8 0.5 convert_reduce_fusion
  10.3 0.2 copy.45
  10.5 0.2 copy.42
  10.7 0.1 copy.41
  10.8 0.8 fusion.4.pos_ref
  11.6 0.0 copy-start.4
  11.6 0.1 conditional.1
  11.6 0.1 broadcast.237
  11.7 0.0 copy-start.3
  11.7 0.2 convolution_convert_fusion
  11.9 0.5 select_reduce_fusion
  12.3 0.9 reshape.250.list_ref
  13.2 0.0 copy-done.3
  13.2 0.0 copy-done.4
  13.2 0.7 copy.51.wq_own_ref
  14.0 0.0 copy-start.2
  14.0 5.4 %copy.55 = bf16[112,8,2,1024]{3,1,2,0:T(8,128)(2,1)} copy(bf16[112,8,2,1024]{3,2,1,0:T(2,128)(2,1)} %bitcast.31) | data formatting | bytes 7340032
  19.4 0.1 fusion.7
  19.6 1.0 maximum_select_fusion
  20.7 0.7 maximum_bitcast_fusion.wqo_ref
  21.4 0.0 copy-done.2
  21.4 0.0 copy-start.1
  21.4 139.3 %shard_map.138 = (bf16[16,128,448]{2,1,0:T(8,128)(2,1)}, bf16[2,128,1024]{2,1,0:T(8,128)(2,1)}, f32[16,896]{1,0:T(8,128)}, f32[16,896]{1,0:T(8,128)}) custom-call(s32[3,16]{1,0:T(4,128)} %add_add_fusion.slot_ref, s32[2,1024]{1,0:T(2,128)} %constant.144.clone.rows_ref, s32[512,1]{1,0:T(8,128)} %fusion.4.pos_ref, bf16[512,896]{1,0:T(8,128)(2,1)} %copy-done.3, ...), custom_call_target="tpu_custom_call" | custom-call | flops 16000000000 | bytes 31457280 | tf_op jit(solution)/shard_map/pallas_call | solution.py:598
  160.7 3.9 %copy.52 = bf16[1,1,16,1,128,448]{4,5,3,2,1,0:T(8,128)(2,1)} copy(bf16[1,1,16,1,128,448]{5,4,2,3,1,0:T(8,128)(2,1)} %bitcast.33) | data formatting | bytes 3670016
  164.6 1.5 dynamic-slice_bitcast_fusion
  166.1 1.9 %copy.59 = bf16[2,128,1024]{2,1,0:T(8,128)(2,1)} copy(bf16[2,128,1024]{2,1,0:T(8,128)(2,1)} %get-tuple-element.63) | data formatting | bytes 1048576
  168.0 0.0 copy-done.1
  (11 shorter events, 0.2 us)
Async XLA Ops:
  0.6 0.7 copy-start
  11.6 1.7 copy-start.4
  11.7 1.6 copy-start.3
  14.0 7.5 %copy-start.2 = (bf16[896,448]{1,0:T(8,128)(2,1)}, bf16[896,448]{1,0:T(8,128)(2,1)S(1)}, u32[]{:S(2)}) copy-start(bf16[896,448]{1,0:T(8,128)(2,1)S(1)} %copy.51.wq_own_ref) | copy-start | bytes 2408452
  21.4 146.5 %copy-start.1 = (s32[1,16,8,1]{1,3,2,0:T(1,128)S(1)}, s32[1,16,8,1]{1,3,2,0:T(1,128)}, u32[]{:S(2)}) copy-start(s32[1,16,8,1]{1,3,2,0:T(1,128)} %param.17) | copy-start | bytes 1540

commit v5 on v4

--- a/solution.py
+++ b/solution.py
@@ -156,8 +156,7 @@
     g_ref,
     core_ref,
     acc1_ref,
-    first1_ref,
-    first2_ref,
+    first_ref,
     acc2_ref,
     second_ref,
     acc3_ref,
@@ -499,64 +498,74 @@
     lax.fori_loop(0, DEC // 256, collect, 0)
     enc_ref[...] = sum_ref[...].astype(BF16)
 
-    def steps(k):
-        sems = sum_sems.at[k]
-        copies = [send(g_ref.at[k, 1 - core], core_ref.at[k], sems.at[0], peer)]
+    def steps(job):
+        k, lanes = ((0, slice(0, 512)), (0, slice(512, DE)), (1, slice(0, DE)))[job]
+        wide = pl.ds(lanes.start, lanes.stop - lanes.start)
+        axis = (0, 1, 1)[job]
+        flip = job == 1
+        p, q = where[axis], where[1 - axis]
+        sems = sum_sems.at[job]
+        copies = [
+            send(g_ref.at[k, 1 - core, :, :, :, :, wide], core_ref.at[k, :, :, :, :, wide], sems.at[0], peer)
+        ]
         yield
         copies[0].wait()
         for i in range(4):
-            acc1_ref[k, i] = add(g_ref[k, core, i], core_ref[k, i]).astype(BF16)
-        p, q = where[k], where[1 - k]
-        far, up, down = mod(p + 2), mod(p + 1), mod(p - 1)
-        one, two = pl.ds(0, 2), pl.ds(2, 2)
-        copies = [
-            send(acc1_ref.at[k, far, one], first1_ref.at[k, 0], sems.at[1], along(k, 1)),
-            send(acc1_ref.at[k, far, two], first1_ref.at[k, 1], sems.at[2], along(k, -1)),
-        ]
+            acc1_ref[k, i, :, :, :, lanes] = add(
+                g_ref[k, core, i, :, :, :, lanes], core_ref[k, i, :, :, :, lanes]
+            ).astype(BF16)
+        copies = []
+        for j in range(1, 4):
+            to = mod(p + j)
+            block = acc1_ref.at[k, :, to, :, :, wide] if flip else acc1_ref.at[k, to, :, :, :, wide]
+            copies.append(send(block, first_ref.at[k, j - 1, :, :, :, wide], sems.at[j], along(axis, j)))
         yield
         for copy in copies:
             copy.wait()
-        acc1_ref[k, up, one] = add(acc1_ref[k, up, one], first1_ref[k, 0]).astype(BF16)
-        acc1_ref[k, down, two] = add(acc1_ref[k, down, two], first1_ref[k, 1]).astype(BF16)
+        own = acc1_ref[k, :, p, :, :, lanes] if flip else acc1_ref[k, p, :, :, :, lanes]
+        acc2_ref[k, :, :, :, lanes] = add(own, *[first_ref[k, j, :, :, :, lanes] for j in range(3)]).astype(BF16)
         copies = [
-            send(acc1_ref.at[k, up], first2_ref.at[k, 0], sems.at[3], along(k, 1)),
-            send(acc1_ref.at[k, down], first2_ref.at[k, 1], sems.at[4], along(k, -1)),
+            send(
+                acc2_ref.at[k, mod(q + j), :, :, wide],
+                second_ref.at[k, j - 1, :, :, wide],
+                sems.at[3 + j],
+                along(1 - axis, j),
+            )
+            for j in range(1, 4)
         ]
         yield
         for copy in copies:
             copy.wait()
-        acc2_ref[k] = add(acc1_ref[k, p], first2_ref[k, 0], first2_ref[k, 1]).astype(BF16)
-        copies = [
-            send(acc2_ref.at[k, mod(q + j)], second_ref.at[k, j - 1], sems.at[4 + j], along(1 - k, j))
-            for j in range(1, 4)
-        ]
-        yield
-        for copy in copies:
-            copy.wait()
-        acc3_ref[k] = add(acc2_ref[k, q], second_ref[k, 0], second_ref[k, 1], second_ref[k, 2]).astype(BF16)
+        acc3_ref[k, :, :, lanes] = add(
+            acc2_ref[k, q, :, :, lanes], *[second_ref[k, j, :, :, lanes] for j in range(3)]
+        ).astype(BF16)
         copies = []
         for n, other in enumerate(others):
             to_low = x_low if n == 1 else 1 - x_low
-            copies.append(send(acc3_ref.at[k, to_low], last_ref.at[k, n], sems.at[8 + n], other))
+            copies.append(
+                send(acc3_ref.at[k, to_low, :, wide], last_ref.at[k, n, :, wide], sems.at[7 + n], other)
+            )
         yield
         for copy in copies:
             copy.wait()
-        (rq_ref, ro_ref)[k][...] = add(acc3_ref[k, x_low], last_ref[k, 0], last_ref[k, 1], last_ref[k, 2])
-        yield
-
-    def outer(k, padded_ref, ref):
+        (rq_ref, ro_ref)[k][:, lanes] = add(
+            acc3_ref[k, x_low, :, lanes], *[last_ref[k, n, :, lanes] for n in range(3)]
+        )
+        yield
+
+    def outer(k, padded_ref, ref, lanes):
         def tile(i, _):
             cols = pl.ds(pl.multiple_of(i * 256, 256), 256)
-            g_ref[k, i // 2, pl.ds((i % 2) * 2, 2)] = (
-                dot_tn(padded_ref[:, cols], ref[...]).astype(BF16).reshape(2, 4, 2, 16, DE)
+            g_ref[k, i // 2, pl.ds((i % 2) * 2, 2), :, :, :, lanes] = (
+                dot_tn(padded_ref[:, cols], ref[:, lanes]).astype(BF16).reshape(2, 4, 2, 16, -1)
             )
             return 0
 
         lax.fori_loop(0, PADDED // 256, tile, 0)
 
     pad(pad_ref, enc_ref, 1)
-    outer(1, pad_ref, att_ref)
-    out_sum = steps(1)
+    outer(1, pad_ref, att_ref, slice(0, DE))
+    out_sum = steps(2)
     next(out_sum)
     for lane_at, size in TILES:
         cols = slice(lane_at, lane_at + size)
@@ -577,14 +586,25 @@
             eq_ref[rows, cols] = dot(ds, kbd).astype(BF16)
         return 0
 
-    lax.fori_loop(0, PAIRS, backward, 0)
+    lax.fori_loop(0, 4, backward, 0)
+    outer(0, pad_emb_ref, eq_ref, slice(0, 512))
+    low_sum = steps(0)
+    next(low_sum)
+    lax.fori_loop(4, PAIRS, backward, 0)
+    next(low_sum)
     next(out_sum)
+    outer(0, pad_emb_ref, eq_ref, slice(512, DE))
+    high_sum = steps(1)
+    next(high_sum)
+    next(high_sum)
+    next(low_sum)
     next(out_sum)
-    outer(0, pad_emb_ref, eq_ref)
-    query_sum = steps(0)
-    for _ in range(6):
-        next(query_sum)
-        next(out_sum, None)
+    next(high_sum)
+    next(low_sum)
+    next(out_sum)
+    next(high_sum)
+    next(low_sum)
+    next(high_sum)
     for copy in waiting:
         copy.wait()
     mine.wait()
@@ -635,8 +655,7 @@
             pltpu.VMEM((2, 2, 4, 4, 2, 16, DE), BF16),
             pltpu.VMEM((2, 4, 4, 2, 16, DE), BF16),
             pltpu.VMEM((2, 4, 4, 2, 16, DE), BF16),
-            pltpu.VMEM((2, 2, 2, 2, 16, DE), BF16),
-            pltpu.VMEM((2, 2, 4, 2, 16, DE), BF16),
+            pltpu.VMEM((2, 3, 4, 2, 16, DE), BF16),
             pltpu.VMEM((2, 4, 2, 16, DE), BF16),
             pltpu.VMEM((2, 3, 2, 16, DE), BF16),
             pltpu.VMEM((2, 2, 16, DE), BF16),
@@ -645,7 +664,7 @@
             dma((5, 2)),
             dma((2, 2, 6, 2)),
             dma((15, 2)),
-            dma((2, 11, 2)),
+            dma((3, 10, 2)),
             dma((13,)),
         ],
         compiler_params=pltpu.CompilerParams(
@@ -730,7 +749,7 @@
         out_grad,
         w_query_enc,
         w_out_enc,
-        w_dec_kv.reshape(DE, dec_cols),
+        jnp.concatenate([w_dec_kv[:, 0], w_dec_kv[:, 1]], axis=1),
         wqo,
     )
     grad_query_enc = lax.dynamic_slice_in_dim(rq[:PIECE], half_index * HALF, HALF, 1)

time: 168 us -> 167 us (level)
  Pallas kernels: 139 us -> 132 us
  local copies, waits for them, and re-layouts: 17.1 us -> 20.2 us
  other arithmetic: 9.93 us -> 12.1 us
    slice x0 -> x1, local copies, waits for them, and re-layouts: none -> 8.19 us  [body(): w_dec_kv[:, 0]]
    pallas_call x1, Pallas kernels: 139 us -> 132 us  [run(): pl.pallas_call(mega, out_shape=(jax.ShapeDtypeStruct((16, R, HALF), BF16)...]
    unnamed x14 -> x19, local copies, waits for them, and re-layouts: 12.6 us -> 6.2 us
    concatenate x0 -> x1, other arithmetic: none -> 2.14 us  [body(): jnp.concatenate([w_dec_kv[:, 0], w_dec_kv[:, 1]], axis=1)]
where the time goes in v5:
time: 167 us; the launch traced here: 166 us
  Pallas kernels  132 us (79%)
  local copies, waits for them, and re-layouts  20.2 us (12%)
  other arithmetic  12.1 us (7%)
    pallas_call x1, Pallas kernels, run(): pl.pallas_call(mega, out_shape=(jax.ShapeDtypeStruct((16, R, HALF), BF16)...  132 us
    slice x1, local copies, waits for them, and re-layouts, body(): w_dec_kv[:, 0]  8.19 us
    unnamed x19, local copies, waits for them, and re-layouts  6.2 us
    reduce_or x1, other arithmetic, lists(): dup = jnp.any(same & (t[None, None, :] < t[None, :, None]), axis=2)  4.28 us

profile of v5, /device:TPU:0, one launch (start us, length us, event | category | flops | bytes accessed | tf_op | source)
XLA Modules:
  0.0 166.5 jit_solution(13916800255221215303)
XLA Ops:
  0.6 0.0 copy-start
  0.7 0.7 copy-done
  1.3 0.3 dynamic-slice_reduce_fusion
  1.6 0.1 select_reduce_fusion.2
  1.7 0.9 reshape.234
  2.6 0.1 iota_compare_fusion.3
  2.7 4.3 %and_reduce_fusion = pred[16,512]{1,0:T(8,128)(4,1)S(1)} fusion(s32[16,512]{1,0:T(8,128)S(1)} %get-tuple-element.45, pred[512,512]{1,0:T(8,128)(4,1)S(1)} %iota_compare_fusion.3), kind=kLoop, calls=%fused_computation.8 | loop fusion | flops 12574720 | bytes 303104 | tf_op jit(solution)/shard_map/reduce_or | solution.py:24
  7.1 0.4 convert_reduce_fusion.1
  7.4 0.6 reduce_max.9
  8.7 0.1 pad.10.clone
  8.8 0.7 add_add_fusion.slot_ref
  9.5 0.3 select_reduce_fusion.1
  9.8 0.5 convert_reduce_fusion
  10.3 0.2 copy.51
  10.5 0.2 copy.48
  10.7 0.1 copy.47
  10.8 0.8 fusion.4.pos_ref
  11.6 0.0 copy-start.4
  11.6 0.3 conditional.1
  11.6 0.1 broadcast.237
  11.8 0.0 copy-start.3
  11.9 0.2 convolution_convert_fusion
  12.0 0.5 select_reduce_fusion
  12.5 0.9 reshape.246.list_ref
  13.4 0.0 copy-done.4
  13.4 0.7 copy.59.wq_own_ref
  14.2 0.0 copy-start.2
  14.2 8.2 %fusion.7 = (bf16[896,1,1024]{2,1,0:T(2,128)(2,1)S(1)}, bf16[896,1,1024]{2,1,0:T(2,128)(2,1)S(1)}) fusion(bf16[896,2,1024]{2,1,0:T(2,128)(2,1)} %param.22), kind=kLoop, calls=%fused_computation.55 | loop fusion | bytes 7340032 | tf_op jit(solution)/shard_map/slice | solution.py:752
  22.4 0.0 copy-done.3
  22.4 1.5 copy_bitcast_fusion
  23.9 2.1 %pad_maximum_fusion.wd_ref = bf16[896,2048]{1,0:T(8,128)(2,1)} fusion(bf16[896,1024]{1,0:T(8,128)(2,1)S(1)} %get-tuple-element.59, bf16[896,1024]{1,0:T(8,128)(2,1)S(1)} %get-tuple-element.60), kind=kLoop, calls=%fused_computation.9 | loop fusion | flops 7340032 | bytes 7340032 | tf_op jit(solution)/shard_map/concatenate | solution.py:752
  26.0 0.1 fusion.8
  26.1 0.0 copy-done.2
  26.2 1.0 maximum_select_fusion
  27.3 0.7 maximum_bitcast_fusion.wqo_ref
  28.1 0.0 copy-start.1
  28.1 132.3 %shard_map.138 = (bf16[16,128,448]{2,1,0:T(8,128)(2,1)}, bf16[2,128,1024]{2,1,0:T(8,128)(2,1)}, f32[16,896]{1,0:T(8,128)}, f32[16,896]{1,0:T(8,128)}) custom-call(s32[3,16]{1,0:T(4,128)} %add_add_fusion.slot_ref, s32[2,1024]{1,0:T(2,128)} %constant.144.clone.rows_ref, s32[512,1]{1,0:T(8,128)} %fusion.4.pos_ref, bf16[512,896]{1,0:T(8,128)(2,1)} %copy-done.3, ...), custom_call_target="tpu_custom_call" | custom-call | flops 16000000000 | bytes 31457280 | tf_op jit(solution)/shard_map/pallas_call | solution.py:618
  160.3 0.0 copy-start.7
  160.3 0.0 copy-start.6
  160.3 0.0 copy-start.5
  160.3 4.0 %copy.60 = bf16[1,1,16,1,128,448]{4,5,3,2,1,0:T(8,128)(2,1)} copy(bf16[1,1,16,1,128,448]{5,4,2,3,1,0:T(8,128)(2,1)} %bitcast.33) | data formatting | bytes 3670016
  164.3 0.0 copy-done.7
  164.3 0.7 constant_dynamic-slice_fusion
  165.0 0.0 copy-done.6
  165.0 0.7 dynamic-slice_bitcast_fusion
  165.7 0.0 copy-done.5
  165.7 0.8 copy.70
  166.5 0.0 copy-done.1
  (11 shorter events, 0.2 us)
Async XLA Ops:
  0.6 0.7 copy-start
  11.6 1.8 %copy-start.4 = (bf16[896,448]{0,1:T(8,128)(2,1)S(1)}, bf16[896,448]{0,1:T(8,128)(2,1)}, u32[]{:S(2)}) copy-start(bf16[896,448]{0,1:T(8,128)(2,1)} %param.20) | copy-start | bytes 2408452
  11.8 10.5 %copy-start.3 = (bf16[512,896]{1,0:T(8,128)(2,1)}, bf16[512,896]{1,0:T(8,128)(2,1)S(1)}, u32[]{:S(2)}) copy-start(bf16[512,896]{1,0:T(8,128)(2,1)S(1)} %get-tuple-element.69.alt_ref) | copy-start | bytes 2752516
  14.2 11.9 %copy-start.2 = (bf16[896,448]{1,0:T(8,128)(2,1)}, bf16[896,448]{1,0:T(8,128)(2,1)S(1)}, u32[]{:S(2)}) copy-start(bf16[896,448]{1,0:T(8,128)(2,1)S(1)} %copy.59.wq_own_ref) | copy-start | bytes 2408452
  28.1 138.4 %copy-start.1 = (s32[1,16,8,1]{1,3,2,0:T(1,128)S(1)}, s32[1,16,8,1]{1,3,2,0:T(1,128)}, u32[]{:S(2)}) copy-start(s32[1,16,8,1]{1,3,2,0:T(1,128)} %param.17) | copy-start | bytes 1540
  160.3 4.0 %copy-start.7 = (f32[16,896]{1,0:T(8,128)S(1)}, f32[16,896]{1,0:T(8,128)}, u32[]{:S(2)}) copy-start(f32[16,896]{1,0:T(8,128)} %get-tuple-element.22) | copy-start | bytes 172036
  160.3 4.7 %copy-start.6 = (f32[16,896]{1,0:T(8,128)S(1)}, f32[16,896]{1,0:T(8,128)}, u32[]{:S(2)}) copy-start(f32[16,896]{1,0:T(8,128)} %get-tuple-element.23) | copy-start | bytes 172036
  160.3 5.4 %copy-start.5 = (bf16[2,128,1024]{2,1,0:T(8,128)(2,1)S(1)}, bf16[2,128,1024]{2,1,0:T(8,128)(2,1)}, u32[]{:S(2)}) copy-start(bf16[2,128,1024]{2,1,0:T(8,128)(2,1)} %get-tuple-element.65) | copy-start | bytes 1572868

commit v6 on v5

--- a/solution.py
+++ b/solution.py
@@ -304,6 +304,8 @@
     small_steps, wide_steps = weight_steps(0), weight_steps(1)
     next(small_steps)
     next(wide_steps)
+    q_swap = send(q_ref.at[1 - half], qo_ref, swap_sems.at[1], partner)
+    og_swap = send(og_ref.at[1 - half], ogo_ref, swap_sems.at[2], partner)
 
     rank = lax.broadcasted_iota(jnp.int32, (1, 512), 1)
     for i, size in enumerate(sizes):
@@ -327,7 +329,6 @@
     ]
     got_ref[span] = sent_ref[span]
     next(small_steps)
-    next(wide_steps)
 
     for copy in spans_in:
         copy.wait()
@@ -344,8 +345,6 @@
 
     lax.fori_loop(0, 2 * DE // 256, project_span, 0)
     kv_swap = send(kvp_ref.at[1 - half], kvg_ref, swap_sems.at[0], partner)
-    q_swap = send(q_ref.at[1 - half], qo_ref, swap_sems.at[1], partner)
-    og_swap = send(og_ref.at[1 - half], ogo_ref, swap_sems.at[2], partner)
 
     next(small_steps)
     next(small_steps)
@@ -368,6 +367,7 @@
 
     for copy in embs:
         copy.wait()
+    next(wide_steps)
     alt_in.wait()
     slot_of = lax.broadcasted_iota(jnp.int32, (1, 16 * ROOM), 1)
     pick = (pos_ref[...] == slot_of).astype(F32).astype(BF16)
@@ -377,7 +377,6 @@
         rows = jnp.concatenate([got_ref[i, :, cols] for i in range(16)], axis=0)
         emb_ref[:, cols] = jnp.where(over, eq_ref[:, cols].astype(F32), dot(pick, rows)).astype(BF16)
 
-    next(wide_steps)
     lane = lax.broadcasted_iota(jnp.int32, (1, PAIR), 1)
     is_low = lane < EHD
     low = is_low.astype(F32).astype(BF16)
@@ -394,6 +393,7 @@
     for lane_at, size in TILES:
         cols = slice(lane_at, lane_at + size)
         eq_ref[:, cols] = dot(emb_ref[...], wq_ref[:, cols]).astype(BF16)
+    next(wide_steps)
 
     def forward(j, _):
         cols = pl.ds(pl.multiple_of(j * PAIR, PAIR), PAIR)
@@ -443,6 +443,8 @@
 
     lax.fori_loop(0, DEC // 256, project_own, 0)
     pad(pad_emb_ref, emb_ref, 0)
+    next(wide_steps)
+    lax.fori_loop(0, DEC // 256, project_other, 0)
 
     att_swap.wait()
     for e in range(16):
@@ -454,8 +456,6 @@
     ]
     stay = pltpu.make_async_copy(slots_ref.at[span], att_out.at[span], local_sems.at[0])
     stay.start()
-    next(wide_steps)
-    lax.fori_loop(0, DEC // 256, project_other, 0)
     q_swap.wait()
     og_swap.wait()
     scale = 1.0 / math.sqrt(HD)
@@ -749,7 +749,7 @@
         out_grad,
         w_query_enc,
         w_out_enc,
-        jnp.concatenate([w_dec_kv[:, 0], w_dec_kv[:, 1]], axis=1),
+        w_dec_kv.reshape(DE, dec_cols),
         wqo,
     )
     grad_query_enc = lax.dynamic_slice_in_dim(rq[:PIECE], half_index * HALF, HALF, 1)

time: 167 us -> 173 us (1.036)
  Pallas kernels: 132 us -> 144 us
  local copies, waits for them, and re-layouts: 20.2 us -> 17.1 us
  other arithmetic: 12.1 us -> 9.93 us
    pallas_call x1, Pallas kernels: 132 us -> 144 us  [run(): pl.pallas_call(mega, out_shape=(jax.ShapeDtypeStruct((16, R, HALF), BF16)...]
    slice x1 -> x0, local copies, waits for them, and re-layouts: 8.19 us -> none  [body(): w_dec_kv[:, 0]]
    unnamed x19 -> x14, local copies, waits for them, and re-layouts: 6.2 us -> 12.6 us
    concatenate x1 -> x0, other arithmetic: 2.14 us -> none  [body(): jnp.concatenate([w_dec_kv[:, 0], w_dec_kv[:, 1]], axis=1)]
where the time goes in v6:
time: 173 us; the launch traced here: 172 us
  Pallas kernels  144 us (83%)
  local copies, waits for them, and re-layouts  17.1 us (10%)
  other arithmetic  9.93 us (6%)
    pallas_call x1, Pallas kernels, run(): pl.pallas_call(mega, out_shape=(jax.ShapeDtypeStruct((16, R, HALF), BF16)...  144 us
    unnamed x14, local copies, waits for them, and re-layouts  12.6 us
    reduce_or x1, other arithmetic, lists(): dup = jnp.any(same & (t[None, None, :] < t[None, :, None]), axis=2)  4.28 us

profile of v6, /device:TPU:0, one launch (start us, length us, event | category | flops | bytes accessed | tf_op | source)
XLA Modules:
  0.0 172.3 jit_solution(187906321515233556)
XLA Ops:
  0.6 0.0 copy-start
  0.7 0.7 copy-done
  1.3 0.3 dynamic-slice_reduce_fusion
  1.6 0.1 select_reduce_fusion.2
  1.7 0.9 reshape.237
  2.6 0.1 iota_compare_fusion.3
  2.7 4.3 %and_reduce_fusion = pred[16,512]{1,0:T(8,128)(4,1)S(1)} fusion(s32[16,512]{1,0:T(8,128)S(1)} %get-tuple-element.45, pred[512,512]{1,0:T(8,128)(4,1)S(1)} %iota_compare_fusion.3), kind=kLoop, calls=%fused_computation.8 | loop fusion | flops 12574720 | bytes 303104 | tf_op jit(solution)/shard_map/reduce_or | solution.py:24
  7.1 0.4 convert_reduce_fusion.1
  7.4 0.6 reduce_max.9
  8.7 0.1 pad.8.clone
  8.8 0.7 add_add_fusion.slot_ref
  9.5 0.3 select_reduce_fusion.1
  9.8 0.5 convert_reduce_fusion
  10.3 0.2 copy.45
  10.5 0.2 copy.42
  10.7 0.1 copy.41
  10.8 0.8 fusion.4.pos_ref
  11.6 0.0 copy-start.4
  11.6 0.1 conditional.1
  11.6 0.1 broadcast.237
  11.7 0.0 copy-start.3
  11.7 0.2 convolution_convert_fusion
  11.9 0.5 select_reduce_fusion
  12.3 0.9 reshape.250.list_ref
  13.2 0.0 copy-done.3
  13.2 0.0 copy-done.4
  13.2 0.7 copy.51.wq_own_ref
  14.0 0.0 copy-start.2
  14.0 5.4 %copy.55 = bf16[112,8,2,1024]{3,1,2,0:T(8,128)(2,1)} copy(bf16[112,8,2,1024]{3,2,1,0:T(2,128)(2,1)} %bitcast.31) | data formatting | bytes 7340032
  19.4 0.1 fusion.7
  19.6 1.0 maximum_select_fusion
  20.7 0.7 maximum_bitcast_fusion.wqo_ref
  21.4 0.0 copy-done.2
  21.4 0.0 copy-start.1
  21.4 143.6 %shard_map.138 = (bf16[16,128,448]{2,1,0:T(8,128)(2,1)}, bf16[2,128,1024]{2,1,0:T(8,128)(2,1)}, f32[16,896]{1,0:T(8,128)}, f32[16,896]{1,0:T(8,128)}) custom-call(s32[3,16]{1,0:T(4,128)} %add_add_fusion.slot_ref, s32[2,1024]{1,0:T(2,128)} %constant.144.clone.rows_ref, s32[512,1]{1,0:T(8,128)} %fusion.4.pos_ref, bf16[512,896]{1,0:T(8,128)(2,1)} %copy-done.3, ...), custom_call_target="tpu_custom_call" | custom-call | flops 16000000000 | bytes 31457280 | tf_op jit(solution)/shard_map/pallas_call | solution.py:618
  165.1 3.9 %copy.52 = bf16[1,1,16,1,128,448]{4,5,3,2,1,0:T(8,128)(2,1)} copy(bf16[1,1,16,1,128,448]{5,4,2,3,1,0:T(8,128)(2,1)} %bitcast.33) | data formatting | bytes 3670016
  169.0 1.5 dynamic-slice_bitcast_fusion
  170.5 1.9 %copy.59 = bf16[2,128,1024]{2,1,0:T(8,128)(2,1)} copy(bf16[2,128,1024]{2,1,0:T(8,128)(2,1)} %get-tuple-element.63) | data formatting | bytes 1048576
  172.3 0.0 copy-done.1
  (11 shorter events, 0.2 us)
Async XLA Ops:
  0.6 0.7 copy-start
  11.6 1.7 copy-start.4
  11.7 1.6 copy-start.3
  14.0 7.5 %copy-start.2 = (bf16[896,448]{1,0:T(8,128)(2,1)}, bf16[896,448]{1,0:T(8,128)(2,1)S(1)}, u32[]{:S(2)}) copy-start(bf16[896,448]{1,0:T(8,128)(2,1)S(1)} %copy.51.wq_own_ref) | copy-start | bytes 2408452
  21.4 150.9 %copy-start.1 = (s32[1,16,8,1]{1,3,2,0:T(1,128)S(1)}, s32[1,16,8,1]{1,3,2,0:T(1,128)}, u32[]{:S(2)}) copy-start(s32[1,16,8,1]{1,3,2,0:T(1,128)} %param.17) | copy-start | bytes 1540

commit v7 on v5

--- a/solution.py
+++ b/solution.py
@@ -443,6 +443,8 @@
 
     lax.fori_loop(0, DEC // 256, project_own, 0)
     pad(pad_emb_ref, emb_ref, 0)
+    next(wide_steps)
+    lax.fori_loop(0, DEC // 256, project_other, 0)
 
     att_swap.wait()
     for e in range(16):
@@ -454,8 +456,6 @@
     ]
     stay = pltpu.make_async_copy(slots_ref.at[span], att_out.at[span], local_sems.at[0])
     stay.start()
-    next(wide_steps)
-    lax.fori_loop(0, DEC // 256, project_other, 0)
     q_swap.wait()
     og_swap.wait()
     scale = 1.0 / math.sqrt(HD)
@@ -749,7 +749,7 @@
         out_grad,
         w_query_enc,
         w_out_enc,
-        jnp.concatenate([w_dec_kv[:, 0], w_dec_kv[:, 1]], axis=1),
+        w_dec_kv.reshape(DE, dec_cols),
         wqo,
     )
     grad_query_enc = lax.dynamic_slice_in_dim(rq[:PIECE], half_index * HALF, HALF, 1)

time: 167 us -> 158 us (0.946)
  local copies, waits for them, and re-layouts: 20.2 us -> 17.1 us
  Pallas kernels: 132 us -> 129 us
  other arithmetic: 12.1 us -> 9.93 us
    slice x1 -> x0, local copies, waits for them, and re-layouts: 8.19 us -> none  [body(): w_dec_kv[:, 0]]
    unnamed x19 -> x14, local copies, waits for them, and re-layouts: 6.2 us -> 12.6 us
    pallas_call x1, Pallas kernels: 132 us -> 129 us  [run(): pl.pallas_call(mega, out_shape=(jax.ShapeDtypeStruct((16, R, HALF), BF16)...]
    concatenate x1 -> x0, other arithmetic: 2.14 us -> none  [body(): jnp.concatenate([w_dec_kv[:, 0], w_dec_kv[:, 1]], axis=1)]
where the time goes in v7:
time: 158 us
  Pallas kernels  129 us (82%)
  local copies, waits for them, and re-layouts  17.1 us (11%)
  other arithmetic  9.93 us (6%)
    pallas_call x1, Pallas kernels, run(): pl.pallas_call(mega, out_shape=(jax.ShapeDtypeStruct((16, R, HALF), BF16)...  129 us
    unnamed x14, local copies, waits for them, and re-layouts  12.6 us
    reduce_or x1, other arithmetic, lists(): dup = jnp.any(same & (t[None, None, :] < t[None, :, None]), axis=2)  4.28 us

profile of v7, /device:TPU:0, one launch (start us, length us, event | category | flops | bytes accessed | tf_op | source)
XLA Modules:
  0.0 157.6 jit_solution(2509990159445514618)
XLA Ops:
  0.6 0.0 copy-start
  0.7 0.7 copy-done
  1.3 0.3 dynamic-slice_reduce_fusion
  1.6 0.1 select_reduce_fusion.2
  1.7 0.9 reshape.237
  2.6 0.1 iota_compare_fusion.3
  2.7 4.3 %and_reduce_fusion = pred[16,512]{1,0:T(8,128)(4,1)S(1)} fusion(s32[16,512]{1,0:T(8,128)S(1)} %get-tuple-element.45, pred[512,512]{1,0:T(8,128)(4,1)S(1)} %iota_compare_fusion.3), kind=kLoop, calls=%fused_computation.8 | loop fusion | flops 12574720 | bytes 303104 | tf_op jit(solution)/shard_map/reduce_or | solution.py:24
  7.1 0.4 convert_reduce_fusion.1
  7.4 0.6 reduce_max.9
  8.7 0.1 pad.8.clone
  8.8 0.7 add_add_fusion.slot_ref
  9.5 0.3 select_reduce_fusion.1
  9.8 0.5 convert_reduce_fusion
  10.3 0.2 copy.45
  10.5 0.2 copy.42
  10.7 0.1 copy.41
  10.8 0.8 fusion.4.pos_ref
  11.6 0.0 copy-start.4
  11.6 0.1 conditional.1
  11.6 0.1 broadcast.237
  11.7 0.0 copy-start.3
  11.7 0.2 convolution_convert_fusion
  11.9 0.5 select_reduce_fusion
  12.3 0.9 reshape.250.list_ref
  13.2 0.0 copy-done.3
  13.2 0.0 copy-done.4
  13.2 0.7 copy.51.wq_own_ref
  14.0 0.0 copy-start.2
  14.0 5.4 %copy.55 = bf16[112,8,2,1024]{3,1,2,0:T(8,128)(2,1)} copy(bf16[112,8,2,1024]{3,2,1,0:T(2,128)(2,1)} %bitcast.31) | data formatting | bytes 7340032
  19.4 0.1 fusion.7
  19.6 1.0 maximum_select_fusion
  20.7 0.7 maximum_bitcast_fusion.wqo_ref
  21.4 0.0 copy-done.2
  21.4 0.0 copy-start.1
  21.4 128.8 %shard_map.138 = (bf16[16,128,448]{2,1,0:T(8,128)(2,1)}, bf16[2,128,1024]{2,1,0:T(8,128)(2,1)}, f32[16,896]{1,0:T(8,128)}, f32[16,896]{1,0:T(8,128)}) custom-call(s32[3,16]{1,0:T(4,128)} %add_add_fusion.slot_ref, s32[2,1024]{1,0:T(2,128)} %constant.144.clone.rows_ref, s32[512,1]{1,0:T(8,128)} %fusion.4.pos_ref, bf16[512,896]{1,0:T(8,128)(2,1)} %copy-done.3, ...), custom_call_target="tpu_custom_call" | custom-call | flops 16000000000 | bytes 31457280 | tf_op jit(solution)/shard_map/pallas_call | solution.py:618
  150.3 3.9 %copy.52 = bf16[1,1,16,1,128,448]{4,5,3,2,1,0:T(8,128)(2,1)} copy(bf16[1,1,16,1,128,448]{5,4,2,3,1,0:T(8,128)(2,1)} %bitcast.33) | data formatting | bytes 3670016
  154.2 1.5 dynamic-slice_bitcast_fusion
  155.7 1.9 %copy.59 = bf16[2,128,1024]{2,1,0:T(8,128)(2,1)} copy(bf16[2,128,1024]{2,1,0:T(8,128)(2,1)} %get-tuple-element.63) | data formatting | bytes 1048576
  157.5 0.0 copy-done.1
  (11 shorter events, 0.2 us)
Async XLA Ops:
  0.6 0.7 copy-start
  11.6 1.7 %copy-start.4 = (bf16[896,448]{0,1:T(8,128)(2,1)S(1)}, bf16[896,448]{0,1:T(8,128)(2,1)}, u32[]{:S(2)}) copy-start(bf16[896,448]{0,1:T(8,128)(2,1)} %param.20) | copy-start | bytes 2408452
  11.7 1.6 copy-start.3
  14.0 7.5 %copy-start.2 = (bf16[896,448]{1,0:T(8,128)(2,1)}, bf16[896,448]{1,0:T(8,128)(2,1)S(1)}, u32[]{:S(2)}) copy-start(bf16[896,448]{1,0:T(8,128)(2,1)S(1)} %copy.51.wq_own_ref) | copy-start | bytes 2408452
  21.4 136.1 %copy-start.1 = (s32[1,16,8,1]{1,3,2,0:T(1,128)S(1)}, s32[1,16,8,1]{1,3,2,0:T(1,128)}, u32[]{:S(2)}) copy-start(s32[1,16,8,1]{1,3,2,0:T(1,128)} %param.17) | copy-start | bytes 1540

commit v8 on v7

--- a/solution.py
+++ b/solution.py
@@ -368,6 +368,7 @@
 
     for copy in embs:
         copy.wait()
+    next(wide_steps)
     alt_in.wait()
     slot_of = lax.broadcasted_iota(jnp.int32, (1, 16 * ROOM), 1)
     pick = (pos_ref[...] == slot_of).astype(F32).astype(BF16)
@@ -377,7 +378,6 @@
         rows = jnp.concatenate([got_ref[i, :, cols] for i in range(16)], axis=0)
         emb_ref[:, cols] = jnp.where(over, eq_ref[:, cols].astype(F32), dot(pick, rows)).astype(BF16)
 
-    next(wide_steps)
     lane = lax.broadcasted_iota(jnp.int32, (1, PAIR), 1)
     is_low = lane < EHD
     low = is_low.astype(F32).astype(BF16)

time: 158 us -> 158 us (level)
  no operation moved by 1% of the time
where the time goes in v8:
time: 158 us; the launch traced here: 157 us
  Pallas kernels  129 us (82%)
  local copies, waits for them, and re-layouts  17.1 us (11%)
  other arithmetic  9.93 us (6%)
    pallas_call x1, Pallas kernels, run(): pl.pallas_call(mega, out_shape=(jax.ShapeDtypeStruct((16, R, HALF), BF16)...  129 us
    unnamed x14, local copies, waits for them, and re-layouts  12.6 us
    reduce_or x1, other arithmetic, lists(): dup = jnp.any(same & (t[None, None, :] < t[None, :, None]), axis=2)  4.28 us

profile of v8, /device:TPU:0, one launch (start us, length us, event | category | flops | bytes accessed | tf_op | source)
XLA Modules:
  0.0 157.4 jit_solution(6583213207590770952)
XLA Ops:
  0.6 0.0 copy-start
  0.7 0.7 copy-done
  1.3 0.3 dynamic-slice_reduce_fusion
  1.6 0.1 select_reduce_fusion.2
  1.7 0.9 reshape.237
  2.6 0.1 iota_compare_fusion.3
  2.7 4.3 %and_reduce_fusion = pred[16,512]{1,0:T(8,128)(4,1)S(1)} fusion(s32[16,512]{1,0:T(8,128)S(1)} %get-tuple-element.45, pred[512,512]{1,0:T(8,128)(4,1)S(1)} %iota_compare_fusion.3), kind=kLoop, calls=%fused_computation.8 | loop fusion | flops 12574720 | bytes 303104 | tf_op jit(solution)/shard_map/reduce_or | solution.py:24
  7.1 0.4 convert_reduce_fusion.1
  7.4 0.6 reduce_max.9
  8.7 0.1 pad.8.clone
  8.8 0.7 add_add_fusion.slot_ref
  9.5 0.3 select_reduce_fusion.1
  9.8 0.5 convert_reduce_fusion
  10.3 0.2 copy.45
  10.5 0.2 copy.42
  10.7 0.1 copy.41
  10.8 0.8 fusion.4.pos_ref
  11.6 0.0 copy-start.4
  11.6 0.1 conditional.1
  11.6 0.1 broadcast.237
  11.7 0.0 copy-start.3
  11.7 0.2 convolution_convert_fusion
  11.9 0.5 select_reduce_fusion
  12.3 0.9 reshape.250.list_ref
  13.2 0.0 copy-done.3
  13.2 0.0 copy-done.4
  13.2 0.7 copy.51.wq_own_ref
  14.0 0.0 copy-start.2
  14.0 5.4 %copy.55 = bf16[112,8,2,1024]{3,1,2,0:T(8,128)(2,1)} copy(bf16[112,8,2,1024]{3,2,1,0:T(2,128)(2,1)} %bitcast.31) | data formatting | bytes 7340032
  19.4 0.1 fusion.7
  19.6 1.0 maximum_select_fusion
  20.7 0.7 maximum_bitcast_fusion.wqo_ref
  21.4 0.0 copy-done.2
  21.4 0.0 copy-start.1
  21.4 128.7 %shard_map.138 = (bf16[16,128,448]{2,1,0:T(8,128)(2,1)}, bf16[2,128,1024]{2,1,0:T(8,128)(2,1)}, f32[16,896]{1,0:T(8,128)}, f32[16,896]{1,0:T(8,128)}) custom-call(s32[3,16]{1,0:T(4,128)} %add_add_fusion.slot_ref, s32[2,1024]{1,0:T(2,128)} %constant.144.clone.rows_ref, s32[512,1]{1,0:T(8,128)} %fusion.4.pos_ref, bf16[512,896]{1,0:T(8,128)(2,1)} %copy-done.3, ...), custom_call_target="tpu_custom_call" | custom-call | flops 16000000000 | bytes 31457280 | tf_op jit(solution)/shard_map/pallas_call | solution.py:618
  150.1 3.9 %copy.52 = bf16[1,1,16,1,128,448]{4,5,3,2,1,0:T(8,128)(2,1)} copy(bf16[1,1,16,1,128,448]{5,4,2,3,1,0:T(8,128)(2,1)} %bitcast.33) | data formatting | bytes 3670016
  154.0 1.5 dynamic-slice_bitcast_fusion
  155.5 1.9 %copy.59 = bf16[2,128,1024]{2,1,0:T(8,128)(2,1)} copy(bf16[2,128,1024]{2,1,0:T(8,128)(2,1)} %get-tuple-element.63) | data formatting | bytes 1048576
  157.4 0.0 copy-done.1
  (11 shorter events, 0.2 us)
Async XLA Ops:
  0.6 0.7 copy-start
  11.6 1.7 %copy-start.4 = (bf16[896,448]{0,1:T(8,128)(2,1)S(1)}, bf16[896,448]{0,1:T(8,128)(2,1)}, u32[]{:S(2)}) copy-start(bf16[896,448]{0,1:T(8,128)(2,1)} %param.20) | copy-start | bytes 2408452
  11.7 1.6 copy-start.3
  14.0 7.5 %copy-start.2 = (bf16[896,448]{1,0:T(8,128)(2,1)}, bf16[896,448]{1,0:T(8,128)(2,1)S(1)}, u32[]{:S(2)}) copy-start(bf16[896,448]{1,0:T(8,128)(2,1)S(1)} %copy.51.wq_own_ref) | copy-start | bytes 2408452
  21.4 135.9 %copy-start.1 = (s32[1,16,8,1]{1,3,2,0:T(1,128)S(1)}, s32[1,16,8,1]{1,3,2,0:T(1,128)}, u32[]{:S(2)}) copy-start(s32[1,16,8,1]{1,3,2,0:T(1,128)} %param.17) | copy-start | bytes 1540
